TPU v7x, 256 devices: a whole 4x4x8 slice. The times are simulated.
256 devices in a mesh: blk: 32 (over z, y_lo, core), tp: 8 (over x, y_hi).
Axes of the slice: x: 4, y: 4 (y_hi: 2, y_lo: 2; y = y_hi * 2 + y_lo), z: 8, core: 2. Of those that a mesh axis runs over, the one named last changes fastest.
Arguments:
- scan_input: bfloat16 [16384, 8192], P('blk', 'tp'), may hold values from -6 to 6
- gate_input: bfloat16 [16384, 8192], P('blk', 'tp'), may hold values from -20 to 20
- state_proj: bfloat16 [16384, 2, 2048], P('blk', None, 'tp'), may hold values from -4 to 4
- step_raw: bfloat16 [16384, 128], P('blk', 'tp')
- log_rate: float32 [128], P('tp'), may hold values from -9 to -2
- step_bias: float32 [128], P('tp'), may hold values from -0.5 to 0.5
- skip_gain: float32 [128], P('tp'), may hold values from 0.5 to 2
- norm_gain: float32 [8192], P('tp'), may hold values from 0.1 to 1.9
- out_proj: bfloat16 [4096, 8192], P('blk', 'tp'), may hold values from -0.0625 to 0.0625
- out_cotangent: bfloat16 [16384, 4096], P('blk', 'tp'), may hold values from -6 to 6
Outputs:
- input_grad: bfloat16 [16384, 8192], P('blk', 'tp')
- gate_grad: bfloat16 [16384, 8192], P('blk', 'tp')
- state_proj_grad: bfloat16 [16384, 2, 2048], P('blk', None, 'tp')
- step_grad: float32 [16384, 128], P('blk', 'tp')
- out_proj_grad: float32 [4096, 8192], P('blk', 'tp')
- log_rate_grad: float32 [128], P('tp')
- step_bias_grad: float32 [128], P('tp')
- skip_grad: float32 [128], P('tp')
- norm_gain_grad: float32 [8192], P('tp')
All inputs are finite; a program needn't handle non-finite values.
Results may differ from a plain program's by a relative error of at most 0.009.
Values may be sent and summed in bfloat16 or wider, within the bound.
No kernel may reach another device: no remote copies, remote signals or barrier semaphores. Data moves between devices by JAX's collectives and lax.ppermute only.
A program may use at most 128 MiB of HBM per device.

v0:
```python
import math

import jax
import jax.numpy as jnp
from jax import lax
from jax.experimental import pallas as pl
from jax.experimental.pallas import tpu as pltpu
from jax.sharding import PartitionSpec as P

TOKENS = 512
CHANNELS = 1024
HEADS = 16
WIDTH = 64
STATE = 256
CHUNK = 128
CHUNKS = TOKENS // CHUNK
LANES = 128
PAIRS = HEADS // 2
EPS = 1e-05

F32 = jnp.float32
BF16 = jnp.bfloat16


def dot(a, b, over=(1, 0)):
    return lax.dot_general(
        a, b, (((over[0],), (over[1],)), ((), ())), preferred_element_type=F32
    )


def three_parts(v):
    hi = v.astype(BF16).astype(F32)
    rest = v - hi
    mid = rest.astype(BF16).astype(F32)
    return hi, mid, rest - mid


def packed(v):
    hi, mid, low = three_parts(v)
    return (hi + pltpu.roll(mid, HEADS, 1) + pltpu.roll(low, 2 * HEADS, 1)).astype(BF16)


def halves(v):
    hi = v.astype(BF16)
    return hi, (v - hi.astype(F32)).astype(BF16)


def folded(v):
    middle = v.shape[1] // 2
    return v[:, :middle] + v[:, middle:]


def triangle(lower):
    i = lax.broadcasted_iota(jnp.int32, (CHUNK, CHUNK), 0)
    j = lax.broadcasted_iota(jnp.int32, (CHUNK, CHUNK), 1)
    return i >= j if lower else i <= j


def picker(pair, width):
    row = lax.broadcasted_iota(jnp.int32, (LANES, 2 * width), 0)
    col = lax.broadcasted_iota(jnp.int32, (LANES, 2 * width), 1)
    head = 2 * pair + col // width
    return jnp.where((row % HEADS == head) & (row < 3 * HEADS), 1.0, 0.0).astype(BF16)


def softplus(v):
    return jnp.maximum(v, 0.0) + jnp.log1p(jnp.exp(-jnp.abs(v)))


def head_lanes():
    return lax.broadcasted_iota(jnp.int32, (TOKENS, LANES), 1) < HEADS


def steps_of(raw_ref, bias_ref, rate_ref):
    step = jnp.where(head_lanes(), softplus(raw_ref[...].astype(F32) + bias_ref[...]), 0.0)
    return step, -step * jnp.exp(rate_ref[...])


def prepare(raw_ref, raw_t_ref, bias_ref, rate_ref, bias_t_ref, rate_t_ref, b_ref, c_ref,
            step_pack, run_pack, run_rows, step_rows, overlap):
    step, decay = steps_of(raw_ref, bias_ref, rate_ref)
    step_pack[...] = packed(step)
    lower = jnp.where(triangle(True), 1.0, 0.0).astype(BF16)
    upper = jnp.where(triangle(False), 1.0, 0.0).astype(BF16)
    decay_pack = packed(decay)
    keep = lax.broadcasted_iota(jnp.int32, (CHUNK, LANES), 1) < HEADS
    step_t = softplus(raw_t_ref[...].astype(F32) + bias_t_ref[...])
    decay_t = three_parts(-step_t * jnp.exp(rate_t_ref[...]))
    for pair in range(PAIRS):
        step_rows[pair] = step_t[2 * pair : 2 * pair + 2, :]
    for c in range(CHUNKS):
        rows = slice(c * CHUNK, (c + 1) * CHUNK)
        total = dot(lower, decay_pack[rows])
        total = total + pltpu.roll(total, LANES - HEADS, 1) + pltpu.roll(total, LANES - 2 * HEADS, 1)
        run_pack[rows, :] = packed(jnp.where(keep, total, 0.0))
        across = sum(dot(part[:, rows].astype(BF16), upper) for part in decay_t)
        for pair in range(PAIRS):
            run_rows[pair, :, rows] = across[2 * pair : 2 * pair + 2, :]
        overlap[c] = jnp.where(triangle(True), dot(c_ref[rows, :], b_ref[rows, :], (1, 1)), 0.0)


def first_half():
    return lax.broadcasted_iota(jnp.int32, (CHUNK, LANES), 1) < WIDTH


def apart(v):
    first = first_half()
    return jnp.concatenate([jnp.where(first, v, 0.0), jnp.where(first, 0.0, v)], axis=0).astype(BF16)


def decays(columns, run_rows, pair, rows):
    out = []
    for h in range(2):
        across = run_rows[pair, h : h + 1, rows]
        out.append(jnp.exp(jnp.minimum(columns[:, h * CHUNK : (h + 1) * CHUNK] - across, 0.0)))
    return out


def forward_kernel(x_ref, g_ref, b_ref, bt_ref, c_ref, raw_ref, raw_t_ref, bias_ref, rate_ref,
                   bias_t_ref, rate_t_ref, skip_ref, gain_ref,
                   low_ref, scan_ref, gated_ref, state_ref, scale_ref,
                   step_pack, run_pack, run_rows, step_rows, overlap, squares):
    pair = pl.program_id(0)

    @pl.when(pair == 0)
    def _():
        prepare(raw_ref, raw_t_ref, bias_ref, rate_ref, bias_t_ref, rate_t_ref, b_ref, c_ref,
                step_pack, run_pack, run_rows, step_rows, overlap)
        squares[...] = jnp.zeros_like(squares)

    narrow, wide = picker(pair, WIDTH), picker(pair, CHUNK)
    skip = skip_ref[:, pl.ds(pl.multiple_of(pair * LANES, LANES), LANES)]
    state = None
    for c in range(CHUNKS):
        rows = slice(c * CHUNK, (c + 1) * CHUNK)
        x = x_ref[rows, :].astype(F32)
        step = dot(step_pack[rows, :], narrow)
        run = dot(run_pack[rows, :], narrow)
        columns = dot(run_pack[rows, :], wide)
        weights = []
        for h, one in enumerate(decays(columns, run_rows, pair, rows)):
            weights.append(halves(one * overlap[c] * step_rows[pair, h : h + 1, rows]))
        x_apart = apart(x)
        y = dot(
            jnp.concatenate([weights[h][part] for part in range(2) for h in range(2)], axis=1),
            jnp.concatenate([x_apart, x_apart], axis=0),
        )
        if c > 0:
            state_ref[0, c - 1] = state
            held = jnp.concatenate(halves(state), axis=1)
            y = y + jnp.exp(run) * folded(dot(c_ref[rows, :], held))
        if c < CHUNKS - 1:
            end = run[CHUNK - 1 :, :]
            fresh = jnp.concatenate(halves(x * step * jnp.exp(end - run)), axis=1)
            local = folded(dot(bt_ref[:, rows], fresh))
            state = local if c == 0 else jnp.exp(end) * state + local
        scan_ref[rows, :] = y
        g = g_ref[rows, :].astype(F32)
        gated = (y + skip * x) * (g / (1.0 + jnp.exp(-g)))
        gated_ref[rows, pl.ds(pl.multiple_of(pair * LANES, LANES), LANES)] = gated
        squares[rows, :] += gated * gated

    @pl.when(pair == PAIRS - 1)
    def _():
        for c in range(CHUNKS):
            rows = slice(c * CHUNK, (c + 1) * CHUNK)
            mean = jnp.sum(squares[rows, :], axis=1, keepdims=True) * (1.0 / CHANNELS)
            scale = lax.rsqrt(mean + EPS)
            scale_ref[rows, :] = jnp.broadcast_to(scale, (CHUNK, LANES))
            low_ref[rows, :] = (gated_ref[rows, :] * scale * gain_ref[...]).astype(BF16)


def backward_kernel(x_ref, g_ref, cot_ref, scan_ref, state_ref, scale_ref, pull_ref,
                    b_ref, c_ref, ct_ref, raw_ref, raw_t_ref, bias_ref, rate_ref,
                    bias_t_ref, rate_t_ref, skip_ref, gain_ref,
                    dx_ref, dg_ref, db_ref, dc_ref, step_ref, small_ref,
                    step_pack, run_pack, run_rows, step_rows, overlap, d_overlap, d_b, d_c, flow, direct, lanes):
    pair = pl.program_id(0)

    @pl.when(pair == 0)
    def _():
        prepare(raw_ref, raw_t_ref, bias_ref, rate_ref, bias_t_ref, rate_t_ref, b_ref, c_ref,
                step_pack, run_pack, run_rows, step_rows, overlap)
        for held in (d_overlap, d_b, d_c, flow, direct, lanes):
            held[...] = jnp.zeros_like(held)

    narrow, wide = picker(pair, WIDTH), picker(pair, CHUNK)
    here = pl.ds(pl.multiple_of(pair * LANES, LANES), LANES)
    skip, gain = skip_ref[:, here], gain_ref[:, here]
    first = first_half()
    lane = lax.broadcasted_iota(jnp.int32, (CHUNK, LANES), 1)

    def by_head(v):
        one = jnp.sum(jnp.where(first, v, 0.0), axis=1, keepdims=True)
        two = jnp.sum(jnp.where(first, 0.0, v), axis=1, keepdims=True)
        return jnp.where(lane == 2 * pair, one, jnp.where(lane == 2 * pair + 1, two, 0.0))

    d_state = None
    skip_sum = jnp.zeros((1, LANES), F32)
    for c in reversed(range(CHUNKS)):
        rows = slice(c * CHUNK, (c + 1) * CHUNK)
        x = x_ref[rows, :].astype(F32)
        g = g_ref[rows, :].astype(F32)
        scan = scan_ref[rows, :]
        out = scan + skip * x
        sig = 1.0 / (1.0 + jnp.exp(-g))
        silu = g * sig
        d_gated = scale_ref[rows, :] * gain * cot_ref[rows, :] - out * silu * pull_ref[rows, :]
        dy = d_gated * silu
        dg_ref[rows, :] = (d_gated * out * (sig + silu * (1.0 - sig))).astype(BF16)
        skip_sum = skip_sum + jnp.sum(dy * x, axis=0, keepdims=True)

        step = dot(step_pack[rows, :], narrow)
        run = dot(run_pack[rows, :], narrow)
        columns = dot(run_pack[rows, :], wide)
        driven = x * step
        dy_hi, dy_low = (apart(part.astype(F32)) for part in halves(dy))
        factor = decays(columns, run_rows, pair, rows)
        products = dot(
            jnp.concatenate([dy_hi, dy_low], axis=1),
            jnp.concatenate([x_ref[rows, :], x_ref[rows, :]], axis=1),
            (1, 1),
        )
        step_row = step_rows[pair, :, rows]
        d_overlap[c] += (
            factor[0] * products[:CHUNK] * step_row[:1] + factor[1] * products[CHUNK:] * step_row[1:]
        )
        weights = [halves(one * overlap[c]) for one in factor]
        weights_hi = jnp.concatenate([one[0] for one in weights], axis=0)
        weights_low = jnp.concatenate([one[1] for one in weights], axis=0)
        d_driven = folded(dot(weights_hi, jnp.concatenate([dy_hi, dy_low], axis=1), (0, 0)))
        d_driven = d_driven + dot(weights_low, dy_hi, (0, 0))
        entering_hi, entering_low = halves(dy * jnp.exp(run))
        entering = jnp.concatenate([entering_hi, entering_low], axis=1)
        end = run[CHUNK - 1 :, :]
        if c > 0:
            held = state_ref[0, c - 1]
            held_hi, held_low = halves(held)
            d_c[rows, :] += dot(
                entering, jnp.concatenate([held_hi, held_hi], axis=1), (1, 1)
            ) + dot(entering_hi, held_low, (1, 1))
        if c < CHUNKS - 1:
            to_end = jnp.exp(end - run)
            d_hi, d_low = halves(d_state)
            from_state = to_end * folded(
                dot(b_ref[rows, :], jnp.concatenate([d_hi, d_low], axis=1))
            )
            fresh_hi, fresh_low = halves(driven * to_end)
            d_b[rows, :] += dot(
                jnp.concatenate([fresh_hi, fresh_low], axis=1),
                jnp.concatenate([d_hi, d_hi], axis=1),
                (1, 1),
            ) + dot(fresh_hi, d_low, (1, 1))
            crossing = jnp.sum(driven * from_state, axis=0, keepdims=True)
            if c > 0:
                carried = jnp.sum(held * d_state, axis=0, keepdims=True)
                crossing = crossing + jnp.exp(end) * carried
            lanes[c : c + 1, here] = crossing
            d_driven = d_driven + from_state
        if c > 0:
            back = folded(dot(ct_ref[:, rows], entering))
            d_state = back if d_state is None else jnp.exp(end) * d_state + back
        flow[rows, :] += by_head(dy * scan - driven * d_driven)
        direct[rows, :] += by_head(x * d_driven)
        dx_ref[rows, :] = (step * d_driven + skip * dy).astype(BF16)
    lanes[CHUNKS : CHUNKS + 1, here] = skip_sum

    @pl.when(pair == PAIRS - 1)
    def _():
        channel = lax.broadcasted_iota(jnp.int32, (CHANNELS, LANES), 0) // WIDTH
        head = lax.broadcasted_iota(jnp.int32, (CHANNELS, LANES), 1)
        gather = jnp.where(channel == head, 1.0, 0.0).astype(BF16)
        heads = sum(dot(part.astype(BF16), gather) for part in three_parts(lanes[...]))
        step_all, decay_all = steps_of(raw_ref, bias_ref, rate_ref)
        rate = jnp.exp(rate_ref[...])
        upper = jnp.where(triangle(False), 1.0, 0.0).astype(BF16)
        keep = lane < HEADS
        rate_sum = jnp.zeros((1, LANES), F32)
        bias_sum = jnp.zeros((1, LANES), F32)
        for c in range(CHUNKS):
            rows = slice(c * CHUNK, (c + 1) * CHUNK)
            d_decay = sum(dot(upper, part.astype(BF16)) for part in three_parts(flow[rows, :]))
            d_decay = d_decay + heads[c : c + 1, :]
            d_step = direct[rows, :] - d_decay * rate
            before = raw_ref[rows, :].astype(F32) + bias_ref[...]
            d_raw = jnp.where(keep, d_step / (1.0 + jnp.exp(-before)), 0.0)
            step_ref[rows, :] = d_raw[:, :HEADS]
            bias_sum = bias_sum + jnp.sum(d_raw, axis=0, keepdims=True)
            rate_sum = rate_sum + jnp.sum(
                jnp.where(keep, d_decay * decay_all[rows], 0.0), axis=0, keepdims=True
            )
            d_hi, d_low = halves(jnp.where(triangle(True), d_overlap[c], 0.0))
            dc_ref[rows, :] = (
                d_c[rows, :] + dot(d_hi, b_ref[rows, :]) + dot(d_low, b_ref[rows, :])
            ).astype(BF16)
            db_ref[rows, :] = (
                d_b[rows, :] + dot(d_hi, c_ref[rows, :], (0, 0)) + dot(d_low, c_ref[rows, :], (0, 0))
            ).astype(BF16)
        small_ref[...] = jnp.concatenate(
            [rate_sum, bias_sum, heads[CHUNKS : CHUNKS + 1, :], jnp.zeros((5, LANES), F32)], axis=0
        )


def whole(shape):
    return pl.BlockSpec(shape, lambda *_: (0,) * len(shape))


def by_pair(rows):
    return pl.BlockSpec((rows, LANES), lambda p, *_: (0, p))


VMEM_LIMIT = 56 * 1024 * 1024

TABLES = [
    pltpu.VMEM((TOKENS, LANES), BF16),
    pltpu.VMEM((TOKENS, LANES), BF16),
    pltpu.VMEM((PAIRS, 2, TOKENS), F32),
    pltpu.VMEM((PAIRS, 2, TOKENS), F32),
    pltpu.VMEM((CHUNKS, CHUNK, CHUNK), F32),
]

PARAMETERS = [
    whole((TOKENS, LANES)),
    whole((HEADS, TOKENS)),
    whole((1, LANES)),
    whole((1, LANES)),
    whole((HEADS, 1)),
    whole((HEADS, 1)),
    whole((1, CHANNELS)),
    whole((1, CHANNELS)),
]


def scan_forward(x, g, b, bt, c, parameters):
    return pl.pallas_call(
        forward_kernel,
        grid=(PAIRS,),
        in_specs=[
            by_pair(TOKENS),
            by_pair(TOKENS),
            whole((TOKENS, STATE)),
            whole((STATE, TOKENS)),
            whole((TOKENS, STATE)),
        ]
        + PARAMETERS,
        out_specs=[
            whole((TOKENS, CHANNELS)),
            by_pair(TOKENS),
            whole((TOKENS, CHANNELS)),
            pl.BlockSpec((1, CHUNKS - 1, STATE, LANES), lambda p: (p, 0, 0, 0)),
            whole((TOKENS, LANES)),
        ],
        out_shape=[
            jax.ShapeDtypeStruct((TOKENS, CHANNELS), BF16),
            jax.ShapeDtypeStruct((TOKENS, CHANNELS), F32),
            jax.ShapeDtypeStruct((TOKENS, CHANNELS), F32),
            jax.ShapeDtypeStruct((PAIRS, CHUNKS - 1, STATE, LANES), F32),
            jax.ShapeDtypeStruct((TOKENS, LANES), F32),
        ],
        scratch_shapes=TABLES + [pltpu.VMEM((TOKENS, LANES), F32)],
        compiler_params=pltpu.CompilerParams(vmem_limit_bytes=VMEM_LIMIT),
        cost_estimate=pl.CostEstimate(flops=16 * 10**9, bytes_accessed=10**7, transcendentals=0),
        name="scan_forward",
    )(x, g, b, bt, c, *parameters)


def scan_backward(x, g, cot, scan, states, scale, pull, b, c, ct, parameters):
    return pl.pallas_call(
        backward_kernel,
        grid=(PAIRS,),
        in_specs=[
            by_pair(TOKENS),
            by_pair(TOKENS),
            by_pair(TOKENS),
            by_pair(TOKENS),
            pl.BlockSpec((1, CHUNKS - 1, STATE, LANES), lambda p: (p, 0, 0, 0)),
            whole((TOKENS, LANES)),
            whole((TOKENS, LANES)),
            whole((TOKENS, STATE)),
            whole((TOKENS, STATE)),
            whole((STATE, TOKENS)),
        ]
        + PARAMETERS,
        out_specs=[
            by_pair(TOKENS),
            by_pair(TOKENS),
            whole((TOKENS, STATE)),
            whole((TOKENS, STATE)),
            whole((TOKENS, HEADS)),
            whole((8, LANES)),
        ],
        out_shape=[
            jax.ShapeDtypeStruct((TOKENS, CHANNELS), BF16),
            jax.ShapeDtypeStruct((TOKENS, CHANNELS), BF16),
            jax.ShapeDtypeStruct((TOKENS, STATE), BF16),
            jax.ShapeDtypeStruct((TOKENS, STATE), BF16),
            jax.ShapeDtypeStruct((TOKENS, HEADS), F32),
            jax.ShapeDtypeStruct((8, LANES), F32),
        ],
        scratch_shapes=TABLES
        + [
            pltpu.VMEM((CHUNKS, CHUNK, CHUNK), F32),
            pltpu.VMEM((TOKENS, STATE), F32),
            pltpu.VMEM((TOKENS, STATE), F32),
            pltpu.VMEM((TOKENS, LANES), F32),
            pltpu.VMEM((TOKENS, LANES), F32),
            pltpu.VMEM((8, CHANNELS), F32),
        ],
        compiler_params=pltpu.CompilerParams(vmem_limit_bytes=VMEM_LIMIT),
        cost_estimate=pl.CostEstimate(flops=20 * 10**9, bytes_accessed=10**7, transcendentals=0),
        name="scan_backward",
    )(x, g, cot, scan, states, scale, pull, b, c, ct, *parameters)


FEATURES = 512
BLOCK = 128
SHARDS = 8


def term_kernel(count, added, slot, slots, places, *refs):
    pieces, low_ref = refs[:count], refs[count]
    sent_ref = refs[count + 1] if added else None
    out_ref, held, done = refs[-3:]
    turned = jnp.concatenate([piece[...] for piece in pieces], axis=1).T
    for n in range(CHANNELS // COLUMNS):
        cols = slice(n * COLUMNS, (n + 1) * COLUMNS)
        term = dot(turned, low_ref[:, cols])
        for k in range(count):
            part = term[k * BLOCK : (k + 1) * BLOCK]
            if added:
                row = pl.multiple_of(places[k] * BLOCK, BLOCK)
                part = part + sent_ref[pl.ds(row, BLOCK), cols].astype(F32)
            held[k * BLOCK : (k + 1) * BLOCK, cols] = part.astype(BF16)
    copies = []
    for k in range(count):
        row = pl.multiple_of((places[k] * slots + slot) * BLOCK, BLOCK)
        copies.append(
            pltpu.make_async_copy(
                held.at[k * BLOCK : (k + 1) * BLOCK], out_ref.at[pl.ds(row, BLOCK)], done.at[k]
            )
        )
        copies[-1].start()
    for copy in copies:
        copy.wait()


def terms(places, block, pieces, low, sent=None, base=None, slot=0, slots=1):
    count = len(pieces)
    rows = SHARDS * slots * BLOCK
    more, specs, aliases = [], [], {}
    if sent is not None:
        more.append(sent)
        specs.append(whole((SHARDS * BLOCK, CHANNELS)))
    if base is not None:
        aliases = {2 + count + len(more): 0}
        more.append(base)
        specs.append(pl.BlockSpec(memory_space=pl.ANY))

    def kernel(*refs):
        term_kernel(count, sent is not None, slot, slots, *refs)

    return pl.pallas_call(
        kernel,
        grid_spec=pltpu.PrefetchScalarGridSpec(
            num_scalar_prefetch=1,
            grid=(1,),
            in_specs=[pl.BlockSpec((TOKENS, BLOCK), lambda _, at: (0, at[count]))] * count
            + [whole((TOKENS, CHANNELS))]
            + specs,
            out_specs=pl.BlockSpec(memory_space=pl.ANY),
            scratch_shapes=[
                pltpu.VMEM((count * BLOCK, CHANNELS), BF16),
                pltpu.SemaphoreType.DMA((count,)),
            ],
        ),
        out_shape=jax.ShapeDtypeStruct((rows, CHANNELS), BF16),
        input_output_aliases=aliases,
        compiler_params=pltpu.CompilerParams(vmem_limit_bytes=VMEM_LIMIT),
        cost_estimate=pl.CostEstimate(
            flops=count * 5 * 10**8, bytes_accessed=4 * 10**6, transcendentals=0
        ),
        name="terms" if sent is None else "terms_added",
    )(jnp.stack(list(places) + [block]).astype(jnp.int32), *pieces, low, *more)


COLUMNS = 256


def product_kernel(places, *refs):
    pieces = refs[:SHARDS]
    rows_ref, gated_ref, scale_ref, gain_ref = refs[SHARDS : SHARDS + 4]
    cot_ref, gain_grad_ref, pull_ref, sums = refs[SHARDS + 4 :]
    step = pl.program_id(0)
    starts = [pl.multiple_of(places[k] * FEATURES, FEATURES) for k in range(SHARDS)]
    cot_ref[...] = dot(
        jnp.concatenate([piece[...] for piece in pieces], axis=1),
        jnp.concatenate([rows_ref[pl.ds(start, FEATURES), :] for start in starts], axis=0),
    )

    @pl.when(step == 0)
    def _():
        sums[...] = jnp.zeros_like(sums)

    scale = scale_ref[...]
    for half in range(COLUMNS // LANES):
        cols = slice(half * LANES, (half + 1) * LANES)
        with_gated = cot_ref[:, cols] * gated_ref[:, cols]
        gain_grad_ref[:, cols] = jnp.sum(with_gated * scale, axis=0, keepdims=True)
        sums[...] += with_gated * gain_ref[:, cols]

    @pl.when(step == pl.num_programs(0) - 1)
    def _():
        pulled = jnp.sum(sums[...], axis=1, keepdims=True) * (1.0 / CHANNELS)
        pull_ref[...] = scale * scale * scale * pulled


def products(places, pieces, rows, gated, scale, gain):
    depth = SHARDS * FEATURES
    return pl.pallas_call(
        product_kernel,
        grid_spec=pltpu.PrefetchScalarGridSpec(
            num_scalar_prefetch=1,
            grid=(CHANNELS // COLUMNS,),
            in_specs=[whole((TOKENS, FEATURES))] * SHARDS
            + [
                pl.BlockSpec((depth, COLUMNS), lambda n, *_: (0, n)),
                pl.BlockSpec((TOKENS, COLUMNS), lambda n, *_: (0, n)),
                whole((TOKENS, LANES)),
                pl.BlockSpec((1, COLUMNS), lambda n, *_: (0, n)),
            ],
            out_specs=[
                pl.BlockSpec((TOKENS, COLUMNS), lambda n, *_: (0, n)),
                pl.BlockSpec((1, COLUMNS), lambda n, *_: (0, n)),
                whole((TOKENS, LANES)),
            ],
            scratch_shapes=[pltpu.VMEM((TOKENS, LANES), F32)],
        ),
        out_shape=[
            jax.ShapeDtypeStruct((TOKENS, CHANNELS), F32),
            jax.ShapeDtypeStruct((1, CHANNELS), F32),
            jax.ShapeDtypeStruct((TOKENS, LANES), F32),
        ],
        compiler_params=pltpu.CompilerParams(vmem_limit_bytes=VMEM_LIMIT),
        cost_estimate=pl.CostEstimate(
            flops=12 * 10**9, bytes_accessed=16 * 10**6, transcendentals=0
        ),
        name="products",
    )(places, *pieces, rows, gated, scale, gain)


def along_x(step):
    return [(x * 2 + h, (x + step) % 4 * 2 + h) for x in range(4) for h in range(2)]


def beside(shard):
    return lax.ppermute(shard, "tp", along_x(1)), lax.ppermute(shard, "tp", along_x(-1))


def beyond(before, after):
    half = before.shape[0] // 2
    top = lax.ppermute(before[:half], "tp", along_x(1))
    low = lax.ppermute(after[half:], "tp", along_x(-1))
    return top, low


def swap(bit):
    return [(b, b ^ bit) for b in range(32)]


def local_parameters(step_raw, log_rate, step_bias, skip_gain, norm_gain):
    def padded(v):
        return jnp.pad(v, (0, LANES - HEADS)).reshape(1, LANES)

    return (
        jnp.pad(step_raw, ((0, 0), (0, LANES - HEADS))),
        step_raw.T,
        padded(step_bias),
        padded(log_rate),
        step_bias.reshape(HEADS, 1),
        log_rate.reshape(HEADS, 1),
        jnp.repeat(skip_gain, WIDTH).reshape(1, CHANNELS),
        norm_gain.reshape(1, CHANNELS),
    )


def shards(
    scan_input,
    gate_input,
    state_proj,
    step_raw,
    log_rate,
    step_bias,
    skip_gain,
    norm_gain,
    out_proj,
    out_cotangent,
):
    norm_scale = 1.0 / math.sqrt(TOKENS * 32)
    block = lax.axis_index("blk")
    core, y_lo = block % 2, block // 2 % 2
    rows = lax.all_gather(out_proj, "blk", axis=0, tiled=True)
    own = out_cotangent
    partner = lax.ppermute(own, "tp", [(t, t ^ 1) for t in range(8)])
    before, after = beside(own)
    partner, before, after, scan_input = lax.optimization_barrier(
        (partner, before, after, scan_input)
    )
    partner_before, partner_after = beside(partner)
    far_parts = beyond(before, after)

    parameters = local_parameters(step_raw, log_rate, step_bias, skip_gain, norm_gain)
    b, c = state_proj[:, 0, :], state_proj[:, 1, :]
    low, scan, gated, states, scale = scan_forward(
        scan_input, gate_input, b, b.T, c, parameters
    )
    partner_before, partner_after, far_parts, low = lax.optimization_barrier(
        (partner_before, partner_after, far_parts, low)
    )
    far = jnp.concatenate(far_parts, axis=0)
    partner_far = jnp.concatenate(beyond(partner_before, partner_after), axis=0)
    early = [own, before, after, far, partner, partner_before, partner_after]
    me = lax.axis_index("tp")
    x, h = me // 2, me % 2
    places = [(x + shift) % 4 * 2 + row for row in (h, 1 - h) for shift in (0, 3, 1, 2)]

    mine, mine_y = 2 * y_lo + core, 2 * (1 - y_lo) + core
    theirs, theirs_y = 2 * y_lo + 1 - core, 2 * (1 - y_lo) + 1 - core

    base_y = terms(places[:-1], theirs_y, early, low)
    base = terms(places[:-1], theirs, early, low)
    base_y, base, partner_far = lax.optimization_barrier((base_y, base, partner_far))
    pieces = early + [partner_far]

    def sent_of(block, base):
        full = terms(places[-1:], block, pieces[-1:], low, base=base)
        return lax.ppermute(full, "blk", swap(1))

    sent_y, sent = sent_of(theirs_y, base_y), sent_of(theirs, base)
    both = terms(places, mine_y, pieces, low, sent_y, slots=2)
    rows, low = lax.optimization_barrier((rows, low))
    both = terms(places, mine, pieces, low, sent, base=both, slot=1, slots=2)
    by_z = [[z * 4 + rest for z in range(8)] for rest in range(4)]
    plane = lax.psum_scatter(
        both, "blk", scatter_dimension=0, tiled=True, axis_index_groups=by_z
    )
    given = lax.ppermute(plane[:BLOCK], "blk", swap(2))
    weight_grad = (plane[BLOCK:].astype(F32) + given.astype(F32)) * norm_scale

    rows, _ = lax.optimization_barrier((rows, both))
    cot, gain_grad, pull = products(
        jnp.stack(places).astype(jnp.int32), pieces, rows, gated, scale, parameters[-1]
    )
    dx, dg, db, dc, step_grad, small = scan_backward(
        scan_input, gate_input, cot, scan, states, scale, pull, b, c, c.T, parameters
    )
    summed = jnp.concatenate([small, gain_grad.reshape(8, LANES)], axis=0)
    for bit in (1, 2, 4, 8, 16):
        summed = summed + lax.ppermute(summed, "blk", swap(bit))
    summed = summed * norm_scale
    return (
        dx,
        dg,
        jnp.stack([db, dc], axis=1),
        step_grad,
        weight_grad,
        summed[0, :HEADS],
        summed[1, :HEADS],
        summed[2, :HEADS],
        summed[8:].reshape(CHANNELS),
    )


def solution(mesh):
    placed = (
        P("blk", "tp"),
        P("blk", "tp"),
        P("blk", None, "tp"),
        P("blk", "tp"),
        P("tp"),
        P("tp"),
        P("tp"),
        P("tp"),
        P("blk", "tp"),
        P("blk", "tp"),
    )
    return jax.shard_map(
        shards,
        mesh=mesh,
        in_specs=placed,
        out_specs=(
            P("blk", "tp"),
            P("blk", "tp"),
            P("blk", None, "tp"),
            P("blk", "tp"),
            P("blk", "tp"),
            P("tp"),
            P("tp"),
            P("tp"),
            P("tp"),
        ),
        check_vma=False,
    )
```

profile of v0, /device:TPU:6, one launch (start us, length us, event | category | flops | bytes accessed | tf_op | source)
XLA Modules:
  0.0 165.8 jit_solution(15996905514099524163)
XLA Ops:
  7.3 0.7 all-gather.2.cloned.1.call-update
  8.0 0.9 collective-permute-start.2
  8.9 2.4 %collective-permute-start.1 = (bf16[512,512]{1,0:T(8,128)(2,1)}, bf16[512,512]{1,0:T(8,128)(2,1)S(1)}, u32[]{:S(2)}, u32[]{:S(2)}) collective-permute-start(bf16[512,512]{1,0:T(8,128)(2,1)} %refs_0_.1), channel_id=1, source_target_pairs={{0,2},{1,3},{2,4},{3,5},{4,6},{5,7},{6,0},{7,1},{8,10},{9,11},{10,... | collective-permute-start | bytes 1572872 | tf_op jit(solution)/shard_map/ppermute | solution.py:556
  11.3 3.2 %collective-permute-start = (bf16[512,512]{1,0:T(8,128)(2,1)}, bf16[512,512]{1,0:T(8,128)(2,1)S(1)}, u32[]{:S(2)}, u32[]{:S(2)}) collective-permute-start(bf16[512,512]{1,0:T(8,128)(2,1)} %refs_0_.1), channel_id=1, source_target_pairs={{0,1},{1,0},{2,3},{3,2},{4,5},{5,4},{6,7},{7,6},{8,9},{9,8},{10,11... | collective-permute-start | bytes 1572872 | tf_op jit(solution)/shard_map/ppermute | solution.py:603
  14.5 2.1 %fusion.1 = (bf16[512,1,256]{2,1,0:T(2,128)(2,1)S(1)}, bf16[512,1,256]{2,1,0:T(2,128)(2,1)S(1)}) fusion(bf16[512,2,256]{2,1,0:T(2,128)(2,1)} %param.12), kind=kLoop, calls=%fused_computation.18 | loop fusion | bytes 1048576 | tf_op jit(solution)/shard_map/slice | solution.py:612
  16.7 0.7 stack.112.refs_0_
  18.1 0.7 copy.27.bias_t_ref
  18.8 0.7 copy.28.rate_t_ref
  19.5 0.7 reshape_reshape.3.skip_ref
  20.3 1.3 copy.36
  21.6 0.7 pad.11.raw_ref
  23.5 0.9 copy_bitcast_fusion
  24.4 2.5 %collective-permute-done.refs_5_.refs_4_ = bf16[512,512]{1,0:T(8,128)(2,1)S(1)} collective-permute-done((bf16[512,512]{1,0:T(8,128)(2,1)}, bf16[512,512]{1,0:T(8,128)(2,1)S(1)}, u32[]{:S(2)}, u32[]{:S(2)}) %collective-permute-start) | collective-permute-done | bytes 524320 | tf_op jit(solution)/shard_map/ppermute | solution.py:603
  27.0 3.2 %collective-permute-start.3 = (bf16[512,512]{1,0:T(8,128)(2,1)S(1)}, bf16[512,512]{1,0:T(8,128)(2,1)S(1)}, u32[]{:S(2)}, u32[]{:S(2)}) collective-permute-start(bf16[512,512]{1,0:T(8,128)(2,1)S(1)} %collective-permute-done.refs_5_.refs_4_), channel_id=1, source_target_pairs={{0,2},{1,3},{2,4},{3,5},{4,6},{5,7},{6,0},{7,1},{8,10},{9,11},{10,... | collective-permute-start | bytes 1572872 | tf_op jit(solution)/shard_map/ppermute | solution.py:556
  30.3 3.2 %collective-permute-start.5 = (bf16[256,512]{1,0:T(8,128)(2,1)S(1)}, bf16[256,512]{1,0:T(8,128)(2,1)S(1)}, u32[]{:S(2)}, u32[]{:S(2)}) collective-permute-start(bf16[256,512]{1,0:T(8,128)(2,1)S(1)} %slice.36), channel_id=1, source_target_pairs={{0,2},{1,3},{2,4},{3,5},{4,6},{5,7},{6,0},{7,1},{8,10},{9,11},{10,... | collective-permute-start | bytes 786440 | tf_op jit(solution)/shard_map/ppermute | solution.py:561
  33.6 13.9 %scan_forward.1 = (bf16[512,1024]{1,0:T(8,128)(2,1)}, f32[512,1024]{1,0:T(8,128)}, f32[512,1024]{1,0:T(8,128)}, f32[8,3,256,128]{3,2,1,0:T(8,128)}, f32[512,128]{1,0:T(8,128)}) custom-call(bf16[512,1024]{1,0:T(8,128)(2,1)} %x_ref.1, bf16[512,1024]{1,0:T(8,128)(2,1)} %g_ref.3, bf16[512,256]{1,0:T(8,128)(2,1)} %get-tuple-element.82.b_ref, ...), custom_call_target="tpu_custom_call" | custom-call | flops 16000000000 | bytes 10000000 | tf_op jit(solution)/shard_map/scan_forward/pallas_call | solution.py:335
  47.7 3.2 %collective-permute-start.7 = (bf16[256,512]{1,0:T(8,128)(2,1)S(1)}, bf16[256,512]{1,0:T(8,128)(2,1)S(1)}, u32[]{:S(2)}, u32[]{:S(2)}) collective-permute-start(bf16[256,512]{1,0:T(8,128)(2,1)S(1)} %slice.40), channel_id=1, source_target_pairs={{0,2},{1,3},{2,4},{3,5},{4,6},{5,7},{6,0},{7,1},{8,10},{9,11},{10,... | collective-permute-start | bytes 786440 | tf_op jit(solution)/shard_map/ppermute | solution.py:561
  51.0 0.8 copy-done.5
  51.8 4.7 %terms.5.refs_3_ = bf16[1024,1024]{1,0:T(8,128)(2,1)} custom-call(s32[8]{0:T(128)} %stack.112.refs_0_, bf16[512,512]{1,0:T(8,128)(2,1)} %refs_0_.1, bf16[512,512]{1,0:T(8,128)(2,1)} %copy-done.2, bf16[512,512]{1,0:T(8,128)(2,1)} %copy-done.1, bf16[512,512]{1,0:T(8,128)(2,1)} %copy-done.5, bf16[512,512]{1,0:T(8,128)(2,1)} %copy-done.6, ...), custom_call_target="tpu_custom_call" | custom-call | flops 3500000000 | bytes 4000000 | tf_op jit(solution)/shard_map/terms/pallas_call | solution.py:462
  56.6 4.8 %terms.4.refs_3_ = bf16[1024,1024]{1,0:T(8,128)(2,1)} custom-call(s32[8]{0:T(128)} %stack.54.refs_0_, bf16[512,512]{1,0:T(8,128)(2,1)} %refs_0_.1, bf16[512,512]{1,0:T(8,128)(2,1)} %copy-done.2, bf16[512,512]{1,0:T(8,128)(2,1)} %copy-done.1, bf16[512,512]{1,0:T(8,128)(2,1)} %copy-done.5, bf16[512,512]{1,0:T(8,128)(2,1)} %copy-done.6, ...), custom_call_target="tpu_custom_call" | custom-call | flops 3500000000 | bytes 4000000 | tf_op jit(solution)/shard_map/terms/pallas_call | solution.py:462
  61.4 0.8 pad_maximum_fusion.refs_1_.refs_8_.refs_7_
  62.3 3.0 %terms.7 = bf16[1024,1024]{1,0:T(8,128)(2,1)} custom-call(s32[2]{0:T(128)} %pad_add_fusion.1.refs_0_, bf16[512,512]{1,0:T(8,128)(2,1)} %pad_maximum_fusion.refs_1_.refs_8_.refs_7_, bf16[512,1024]{1,0:T(8,128)(2,1)} %get-tuple-element.50.refs_8_.refs_2_.refs_9_, bf16[1024,1024]{1,0:T(8,128)(2,1)} %terms.4.refs_3_), custom_call_target="tpu_custom_call", output_to_operand_aliasing={{}: (3, {})} | custom-call | flops 500000000 | bytes 4000000 | tf_op jit(solution)/shard_map/terms/pallas_call | solution.py:462
  66.1 3.0 %terms.6 = bf16[1024,1024]{1,0:T(8,128)(2,1)} custom-call(s32[2]{0:T(128)} %pad_add_fusion.refs_0_, bf16[512,512]{1,0:T(8,128)(2,1)} %pad_maximum_fusion.refs_1_.refs_8_.refs_7_, bf16[512,1024]{1,0:T(8,128)(2,1)} %get-tuple-element.50.refs_8_.refs_2_.refs_9_, bf16[1024,1024]{1,0:T(8,128)(2,1)} %terms.5.refs_3_), custom_call_target="tpu_custom_call", output_to_operand_aliasing={{}: (3, {})} | custom-call | flops 500000000 | bytes 4000000 | tf_op jit(solution)/shard_map/terms/pallas_call | solution.py:462
  70.3 0.7 stack.114.refs_0_
  71.0 5.8 %terms_added.2.refs_11_ = bf16[2048,1024]{1,0:T(8,128)(2,1)} custom-call(s32[9]{0:T(128)} %stack.117.refs_0_, bf16[512,512]{1,0:T(8,128)(2,1)} %refs_0_.1, bf16[512,512]{1,0:T(8,128)(2,1)} %copy-done.2, bf16[512,512]{1,0:T(8,128)(2,1)} %copy-done.1, bf16[512,512]{1,0:T(8,128)(2,1)} %copy-done.5, bf16[512,512]{1,0:T(8,128)(2,1)} %copy-done.6, ...), custom_call_target="tpu_custom_call" | custom-call | flops 4000000000 | bytes 4000000 | tf_op jit(solution)/shard_map/terms_added/pallas_call | solution.py:462
  76.9 8.2 %all-gather.2.cloned.1.call-done.refs_8_ = bf16[4096,1024]{1,0:T(8,128)(2,1)} async-done(((bf16[128,1024]{1,0:T(8,128)(2,1)}), bf16[4096,1024]{1,0:T(8,128)(2,1)}) %all-gather.2.cloned.1.call-update) | async-done | bytes 8388624 | tf_op jit(solution)/shard_map/all_gather | solution.py:601
  85.1 1.3 copy-done
  86.4 5.7 %terms_added.3 = bf16[2048,1024]{1,0:T(8,128)(2,1)} custom-call(s32[9]{0:T(128)} %stack.114.refs_0_, bf16[512,512]{1,0:T(8,128)(2,1)} %refs_0_.1, bf16[512,512]{1,0:T(8,128)(2,1)} %copy-done.2, bf16[512,512]{1,0:T(8,128)(2,1)} %copy-done.1, bf16[512,512]{1,0:T(8,128)(2,1)} %copy-done.5, bf16[512,512]{1,0:T(8,128)(2,1)} %copy-done.6, ...), custom_call_target="tpu_custom_call", output_to_operand_aliasing={{}: (11, {})} | custom-call | flops 4000000000 | bytes 4000000 | tf_op jit(solution)/shard_map/terms_added/pallas_call | solution.py:462
  92.8 1.3 copy.35
  94.1 11.4 %products.1 = (f32[512,1024]{1,0:T(8,128)}, f32[1,1024]{1,0:T(1,128)}, f32[512,128]{1,0:T(8,128)}) custom-call(s32[8]{0:T(128)} %stack.52.places, bf16[512,512]{1,0:T(8,128)(2,1)} %refs_0_.1, bf16[512,512]{1,0:T(8,128)(2,1)} %copy-done.2, bf16[512,512]{1,0:T(8,128)(2,1)} %copy-done.1, bf16[512,512]{1,0:T(8,128)(2,1)} %copy-done.5, ...), custom_call_target="tpu_custom_call" | custom-call | flops 12000000000 | bytes 16000000 | tf_op jit(solution)/shard_map/products/pallas_call | solution.py:519
  105.6 18.1 %scan_backward.1 = (bf16[512,1024]{1,0:T(8,128)(2,1)}, bf16[512,1024]{1,0:T(8,128)(2,1)}, bf16[512,256]{1,0:T(8,128)(2,1)}, bf16[512,256]{1,0:T(8,128)(2,1)}, f32[512,16]{1,0:T(8,128)}, /*index=5*/f32[8,128]{1,0:T(8,128)}) custom-call(bf16[512,1024]{1,0:T(8,128)(2,1)} %x_ref.1, bf16[512,1024]{1,0:T(8,128)(2,1)} %g_ref.3, ...), custom_call_target="tpu_custom_call" | custom-call | flops 20000000000 | bytes 10000000 | tf_op jit(solution)/shard_map/scan_backward/pallas_call | solution.py:368
  123.7 0.7 pad_maximum_fusion.2
  124.6 0.9 collective-permute-done.12
  125.5 0.7 fusion
  126.2 1.8 %collective-permute-start.13 = (f32[16,128]{1,0:T(8,128)S(1)}, f32[16,128]{1,0:T(8,128)S(1)}, u32[]{:S(2)}, u32[]{:S(2)}) collective-permute-start(f32[16,128]{1,0:T(8,128)S(1)} %fusion), channel_id=1, source_target_pairs={{0,16},{8,24},{16,0},{24,8},{32,48},{40,56},{48,32},{56,40},{64,80... | collective-permute-start | bytes 24584 | tf_op jit(solution)/shard_map/ppermute | solution.py:658
  128.0 1.9 %collective-permute-done.13 = f32[16,128]{1,0:T(8,128)S(1)} collective-permute-done((f32[16,128]{1,0:T(8,128)S(1)}, f32[16,128]{1,0:T(8,128)S(1)}, u32[]{:S(2)}, u32[]{:S(2)}) %collective-permute-start.13) | collective-permute-done | bytes 8224 | tf_op jit(solution)/shard_map/ppermute | solution.py:658
  129.9 1.2 collective-permute-start.14
  131.0 2.8 %collective-permute-done.14 = f32[16,128]{1,0:T(8,128)S(1)} collective-permute-done((f32[16,128]{1,0:T(8,128)S(1)}, f32[16,128]{1,0:T(8,128)S(1)}, u32[]{:S(2)}, u32[]{:S(2)}) %collective-permute-start.14) | collective-permute-done | bytes 8224 | tf_op jit(solution)/shard_map/ppermute | solution.py:658
  133.8 2.1 %collective-permute-start.15 = (f32[16,128]{1,0:T(8,128)S(1)}, f32[16,128]{1,0:T(8,128)S(1)}, u32[]{:S(2)}, u32[]{:S(2)}) collective-permute-start(f32[16,128]{1,0:T(8,128)S(1)} %add.127), channel_id=1, source_target_pairs={{0,64},{8,72},{16,80},{24,88},{32,96},{40,104},{48,112},{56,120},{... | collective-permute-start | bytes 24584 | tf_op jit(solution)/shard_map/ppermute | solution.py:658
  135.9 2.8 %collective-permute-done.15 = f32[16,128]{1,0:T(8,128)S(1)} collective-permute-done((f32[16,128]{1,0:T(8,128)S(1)}, f32[16,128]{1,0:T(8,128)S(1)}, u32[]{:S(2)}, u32[]{:S(2)}) %collective-permute-start.15) | collective-permute-done | bytes 8224 | tf_op jit(solution)/shard_map/ppermute | solution.py:658
  138.7 4.5 %collective-permute-start.16 = (f32[16,128]{1,0:T(8,128)S(1)}, f32[16,128]{1,0:T(8,128)S(1)}, u32[]{:S(2)}, u32[]{:S(2)}) collective-permute-start(f32[16,128]{1,0:T(8,128)S(1)} %add.128), channel_id=1, source_target_pairs={{0,128},{8,136},{16,144},{24,152},{32,160},{40,168},{48,176},{56,1... | collective-permute-start | bytes 24584 | tf_op jit(solution)/shard_map/ppermute | solution.py:658
  143.3 1.1 pad_maximum_fusion.1
  144.3 1.7 %copy.33 = f32[512,16]{0,1:T(8,128)} copy(f32[512,16]{1,0:T(8,128)} %get-tuple-element.70) | data formatting | bytes 65536
  146.0 1.3 copy.32
  148.0 1.0 slice.49
  148.9 1.5 collective-permute-start.11
  151.6 5.6 %collective-permute-done.11 = bf16[128,1024]{1,0:T(8,128)(2,1)S(1)} collective-permute-done((bf16[128,1024]{1,0:T(8,128)(2,1)S(1)}, bf16[128,1024]{1,0:T(8,128)(2,1)S(1)}, u32[]{:S(2)}, u32[]{:S(2)}) %collective-permute-start.11) | collective-permute-done | bytes 262176 | tf_op jit(solution)/shard_map/ppermute | solution.py:646
  157.1 1.8 %add_multiply_fusion = f32[128,1024]{1,0:T(8,128)} fusion(bf16[128,1024]{1,0:T(8,128)(2,1)S(1)} %collective-permute-done.11, bf16[256,1024]{1,0:T(8,128)(2,1)} %reduce-scatter.2.cloned.1.call-done), kind=kLoop, calls=%fused_computation.2 | loop fusion | flops 524288 | bytes 1048576 | tf_op jit(solution)/shard_map/mul | solution.py:647
  (63 shorter events, 7.1 us)
Async XLA Ops:
  7.2 10.9 %copy-start.10 = (f32[16]{0:T(128)S(1)}, f32[16]{0:T(128)}, u32[]{:S(2)}) copy-start(f32[16]{0:T(128)} %param.15) | copy-start | bytes 196
  7.2 11.6 %copy-start.9 = (f32[16]{0:T(128)S(1)}, f32[16]{0:T(128)}, u32[]{:S(2)}) copy-start(f32[16]{0:T(128)} %param.14) | copy-start | bytes 196
  7.2 12.3 %copy-start.11 = (f32[16]{0:T(128)S(1)}, f32[16]{0:T(128)}, u32[]{:S(2)}) copy-start(f32[16]{0:T(128)} %param.16) | copy-start | bytes 196
  7.2 13.0 %copy-start.7 = (bf16[512,16]{0,1:T(8,128)(2,1)S(1)}, bf16[512,16]{0,1:T(8,128)(2,1)}, u32[]{:S(2)}) copy-start(bf16[512,16]{0,1:T(8,128)(2,1)} %param.13) | copy-start | bytes 49156
  7.2 77.9 %all-gather.2.cloned.1.call-start = ((), (), s32[]{:S(2)}) async-start(), calls=%async_computation.1 | async-start | bytes 8650752 | tf_op jit(solution)/shard_map/all_gather | solution.py:601
  8.0 140.0 %reduce-scatter.2.cloned.1.call-start = ((), (), s32[]{:S(2)}) async-start(), calls=%async_computation.2 | async-start | bytes 4718592 | tf_op jit(solution)/shard_map/reduce_scatter | solution.py:643
  8.0 16.4 %collective-permute-start.2 = (bf16[512,512]{1,0:T(8,128)(2,1)}, bf16[512,512]{1,0:T(8,128)(2,1)S(1)}, u32[]{:S(2)}, u32[]{:S(2)}) collective-permute-start(bf16[512,512]{1,0:T(8,128)(2,1)} %refs_0_.1), channel_id=1, source_target_pairs={{0,6},{1,7},{2,0},{3,1},{4,2},{5,3},{6,4},{7,5},{8,14},{9,15},{10,... | collective-permute-start | bytes 1572872 | tf_op jit(solution)/shard_map/ppermute | solution.py:556
  8.9 15.5 %collective-permute-start.1 = (bf16[512,512]{1,0:T(8,128)(2,1)}, bf16[512,512]{1,0:T(8,128)(2,1)S(1)}, u32[]{:S(2)}, u32[]{:S(2)}) collective-permute-start(bf16[512,512]{1,0:T(8,128)(2,1)} %refs_0_.1), channel_id=1, source_target_pairs={{0,2},{1,3},{2,4},{3,5},{4,6},{5,7},{6,0},{7,1},{8,10},{9,11},{10,... | collective-permute-start | bytes 1572872 | tf_op jit(solution)/shard_map/ppermute | solution.py:556
  11.3 15.6 %collective-permute-start = (bf16[512,512]{1,0:T(8,128)(2,1)}, bf16[512,512]{1,0:T(8,128)(2,1)S(1)}, u32[]{:S(2)}, u32[]{:S(2)}) collective-permute-start(bf16[512,512]{1,0:T(8,128)(2,1)} %refs_0_.1), channel_id=1, source_target_pairs={{0,1},{1,0},{2,3},{3,2},{4,5},{5,4},{6,7},{7,6},{8,9},{9,8},{10,11... | collective-permute-start | bytes 1572872 | tf_op jit(solution)/shard_map/ppermute | solution.py:603
  24.4 23.1 %copy-start.1 = (bf16[512,512]{1,0:T(8,128)(2,1)}, bf16[512,512]{1,0:T(8,128)(2,1)S(1)}, u32[]{:S(2)}) copy-start(bf16[512,512]{1,0:T(8,128)(2,1)S(1)} %collective-permute-done.2.refs_3_.refs_2_) | copy-start | bytes 1572868
  24.4 23.1 %copy-start.2 = (bf16[512,512]{1,0:T(8,128)(2,1)}, bf16[512,512]{1,0:T(8,128)(2,1)S(1)}, u32[]{:S(2)}) copy-start(bf16[512,512]{1,0:T(8,128)(2,1)S(1)} %collective-permute-done.1.refs_2_.refs_1_) | copy-start | bytes 1572868
  26.9 20.6 %copy-start.6 = (bf16[512,512]{1,0:T(8,128)(2,1)}, bf16[512,512]{1,0:T(8,128)(2,1)S(1)}, u32[]{:S(2)}) copy-start(bf16[512,512]{1,0:T(8,128)(2,1)S(1)} %collective-permute-done.refs_5_.refs_4_) | copy-start | bytes 1572868
  27.0 20.6 %collective-permute-start.4 = (bf16[512,512]{1,0:T(8,128)(2,1)S(1)}, bf16[512,512]{1,0:T(8,128)(2,1)S(1)}, u32[]{:S(2)}, u32[]{:S(2)}) collective-permute-start(bf16[512,512]{1,0:T(8,128)(2,1)S(1)} %collective-permute-done.refs_5_.refs_4_), channel_id=1, source_target_pairs={{0,6},{1,7},{2,0},{3,1},{4,2},{5,3},{6,4},{7,5},{8,14},{9,15},{10,... | collective-permute-start | bytes 1572872 | tf_op jit(solution)/shard_map/ppermute | solution.py:556
  27.0 20.6 %collective-permute-start.3 = (bf16[512,512]{1,0:T(8,128)(2,1)S(1)}, bf16[512,512]{1,0:T(8,128)(2,1)S(1)}, u32[]{:S(2)}, u32[]{:S(2)}) collective-permute-start(bf16[512,512]{1,0:T(8,128)(2,1)S(1)} %collective-permute-done.refs_5_.refs_4_), channel_id=1, source_target_pairs={{0,2},{1,3},{2,4},{3,5},{4,6},{5,7},{6,0},{7,1},{8,10},{9,11},{10,... | collective-permute-start | bytes 1572872 | tf_op jit(solution)/shard_map/ppermute | solution.py:556
  30.3 17.3 %collective-permute-start.6 = (bf16[256,512]{1,0:T(8,128)(2,1)S(1)}, bf16[256,512]{1,0:T(8,128)(2,1)S(1)}, u32[]{:S(2)}, u32[]{:S(2)}) collective-permute-start(bf16[256,512]{1,0:T(8,128)(2,1)S(1)} %slice.37), channel_id=1, source_target_pairs={{0,6},{1,7},{2,0},{3,1},{4,2},{5,3},{6,4},{7,5},{8,14},{9,15},{10,... | collective-permute-start | bytes 786440 | tf_op jit(solution)/shard_map/ppermute | solution.py:562
  30.3 17.2 %collective-permute-start.5 = (bf16[256,512]{1,0:T(8,128)(2,1)S(1)}, bf16[256,512]{1,0:T(8,128)(2,1)S(1)}, u32[]{:S(2)}, u32[]{:S(2)}) collective-permute-start(bf16[256,512]{1,0:T(8,128)(2,1)S(1)} %slice.36), channel_id=1, source_target_pairs={{0,2},{1,3},{2,4},{3,5},{4,6},{5,7},{6,0},{7,1},{8,10},{9,11},{10,... | collective-permute-start | bytes 786440 | tf_op jit(solution)/shard_map/ppermute | solution.py:561
  47.6 3.5 %copy-start.3 = (bf16[512,512]{1,0:T(8,128)(2,1)}, bf16[512,512]{1,0:T(8,128)(2,1)S(1)}, u32[]{:S(2)}) copy-start(bf16[512,512]{1,0:T(8,128)(2,1)S(1)} %collective-permute-done.4.refs_7_.refs_6_) | copy-start | bytes 1572868
  47.6 3.4 %copy-start.4 = (bf16[512,512]{1,0:T(8,128)(2,1)}, bf16[512,512]{1,0:T(8,128)(2,1)S(1)}, u32[]{:S(2)}) copy-start(bf16[512,512]{1,0:T(8,128)(2,1)S(1)} %collective-permute-done.3.refs_6_.refs_5_) | copy-start | bytes 1572868
  47.7 13.8 %collective-permute-start.8 = (bf16[256,512]{1,0:T(8,128)(2,1)S(1)}, bf16[256,512]{1,0:T(8,128)(2,1)S(1)}, u32[]{:S(2)}, u32[]{:S(2)}) collective-permute-start(bf16[256,512]{1,0:T(8,128)(2,1)S(1)} %slice.41), channel_id=1, source_target_pairs={{0,6},{1,7},{2,0},{3,1},{4,2},{5,3},{6,4},{7,5},{8,14},{9,15},{10,... | collective-permute-start | bytes 786440 | tf_op jit(solution)/shard_map/ppermute | solution.py:562
  47.7 13.7 %collective-permute-start.7 = (bf16[256,512]{1,0:T(8,128)(2,1)S(1)}, bf16[256,512]{1,0:T(8,128)(2,1)S(1)}, u32[]{:S(2)}, u32[]{:S(2)}) collective-permute-start(bf16[256,512]{1,0:T(8,128)(2,1)S(1)} %slice.40), channel_id=1, source_target_pairs={{0,2},{1,3},{2,4},{3,5},{4,6},{5,7},{6,0},{7,1},{8,10},{9,11},{10,... | collective-permute-start | bytes 786440 | tf_op jit(solution)/shard_map/ppermute | solution.py:561
  51.0 0.8 copy-start.5
  65.3 5.7 %collective-permute-start.10 = (bf16[1024,1024]{1,0:T(8,128)(2,1)}, bf16[1024,1024]{1,0:T(8,128)(2,1)}, u32[]{:S(2)}, u32[]{:S(2)}) collective-permute-start(bf16[1024,1024]{1,0:T(8,128)(2,1)} %terms.7), channel_id=1, source_target_pairs={{0,8},{8,0},{16,24},{24,16},{32,40},{40,32},{48,56},{56,48},{64,72... | collective-permute-start | bytes 6291464 | tf_op jit(solution)/shard_map/ppermute | solution.py:636
  69.1 16.0 %collective-permute-start.9 = (bf16[1024,1024]{1,0:T(8,128)(2,1)}, bf16[1024,1024]{1,0:T(8,128)(2,1)S(1)}, u32[]{:S(2)}, u32[]{:S(2)}) collective-permute-start(bf16[1024,1024]{1,0:T(8,128)(2,1)} %terms.6), channel_id=1, source_target_pairs={{0,8},{8,0},{16,24},{24,16},{32,40},{40,32},{48,56},{56,48},{64,72... | collective-permute-start | bytes 6291464 | tf_op jit(solution)/shard_map/ppermute | solution.py:636
  85.1 1.3 copy-start
  105.6 18.1 %copy-start.8 = (f32[1,1024]{1,0:T(1,128)S(1)}, f32[1,1024]{1,0:T(1,128)}, u32[]{:S(2)}) copy-start(f32[1,1024]{1,0:T(1,128)} %get-tuple-element.66) | copy-start | bytes 12292
  124.4 1.2 collective-permute-start.12
  126.2 3.7 %collective-permute-start.13 = (f32[16,128]{1,0:T(8,128)S(1)}, f32[16,128]{1,0:T(8,128)S(1)}, u32[]{:S(2)}, u32[]{:S(2)}) collective-permute-start(f32[16,128]{1,0:T(8,128)S(1)} %fusion), channel_id=1, source_target_pairs={{0,16},{8,24},{16,0},{24,8},{32,48},{40,56},{48,32},{56,40},{64,80... | collective-permute-start | bytes 24584 | tf_op jit(solution)/shard_map/ppermute | solution.py:658
  129.9 4.0 %collective-permute-start.14 = (f32[16,128]{1,0:T(8,128)S(1)}, f32[16,128]{1,0:T(8,128)S(1)}, u32[]{:S(2)}, u32[]{:S(2)}) collective-permute-start(f32[16,128]{1,0:T(8,128)S(1)} %add.126), channel_id=1, source_target_pairs={{0,32},{8,40},{16,48},{24,56},{32,0},{40,8},{48,16},{56,24},{64,96... | collective-permute-start | bytes 24584 | tf_op jit(solution)/shard_map/ppermute | solution.py:658
  133.8 4.9 %collective-permute-start.15 = (f32[16,128]{1,0:T(8,128)S(1)}, f32[16,128]{1,0:T(8,128)S(1)}, u32[]{:S(2)}, u32[]{:S(2)}) collective-permute-start(f32[16,128]{1,0:T(8,128)S(1)} %add.127), channel_id=1, source_target_pairs={{0,64},{8,72},{16,80},{24,88},{32,96},{40,104},{48,112},{56,120},{... | collective-permute-start | bytes 24584 | tf_op jit(solution)/shard_map/ppermute | solution.py:658
  138.7 8.6 %collective-permute-start.16 = (f32[16,128]{1,0:T(8,128)S(1)}, f32[16,128]{1,0:T(8,128)S(1)}, u32[]{:S(2)}, u32[]{:S(2)}) collective-permute-start(f32[16,128]{1,0:T(8,128)S(1)} %add.128), channel_id=1, source_target_pairs={{0,128},{8,136},{16,144},{24,152},{32,160},{40,168},{48,176},{56,1... | collective-permute-start | bytes 24584 | tf_op jit(solution)/shard_map/ppermute | solution.py:658
  148.9 8.2 %collective-permute-start.11 = (bf16[128,1024]{1,0:T(8,128)(2,1)S(1)}, bf16[128,1024]{1,0:T(8,128)(2,1)S(1)}, u32[]{:S(2)}, u32[]{:S(2)}) collective-permute-start(bf16[128,1024]{1,0:T(8,128)(2,1)S(1)} %slice.49), channel_id=1, source_target_pairs={{0,16},{8,24},{16,0},{24,8},{32,48},{40,56},{48,32},{56,40},{64,80... | collective-permute-start | bytes 786440 | tf_op jit(solution)/shard_map/ppermute | solution.py:646
Sparse Core Ops, SparseCore 0:
  9.9 75.1 all-gather.1
  92.3 55.6 reduce-scatter.1
where the time goes:
time: 167 us; the launch traced here: 166 us
  Pallas kernels  70.7 us (42%)
  starting transfers between devices  28.4 us (17%)
  waiting for transfers between devices  26.1 us (16%)
  local copies, waits for them, and re-layouts  19.7 us (12%)
  between operations  14.5 us (9%)
  other arithmetic  6.4 us (4%)
    pallas_call x6, Pallas kernels, terms(): pl.pallas_call(kernel, grid_spec=pltpu.PrefetchScalarGridSpec(num_scalar_...  27.2 us
    pallas_call x1, Pallas kernels, scan_backward(): pl.pallas_call(backward_kernel, grid=(PAIRS,), in_specs=[by_pair(TOKENS),...  18.1 us
    pallas_call x1, Pallas kernels, scan_forward(): pl.pallas_call(forward_kernel, grid=(PAIRS,), in_specs=[by_pair(TOKENS),...  13.9 us
    pallas_call x1, Pallas kernels, products(): pl.pallas_call(product_kernel, grid_spec=pltpu.PrefetchScalarGridSpec(num...  11.4 us
    ppermute x5, starting transfers between devices, shards(): summed = summed + lax.ppermute(summed, 'blk', swap(bit))  9.78 us
    ppermute x5, waiting for transfers between devices, shards(): summed = summed + lax.ppermute(summed, 'blk', swap(bit))  8.43 us
    all_gather x1, waiting for transfers between devices, shards(): rows = lax.all_gather(out_proj, 'blk', axis=0, tiled=True)  8.24 us
    unnamed x29, local copies, waits for them, and re-layouts  6.61 us
  transfers between devices with their start and end apart: 19, of which 8 were waited for; matrix products, arithmetic and copies ran while one was open for 13% of the time, Pallas kernels for 39%

commit v1 on v0

--- a/solution.py
+++ b/solution.py
@@ -167,7 +167,7 @@
             mean = jnp.sum(squares[rows, :], axis=1, keepdims=True) * (1.0 / CHANNELS)
             scale = lax.rsqrt(mean + EPS)
             scale_ref[rows, :] = jnp.broadcast_to(scale, (CHUNK, LANES))
-            low_ref[rows, :] = (gated_ref[rows, :] * scale * gain_ref[...]).astype(BF16)
+            low_ref[:, rows] = (gated_ref[rows, :] * scale * gain_ref[...]).T.astype(BF16)
 
 
 def backward_kernel(x_ref, g_ref, cot_ref, scan_ref, state_ref, scale_ref, pull_ref,
@@ -344,14 +344,14 @@
         ]
         + PARAMETERS,
         out_specs=[
-            whole((TOKENS, CHANNELS)),
+            whole((CHANNELS, TOKENS)),
             by_pair(TOKENS),
             whole((TOKENS, CHANNELS)),
             pl.BlockSpec((1, CHUNKS - 1, STATE, LANES), lambda p: (p, 0, 0, 0)),
             whole((TOKENS, LANES)),
         ],
         out_shape=[
-            jax.ShapeDtypeStruct((TOKENS, CHANNELS), BF16),
+            jax.ShapeDtypeStruct((CHANNELS, TOKENS), BF16),
             jax.ShapeDtypeStruct((TOKENS, CHANNELS), F32),
             jax.ShapeDtypeStruct((TOKENS, CHANNELS), F32),
             jax.ShapeDtypeStruct((PAIRS, CHUNKS - 1, STATE, LANES), F32),
@@ -417,70 +417,94 @@
 SHARDS = 8
 
 
-def term_kernel(count, added, slot, slots, places, *refs):
-    pieces, low_ref = refs[:count], refs[count]
-    sent_ref = refs[count + 1] if added else None
+def term_kernel(count, added, placed, places, *refs):
+    pieces, low_ref = refs[: 2 * count], refs[2 * count]
+    sent_ref = refs[2 * count + 1] if added else None
     out_ref, held, done = refs[-3:]
-    turned = jnp.concatenate([piece[...] for piece in pieces], axis=1).T
-    for n in range(CHANNELS // COLUMNS):
-        cols = slice(n * COLUMNS, (n + 1) * COLUMNS)
-        term = dot(turned, low_ref[:, cols])
-        for k in range(count):
-            part = term[k * BLOCK : (k + 1) * BLOCK]
-            if added:
-                row = pl.multiple_of(places[k] * BLOCK, BLOCK)
-                part = part + sent_ref[pl.ds(row, BLOCK), cols].astype(F32)
-            held[k * BLOCK : (k + 1) * BLOCK, cols] = part.astype(BF16)
     copies = []
     for k in range(count):
-        row = pl.multiple_of((places[k] * slots + slot) * BLOCK, BLOCK)
-        copies.append(
-            pltpu.make_async_copy(
-                held.at[k * BLOCK : (k + 1) * BLOCK], out_ref.at[pl.ds(row, BLOCK)], done.at[k]
+        blocks = [piece[...] for piece in pieces[2 * k : 2 * k + 2]]
+        term = dot(low_ref[...], jnp.concatenate(blocks, axis=1))
+        for slot in range(2):
+            n = 2 * k + slot
+            here = slice(n * CHANNELS, (n + 1) * CHANNELS)
+            part = term[:, slot * BLOCK : (slot + 1) * BLOCK]
+            if added:
+                part = part + sent_ref[here, :].astype(F32)
+            held[here, :] = part.astype(BF16)
+            start = n * CHANNELS
+            if placed:
+                start = pl.multiple_of((places[k] * 2 + slot) * CHANNELS, CHANNELS)
+            copies.append(
+                pltpu.make_async_copy(
+                    held.at[here], out_ref.at[pl.ds(start, CHANNELS)], done.at[n]
+                )
             )
-        )
-        copies[-1].start()
+            copies[-1].start()
     for copy in copies:
         copy.wait()
 
 
-def terms(places, block, pieces, low, sent=None, base=None, slot=0, slots=1):
+def terms(places, blocks, pieces, low, sent=None, base=None):
     count = len(pieces)
-    rows = SHARDS * slots * BLOCK
+    added = sent is not None
+    rows = 2 * CHANNELS * (SHARDS if added else count)
     more, specs, aliases = [], [], {}
-    if sent is not None:
+    if added:
         more.append(sent)
-        specs.append(whole((SHARDS * BLOCK, CHANNELS)))
+        specs.append(whole((2 * CHANNELS * count, BLOCK)))
     if base is not None:
-        aliases = {2 + count + len(more): 0}
+        aliases = {2 + 2 * count + len(more): 0}
         more.append(base)
         specs.append(pl.BlockSpec(memory_space=pl.ANY))
 
     def kernel(*refs):
-        term_kernel(count, sent is not None, slot, slots, *refs)
+        term_kernel(count, added, added, *refs)
+
+    def lanes(slot):
+        return pl.BlockSpec((TOKENS, BLOCK), lambda _, at: (0, at[count + slot]))
 
     return pl.pallas_call(
         kernel,
         grid_spec=pltpu.PrefetchScalarGridSpec(
             num_scalar_prefetch=1,
             grid=(1,),
-            in_specs=[pl.BlockSpec((TOKENS, BLOCK), lambda _, at: (0, at[count]))] * count
-            + [whole((TOKENS, CHANNELS))]
-            + specs,
+            in_specs=[lanes(0), lanes(1)] * count + [whole((CHANNELS, TOKENS))] + specs,
             out_specs=pl.BlockSpec(memory_space=pl.ANY),
             scratch_shapes=[
-                pltpu.VMEM((count * BLOCK, CHANNELS), BF16),
-                pltpu.SemaphoreType.DMA((count,)),
+                pltpu.VMEM((2 * count * CHANNELS, BLOCK), BF16),
+                pltpu.SemaphoreType.DMA((2 * count,)),
             ],
         ),
-        out_shape=jax.ShapeDtypeStruct((rows, CHANNELS), BF16),
+        out_shape=jax.ShapeDtypeStruct((rows, BLOCK), BF16),
         input_output_aliases=aliases,
         compiler_params=pltpu.CompilerParams(vmem_limit_bytes=VMEM_LIMIT),
         cost_estimate=pl.CostEstimate(
-            flops=count * 5 * 10**8, bytes_accessed=4 * 10**6, transcendentals=0
+            flops=(count + 1) * 7 * 10**8, bytes_accessed=2 * 10**6, transcendentals=0
         ),
-        name="terms" if sent is None else "terms_added",
-    )(jnp.stack(list(places) + [block]).astype(jnp.int32), *pieces, low, *more)
+        name="terms_added" if added else "terms",
+    )(
+        jnp.stack(list(places) + list(blocks)).astype(jnp.int32),
+        *[piece for piece in pieces for _ in range(2)],
+        low,
+        *more,
+    )
+
+
+def finish_kernel(scale, kept_ref, given_ref, out_ref):
+    total = kept_ref[...].astype(F32) + given_ref[...].astype(F32)
+    out_ref[...] = (total * scale).T
+
+
+def finish(plane, given, scale):
+    return pl.pallas_call(
+        lambda *refs: finish_kernel(scale, *refs),
+        grid=(1,),
+        in_specs=[pl.BlockSpec((CHANNELS, BLOCK), lambda _: (1, 0)), whole((CHANNELS, BLOCK))],
+        out_specs=whole((BLOCK, CHANNELS)),
+        out_shape=jax.ShapeDtypeStruct((BLOCK, CHANNELS), F32),
+        name="finish",
+    )(plane, given)
 
 
 COLUMNS = 256
@@ -598,6 +622,7 @@
     norm_scale = 1.0 / math.sqrt(TOKENS * 32)
     block = lax.axis_index("blk")
     core, y_lo = block % 2, block // 2 % 2
+    by_z = [[z * 4 + rest for z in range(8)] for rest in range(4)]
     rows = lax.all_gather(out_proj, "blk", axis=0, tiled=True)
     own = out_cotangent
     partner = lax.ppermute(own, "tp", [(t, t ^ 1) for t in range(8)])
@@ -617,7 +642,7 @@
         (partner_before, partner_after, far_parts, low)
     )
     far = jnp.concatenate(far_parts, axis=0)
-    partner_far = jnp.concatenate(beyond(partner_before, partner_after), axis=0)
+    partner_far = beyond(partner_before, partner_after)
     early = [own, before, after, far, partner, partner_before, partner_after]
     me = lax.axis_index("tp")
     x, h = me // 2, me % 2
@@ -626,29 +651,27 @@
     mine, mine_y = 2 * y_lo + core, 2 * (1 - y_lo) + core
     theirs, theirs_y = 2 * y_lo + 1 - core, 2 * (1 - y_lo) + 1 - core
 
-    base_y = terms(places[:-1], theirs_y, early, low)
-    base = terms(places[:-1], theirs, early, low)
-    base_y, base, partner_far = lax.optimization_barrier((base_y, base, partner_far))
-    pieces = early + [partner_far]
-
-    def sent_of(block, base):
-        full = terms(places[-1:], block, pieces[-1:], low, base=base)
-        return lax.ppermute(full, "blk", swap(1))
-
-    sent_y, sent = sent_of(theirs_y, base_y), sent_of(theirs, base)
-    both = terms(places, mine_y, pieces, low, sent_y, slots=2)
-    rows, low = lax.optimization_barrier((rows, low))
-    both = terms(places, mine, pieces, low, sent, base=both, slot=1, slots=2)
-    by_z = [[z * 4 + rest for z in range(8)] for rest in range(4)]
+    theirs_early = terms(places[:-1], (theirs_y, theirs), early, low)
+    sent_early = lax.ppermute(theirs_early, "blk", swap(1))
+    partner_far, _ = lax.optimization_barrier((partner_far, theirs_early))
+    last = [jnp.concatenate(partner_far, axis=0)]
+    sent_last = lax.ppermute(terms(places[-1:], (theirs_y, theirs), last, low), "blk", swap(1))
+    both = terms(places[:-1], (mine_y, mine), early, low, sent_early)
+    both = terms(places[-1:], (mine_y, mine), last, low, sent_last, base=both)
     plane = lax.psum_scatter(
         both, "blk", scatter_dimension=0, tiled=True, axis_index_groups=by_z
     )
-    given = lax.ppermute(plane[:BLOCK], "blk", swap(2))
-    weight_grad = (plane[BLOCK:].astype(F32) + given.astype(F32)) * norm_scale
+    given = lax.ppermute(plane[:CHANNELS], "blk", swap(2))
+    weight_grad = finish(plane, given, norm_scale)
 
     rows, _ = lax.optimization_barrier((rows, both))
     cot, gain_grad, pull = products(
-        jnp.stack(places).astype(jnp.int32), pieces, rows, gated, scale, parameters[-1]
+        jnp.stack(places).astype(jnp.int32),
+        early + last,
+        rows,
+        gated,
+        scale,
+        parameters[-1],
     )
     dx, dg, db, dc, step_grad, small = scan_backward(
         scan_input, gate_input, cot, scan, states, scale, pull, b, c, c.T, parameters

time: 167 us -> 253 us (1.51)
  waiting for transfers between devices: 26.1 us -> 118 us
  Pallas kernels: 70.7 us -> 65.5 us
  local copies, waits for them, and re-layouts: 19.7 us -> 24.5 us
  starting transfers between devices: 28.4 us -> 24.4 us
  other arithmetic: 6.4 us -> 3.74 us
    reduce_scatter x1, waiting for transfers between devices: 0.61 us -> 68.9 us  [shards(): lax.psum_scatter(both, 'blk', scatter_dimension=0, tiled=True, axis_index...]
    all_gather x1, waiting for transfers between devices: 8.24 us -> 32.9 us  [shards(): rows = lax.all_gather(out_proj, 'blk', axis=0, tiled=True)]
    pallas_call x6 -> x4, Pallas kernels: 27.2 us -> 19.8 us  [terms(): pl.pallas_call(kernel, grid_spec=pltpu.PrefetchScalarGridSpec(num_scalar_...]
    ppermute x3, waiting for transfers between devices: 5.57 us -> 0.01 us  [the longest x1 0.01 us: shards(): given = lax.ppermute(plane[:CHANNELS], 'blk', swap(2))]
    ppermute x2, waiting for transfers between devices: 0.01 us -> 4.88 us  [beyond(): top = lax.ppermute(before[:half], 'tp', along_x(1))]
    ppermute x2, starting transfers between devices: 5.66 us -> 1.11 us  [beside(): lax.ppermute(shard, 'tp', along_x(1))]
    ppermute x2, waiting for transfers between devices: 0.01 us -> 4 us  [beyond(): low = lax.ppermute(after[half:], 'tp', along_x(-1))]
    ppermute x2, starting transfers between devices: 6.45 us -> 3.61 us  [beyond(): top = lax.ppermute(before[:half], 'tp', along_x(1))]
  transfers between devices with their start and end apart: 19 -> 19, of which waited for: 8 -> 10; matrix products, arithmetic and copies ran while one was open for 13% -> 9% of each run, Pallas kernels for 39% -> 22%
where the time goes in v1:
time: 253 us; the launch traced here: 252 us
  waiting for transfers between devices  118 us (47%)
  Pallas kernels  65.5 us (26%)
  local copies, waits for them, and re-layouts  24.5 us (10%)
  starting transfers between devices  24.4 us (10%)
  between operations  15.7 us (6%)
  other arithmetic  3.74 us (1%)
    reduce_scatter x1, waiting for transfers between devices, shards(): lax.psum_scatter(both, 'blk', scatter_dimension=0, tiled=True, axis_index...  68.9 us
    all_gather x1, waiting for transfers between devices, shards(): rows = lax.all_gather(out_proj, 'blk', axis=0, tiled=True)  32.9 us
    pallas_call x4, Pallas kernels, terms(): pl.pallas_call(kernel, grid_spec=pltpu.PrefetchScalarGridSpec(num_scalar_...  19.8 us
    pallas_call x1, Pallas kernels, scan_backward(): pl.pallas_call(backward_kernel, grid=(PAIRS,), in_specs=[by_pair(TOKENS),...  18.1 us
    pallas_call x1, Pallas kernels, scan_forward(): pl.pallas_call(forward_kernel, grid=(PAIRS,), in_specs=[by_pair(TOKENS),...  14.1 us
    pallas_call x1, Pallas kernels, products(): pl.pallas_call(product_kernel, grid_spec=pltpu.PrefetchScalarGridSpec(num...  11.4 us
    ppermute x5, starting transfers between devices, shards(): summed = summed + lax.ppermute(summed, 'blk', swap(bit))  10.8 us
    unnamed x28, local copies, waits for them, and re-layouts  8.26 us
  transfers between devices with their start and end apart: 19, of which 10 were waited for; matrix products, arithmetic and copies ran while one was open for 9% of the time, Pallas kernels for 22%

profile of v1, /device:TPU:6, one launch (start us, length us, event | category | flops | bytes accessed | tf_op | source)
XLA Modules:
  0.0 252.3 jit_solution(13751907627873002412)
XLA Ops:
  8.1 3.3 %collective-permute-start = (bf16[512,512]{1,0:T(8,128)(2,1)}, bf16[512,512]{1,0:T(8,128)(2,1)S(1)}, u32[]{:S(2)}, u32[]{:S(2)}) collective-permute-start(bf16[512,512]{1,0:T(8,128)(2,1)} %refs_0_.1), channel_id=1, source_target_pairs={{0,1},{1,0},{2,3},{3,2},{4,5},{5,4},{6,7},{7,6},{8,9},{9,8},{10,11... | collective-permute-start | bytes 1572872 | tf_op jit(solution)/shard_map/ppermute | solution.py:628
  11.8 1.5 collective-permute-start.2
  13.4 2.1 fusion.1
  15.5 1.3 copy.34
  16.8 0.8 copy.22
  17.6 0.7 broadcast_in_dim.3
  19.0 1.3 copy.25.bias_t_ref
  20.4 1.3 copy.26.rate_t_ref
  23.0 1.3 pad_bitcast_fusion
  24.3 0.9 copy_bitcast_fusion
  25.2 1.1 collective-permute-done.2.refs_5_.refs_6_.refs_2_
  27.0 1.4 collective-permute-start.4
  28.4 1.9 collective-permute-start.5
  30.6 14.1 %scan_forward.1 = (bf16[1024,512]{1,0:T(8,128)(2,1)}, f32[512,1024]{1,0:T(8,128)}, f32[512,1024]{1,0:T(8,128)}, f32[8,3,256,128]{3,2,1,0:T(8,128)}, f32[512,128]{1,0:T(8,128)}) custom-call(bf16[512,1024]{1,0:T(8,128)(2,1)} %x_ref.1, bf16[512,1024]{1,0:T(8,128)(2,1)} %g_ref.3, bf16[512,256]{1,0:T(8,128)(2,1)} %get-tuple-element.76.b_ref, ...), custom_call_target="tpu_custom_call" | custom-call | flops 16000000000 | bytes 10000000 | tf_op jit(solution)/shard_map/scan_forward/pallas_call | solution.py:335
  44.7 1.6 collective-permute-done.6
  46.4 0.7 copy-done.6
  47.3 0.8 copy-done.8
  48.1 6.0 %terms.2 = bf16[14336,128]{1,0:T(8,128)(2,1)} custom-call(s32[9]{0:T(128)} %stack.91.refs_0_, bf16[512,512]{1,0:T(8,128)(2,1)} %refs_0_.1, bf16[512,512]{1,0:T(8,128)(2,1)} %refs_0_.1, bf16[512,512]{1,0:T(8,128)(2,1)} %copy-done.4, bf16[512,512]{1,0:T(8,128)(2,1)} %copy-done.4, bf16[512,512]{1,0:T(8,128)(2,1)} %copy-done.5, bf16[512,512]{1,0:T(8,128)(2,1)} %copy-done.5, ...), custom_call_target="tpu_custom_call" | custom-call | flops 5600000000 | bytes 2000000 | tf_op jit(solution)/shard_map/terms/pallas_call | solution.py:467
  54.2 1.0 slice.37
  55.2 1.0 slice.38
  56.1 1.7 collective-permute-start.7
  60.2 4.9 %collective-permute-done.7 = bf16[256,512]{1,0:T(8,128)(2,1)S(1)} collective-permute-done((bf16[256,512]{1,0:T(8,128)(2,1)S(1)}, bf16[256,512]{1,0:T(8,128)(2,1)S(1)}, u32[]{:S(2)}, u32[]{:S(2)}) %collective-permute-start.7) | collective-permute-done | bytes 262176 | tf_op jit(solution)/shard_map/ppermute | solution.py:585
  65.1 2.4 collective-permute-done.8
  67.5 0.8 copy-done
  68.3 3.3 %terms.3 = bf16[2048,128]{1,0:T(8,128)(2,1)} custom-call(s32[3]{0:T(128)} %pad_add_fusion.1.refs_0_, bf16[512,512]{1,0:T(8,128)(2,1)} %copy-done, bf16[512,512]{1,0:T(8,128)(2,1)} %copy-done, bf16[1024,512]{1,0:T(8,128)(2,1)} %get-tuple-element.44.refs_15_.refs_3_), custom_call_target="tpu_custom_call" | custom-call | flops 1400000000 | bytes 2000000 | tf_op jit(solution)/shard_map/terms/pallas_call | solution.py:467
  71.7 7.1 %terms_added.2.refs_5_ = bf16[16384,128]{1,0:T(8,128)(2,1)} custom-call(s32[9]{0:T(128)} %stack.96.refs_0_, bf16[512,512]{1,0:T(8,128)(2,1)} %refs_0_.1, bf16[512,512]{1,0:T(8,128)(2,1)} %refs_0_.1, bf16[512,512]{1,0:T(8,128)(2,1)} %copy-done.4, bf16[512,512]{1,0:T(8,128)(2,1)} %copy-done.4, bf16[512,512]{1,0:T(8,128)(2,1)} %copy-done.5, ...), custom_call_target="tpu_custom_call" | custom-call | flops 5600000000 | bytes 2000000 | tf_op jit(solution)/shard_map/terms_added/pallas_call | solution.py:467
  78.9 0.8 copy-done.1
  79.7 3.4 %terms_added.3 = bf16[16384,128]{1,0:T(8,128)(2,1)} custom-call(s32[3]{0:T(128)} %pad_add_fusion.refs_0_, bf16[512,512]{1,0:T(8,128)(2,1)} %copy-done, bf16[512,512]{1,0:T(8,128)(2,1)} %copy-done, bf16[1024,512]{1,0:T(8,128)(2,1)} %get-tuple-element.44.refs_15_.refs_3_, bf16[2048,128]{1,0:T(8,128)(2,1)} %copy-done.1, ...), custom_call_target="tpu_custom_call", output_to_operand_aliasing={{}: (5, {})} | custom-call | flops 1400000000 | bytes 2000000 | tf_op jit(solution)/shard_map/terms_added/pallas_call | solution.py:467
  84.4 1.3 copy.33
  85.7 68.9 %reduce-scatter.2.cloned.1.call-done.refs_0_ = bf16[2048,128]{1,0:T(8,128)(2,1)} async-done(((bf16[16384,128]{1,0:T(8,128)(2,1)}), bf16[2048,128]{1,0:T(8,128)(2,1)}) %reduce-scatter.2.cloned.1.call-update) | async-done | bytes 524304 | tf_op jit(solution)/shard_map/reduce_scatter | solution.py:661
  154.6 1.0 slice.44
  155.5 1.6 collective-permute-start.11
  157.1 32.9 %all-gather.2.cloned.1.call-done.refs_8_ = bf16[4096,1024]{1,0:T(8,128)(2,1)} async-done(((bf16[128,1024]{1,0:T(8,128)(2,1)}), bf16[4096,1024]{1,0:T(8,128)(2,1)}) %all-gather.2.cloned.1.call-update) | async-done | bytes 8388624 | tf_op jit(solution)/shard_map/all_gather | solution.py:626
  190.0 11.4 %products.1 = (f32[512,1024]{1,0:T(8,128)}, f32[1,1024]{1,0:T(1,128)}, f32[512,128]{1,0:T(8,128)}) custom-call(s32[8]{0:T(128)} %stack.88.places, bf16[512,512]{1,0:T(8,128)(2,1)} %refs_0_.1, bf16[512,512]{1,0:T(8,128)(2,1)} %copy-done.4, bf16[512,512]{1,0:T(8,128)(2,1)} %copy-done.5, bf16[512,512]{1,0:T(8,128)(2,1)} %copy-done.8, ...), custom_call_target="tpu_custom_call" | custom-call | flops 12000000000 | bytes 16000000 | tf_op jit(solution)/shard_map/products/pallas_call | solution.py:543
  201.4 18.1 %scan_backward.1 = (bf16[512,1024]{1,0:T(8,128)(2,1)}, bf16[512,1024]{1,0:T(8,128)(2,1)}, bf16[512,256]{1,0:T(8,128)(2,1)}, bf16[512,256]{1,0:T(8,128)(2,1)}, f32[512,16]{1,0:T(8,128)}, /*index=5*/f32[8,128]{1,0:T(8,128)}) custom-call(bf16[512,1024]{1,0:T(8,128)(2,1)} %x_ref.1, bf16[512,1024]{1,0:T(8,128)(2,1)} %g_ref.3, ...), custom_call_target="tpu_custom_call" | custom-call | flops 20000000000 | bytes 10000000 | tf_op jit(solution)/shard_map/scan_backward/pallas_call | solution.py:368
  219.6 0.7 pad_maximum_fusion.1
  220.5 0.9 collective-permute-done.12
  222.2 0.7 collective-permute-start.13
  222.9 2.9 %collective-permute-done.13 = f32[16,128]{1,0:T(8,128)S(1)} collective-permute-done((f32[16,128]{1,0:T(8,128)S(1)}, f32[16,128]{1,0:T(8,128)S(1)}, u32[]{:S(2)}, u32[]{:S(2)}) %collective-permute-start.13) | collective-permute-done | bytes 8224 | tf_op jit(solution)/shard_map/ppermute | solution.py:681
  225.8 2.3 collective-permute-start.14
  228.1 1.6 collective-permute-done.14
  229.7 3.6 %collective-permute-start.15 = (f32[16,128]{1,0:T(8,128)S(1)}, f32[16,128]{1,0:T(8,128)S(1)}, u32[]{:S(2)}, u32[]{:S(2)}) collective-permute-start(f32[16,128]{1,0:T(8,128)S(1)} %add.123), channel_id=1, source_target_pairs={{0,64},{8,72},{16,80},{24,88},{32,96},{40,104},{48,112},{56,120},{... | collective-permute-start | bytes 24584 | tf_op jit(solution)/shard_map/ppermute | solution.py:681
  233.4 0.7 copy-done.2
  234.1 2.0 finish.1
  236.1 3.9 %collective-permute-start.16 = (f32[16,128]{1,0:T(8,128)S(1)}, f32[16,128]{1,0:T(8,128)S(1)}, u32[]{:S(2)}, u32[]{:S(2)}) collective-permute-start(f32[16,128]{1,0:T(8,128)S(1)} %add.124), channel_id=1, source_target_pairs={{0,128},{8,136},{16,144},{24,152},{32,160},{40,168},{48,176},{56,1... | collective-permute-start | bytes 24584 | tf_op jit(solution)/shard_map/ppermute | solution.py:681
  240.0 1.1 pad_maximum_fusion
  241.1 1.3 copy.30
  242.4 0.7 copy.31
  (58 shorter events, 10.1 us)
Async XLA Ops:
  8.0 146.6 %reduce-scatter.2.cloned.1.call-start = ((), (), s32[]{:S(2)}) async-start(), calls=%async_computation.2 | async-start | bytes 4718592 | tf_op jit(solution)/shard_map/reduce_scatter | solution.py:661
  8.1 17.1 %collective-permute-start = (bf16[512,512]{1,0:T(8,128)(2,1)}, bf16[512,512]{1,0:T(8,128)(2,1)S(1)}, u32[]{:S(2)}, u32[]{:S(2)}) collective-permute-start(bf16[512,512]{1,0:T(8,128)(2,1)} %refs_0_.1), channel_id=1, source_target_pairs={{0,1},{1,0},{2,3},{3,2},{4,5},{5,4},{6,7},{7,6},{8,9},{9,8},{10,11... | collective-permute-start | bytes 1572872 | tf_op jit(solution)/shard_map/ppermute | solution.py:628
  11.3 13.8 %collective-permute-start.1 = (bf16[512,512]{1,0:T(8,128)(2,1)}, bf16[512,512]{1,0:T(8,128)(2,1)S(1)}, u32[]{:S(2)}, u32[]{:S(2)}) collective-permute-start(bf16[512,512]{1,0:T(8,128)(2,1)} %refs_0_.1), channel_id=1, source_target_pairs={{0,2},{1,3},{2,4},{3,5},{4,6},{5,7},{6,0},{7,1},{8,10},{9,11},{10,... | collective-permute-start | bytes 1572872 | tf_op jit(solution)/shard_map/ppermute | solution.py:580
  11.8 14.5 %collective-permute-start.2 = (bf16[512,512]{1,0:T(8,128)(2,1)}, bf16[512,512]{1,0:T(8,128)(2,1)S(1)}, u32[]{:S(2)}, u32[]{:S(2)}) collective-permute-start(bf16[512,512]{1,0:T(8,128)(2,1)} %refs_0_.1), channel_id=1, source_target_pairs={{0,6},{1,7},{2,0},{3,1},{4,2},{5,3},{6,4},{7,5},{8,14},{9,15},{10,... | collective-permute-start | bytes 1572872 | tf_op jit(solution)/shard_map/ppermute | solution.py:580
  25.2 19.5 %copy-start.10 = (bf16[512,512]{1,0:T(8,128)(2,1)}, bf16[512,512]{1,0:T(8,128)(2,1)S(1)}, u32[]{:S(2)}) copy-start(bf16[512,512]{1,0:T(8,128)(2,1)S(1)} %collective-permute-done.refs_9_.refs_10_.refs_4_) | copy-start | bytes 1572868
  25.2 19.5 %copy-start.4 = (bf16[512,512]{1,0:T(8,128)(2,1)}, bf16[512,512]{1,0:T(8,128)(2,1)S(1)}, u32[]{:S(2)}) copy-start(bf16[512,512]{1,0:T(8,128)(2,1)S(1)} %collective-permute-done.1.refs_3_.refs_4_.refs_1_) | copy-start | bytes 1572868
  26.3 18.3 %copy-start.5 = (bf16[512,512]{1,0:T(8,128)(2,1)}, bf16[512,512]{1,0:T(8,128)(2,1)S(1)}, u32[]{:S(2)}) copy-start(bf16[512,512]{1,0:T(8,128)(2,1)S(1)} %collective-permute-done.2.refs_5_.refs_6_.refs_2_) | copy-start | bytes 1572868
  26.3 20.0 %collective-permute-start.3 = (bf16[512,512]{1,0:T(8,128)(2,1)S(1)}, bf16[512,512]{1,0:T(8,128)(2,1)S(1)}, u32[]{:S(2)}, u32[]{:S(2)}) collective-permute-start(bf16[512,512]{1,0:T(8,128)(2,1)S(1)} %collective-permute-done.refs_9_.refs_10_.refs_4_), channel_id=1, source_target_pairs={{0,2},{1,3},{2,4},{3,5},{4,6},{5,7},{6,0},{7,1},{8,10},{9,11},{10,... | collective-permute-start | bytes 1572872 | tf_op jit(solution)/shard_map/ppermute | solution.py:580
  27.0 19.4 %collective-permute-start.4 = (bf16[512,512]{1,0:T(8,128)(2,1)S(1)}, bf16[512,512]{1,0:T(8,128)(2,1)S(1)}, u32[]{:S(2)}, u32[]{:S(2)}) collective-permute-start(bf16[512,512]{1,0:T(8,128)(2,1)S(1)} %collective-permute-done.refs_9_.refs_10_.refs_4_), channel_id=1, source_target_pairs={{0,6},{1,7},{2,0},{3,1},{4,2},{5,3},{6,4},{7,5},{8,14},{9,15},{10,... | collective-permute-start | bytes 1572872 | tf_op jit(solution)/shard_map/ppermute | solution.py:580
  28.4 16.3 %collective-permute-start.5 = (bf16[256,512]{1,0:T(8,128)(2,1)S(1)}, bf16[256,512]{1,0:T(8,128)(2,1)S(1)}, u32[]{:S(2)}, u32[]{:S(2)}) collective-permute-start(bf16[256,512]{1,0:T(8,128)(2,1)S(1)} %slice.33), channel_id=1, source_target_pairs={{0,2},{1,3},{2,4},{3,5},{4,6},{5,7},{6,0},{7,1},{8,10},{9,11},{10,... | collective-permute-start | bytes 786440 | tf_op jit(solution)/shard_map/ppermute | solution.py:585
  30.3 16.0 %collective-permute-start.6 = (bf16[256,512]{1,0:T(8,128)(2,1)S(1)}, bf16[256,512]{1,0:T(8,128)(2,1)S(1)}, u32[]{:S(2)}, u32[]{:S(2)}) collective-permute-start(bf16[256,512]{1,0:T(8,128)(2,1)S(1)} %slice.34), channel_id=1, source_target_pairs={{0,6},{1,7},{2,0},{3,1},{4,2},{5,3},{6,4},{7,5},{8,14},{9,15},{10,... | collective-permute-start | bytes 786440 | tf_op jit(solution)/shard_map/ppermute | solution.py:586
  46.4 0.8 copy-start.6
  46.4 1.0 copy-start.7
  47.3 0.8 copy-start.8
  54.1 17.6 %collective-permute-start.10 = (bf16[14336,128]{1,0:T(8,128)(2,1)}, bf16[14336,128]{1,0:T(8,128)(2,1)}, u32[]{:S(2)}, u32[]{:S(2)}) collective-permute-start(bf16[14336,128]{1,0:T(8,128)(2,1)} %terms.2), channel_id=1, source_target_pairs={{0,8},{8,0},{16,24},{24,16},{32,40},{40,32},{48,56},{56,48},{64,72... | collective-permute-start | bytes 11010056 | tf_op jit(solution)/shard_map/ppermute | solution.py:655
  56.1 9.0 %collective-permute-start.7 = (bf16[256,512]{1,0:T(8,128)(2,1)S(1)}, bf16[256,512]{1,0:T(8,128)(2,1)S(1)}, u32[]{:S(2)}, u32[]{:S(2)}) collective-permute-start(bf16[256,512]{1,0:T(8,128)(2,1)S(1)} %slice.37), channel_id=1, source_target_pairs={{0,2},{1,3},{2,4},{3,5},{4,6},{5,7},{6,0},{7,1},{8,10},{9,11},{10,... | collective-permute-start | bytes 786440 | tf_op jit(solution)/shard_map/ppermute | solution.py:585
  57.8 9.6 %collective-permute-start.8 = (bf16[256,512]{1,0:T(8,128)(2,1)S(1)}, bf16[256,512]{1,0:T(8,128)(2,1)S(1)}, u32[]{:S(2)}, u32[]{:S(2)}) collective-permute-start(bf16[256,512]{1,0:T(8,128)(2,1)S(1)} %slice.38), channel_id=1, source_target_pairs={{0,6},{1,7},{2,0},{3,1},{4,2},{5,3},{6,4},{7,5},{8,14},{9,15},{10,... | collective-permute-start | bytes 786440 | tf_op jit(solution)/shard_map/ppermute | solution.py:586
  67.5 0.8 copy-start
  71.6 7.2 %collective-permute-start.9 = (bf16[2048,128]{1,0:T(8,128)(2,1)}, bf16[2048,128]{1,0:T(8,128)(2,1)S(1)}, u32[]{:S(2)}, u32[]{:S(2)}) collective-permute-start(bf16[2048,128]{1,0:T(8,128)(2,1)} %terms.3), channel_id=1, source_target_pairs={{0,8},{8,0},{16,24},{24,16},{32,40},{40,32},{48,56},{56,48},{64,72... | collective-permute-start | bytes 1572872 | tf_op jit(solution)/shard_map/ppermute | solution.py:658
  78.9 0.8 copy-start.1
  83.2 106.8 %all-gather.2.cloned.1.call-start = ((), (), s32[]{:S(2)}) async-start(), calls=%async_computation.1 | async-start | bytes 8650752 | tf_op jit(solution)/shard_map/all_gather | solution.py:626
  155.5 77.9 %collective-permute-start.11 = (bf16[1024,128]{1,0:T(8,128)(2,1)S(1)}, bf16[1024,128]{1,0:T(8,128)(2,1)S(1)}, u32[]{:S(2)}, u32[]{:S(2)}) collective-permute-start(bf16[1024,128]{1,0:T(8,128)(2,1)S(1)} %slice.44), channel_id=1, source_target_pairs={{0,16},{8,24},{16,0},{24,8},{32,48},{40,56},{48,32},{56,40},{64,80... | collective-permute-start | bytes 786440 | tf_op jit(solution)/shard_map/ppermute | solution.py:664
  201.4 18.1 %copy-start.9 = (f32[1,1024]{1,0:T(1,128)S(1)}, f32[1,1024]{1,0:T(1,128)}, u32[]{:S(2)}) copy-start(f32[1,1024]{1,0:T(1,128)} %get-tuple-element.60) | copy-start | bytes 12292
  219.5 22.9 %copy-start.3 = (f32[512,16]{1,0:T(8,128)S(1)}, f32[512,16]{1,0:T(8,128)}, u32[]{:S(2)}) copy-start(f32[512,16]{1,0:T(8,128)} %get-tuple-element.64) | copy-start | bytes 98308
  220.3 1.2 collective-permute-start.12
  222.2 3.7 %collective-permute-start.13 = (f32[16,128]{1,0:T(8,128)S(1)}, f32[16,128]{1,0:T(8,128)S(1)}, u32[]{:S(2)}, u32[]{:S(2)}) collective-permute-start(f32[16,128]{1,0:T(8,128)S(1)} %fusion), channel_id=1, source_target_pairs={{0,16},{8,24},{16,0},{24,8},{32,48},{40,56},{48,32},{56,40},{64,80... | collective-permute-start | bytes 24584 | tf_op jit(solution)/shard_map/ppermute | solution.py:681
  225.8 3.9 %collective-permute-start.14 = (f32[16,128]{1,0:T(8,128)S(1)}, f32[16,128]{1,0:T(8,128)S(1)}, u32[]{:S(2)}, u32[]{:S(2)}) collective-permute-start(f32[16,128]{1,0:T(8,128)S(1)} %add.122), channel_id=1, source_target_pairs={{0,32},{8,40},{16,48},{24,56},{32,0},{40,8},{48,16},{56,24},{64,96... | collective-permute-start | bytes 24584 | tf_op jit(solution)/shard_map/ppermute | solution.py:681
  229.7 6.4 %collective-permute-start.15 = (f32[16,128]{1,0:T(8,128)S(1)}, f32[16,128]{1,0:T(8,128)S(1)}, u32[]{:S(2)}, u32[]{:S(2)}) collective-permute-start(f32[16,128]{1,0:T(8,128)S(1)} %add.123), channel_id=1, source_target_pairs={{0,64},{8,72},{16,80},{24,88},{32,96},{40,104},{48,112},{56,120},{... | collective-permute-start | bytes 24584 | tf_op jit(solution)/shard_map/ppermute | solution.py:681
  233.4 0.7 copy-start.2
  236.1 7.6 %collective-permute-start.16 = (f32[16,128]{1,0:T(8,128)S(1)}, f32[16,128]{1,0:T(8,128)S(1)}, u32[]{:S(2)}, u32[]{:S(2)}) collective-permute-start(f32[16,128]{1,0:T(8,128)S(1)} %add.124), channel_id=1, source_target_pairs={{0,128},{8,136},{16,144},{24,152},{32,160},{40,168},{48,176},{56,1... | collective-permute-start | bytes 24584 | tf_op jit(solution)/shard_map/ppermute | solution.py:681
Sparse Core Ops, SparseCore 0:
  83.3 71.2 reduce-scatter.1
Sparse Core Ops, SparseCore 1:
  85.5 104.4 all-gather.1

commit v2 on v1

--- a/solution.py
+++ b/solution.py
@@ -419,8 +419,12 @@
 
 def term_kernel(count, added, placed, places, *refs):
     pieces, low_ref = refs[: 2 * count], refs[2 * count]
-    sent_ref = refs[2 * count + 1] if added else None
+    sent_refs = refs[2 * count + 1 : -3]
     out_ref, held, done = refs[-3:]
+    per = 2 * CHANNELS
+    sent = [
+        ref.at[start : start + per] for ref in sent_refs for start in range(0, ref.shape[0], per)
+    ]
     copies = []
     for k in range(count):
         blocks = [piece[...] for piece in pieces[2 * k : 2 * k + 2]]
@@ -430,7 +434,7 @@
             here = slice(n * CHANNELS, (n + 1) * CHANNELS)
             part = term[:, slot * BLOCK : (slot + 1) * BLOCK]
             if added:
-                part = part + sent_ref[here, :].astype(F32)
+                part = part + sent[k][slot * CHANNELS : (slot + 1) * CHANNELS, :].astype(F32)
             held[here, :] = part.astype(BF16)
             start = n * CHANNELS
             if placed:
@@ -445,18 +449,11 @@
         copy.wait()
 
 
-def terms(places, blocks, pieces, low, sent=None, base=None):
+def terms(places, blocks, pieces, low, sent=()):
     count = len(pieces)
-    added = sent is not None
-    rows = 2 * CHANNELS * (SHARDS if added else count)
-    more, specs, aliases = [], [], {}
-    if added:
-        more.append(sent)
-        specs.append(whole((2 * CHANNELS * count, BLOCK)))
-    if base is not None:
-        aliases = {2 + 2 * count + len(more): 0}
-        more.append(base)
-        specs.append(pl.BlockSpec(memory_space=pl.ANY))
+    added = len(sent) > 0
+    rows = 2 * CHANNELS * count
+    specs = [whole(part.shape) for part in sent]
 
     def kernel(*refs):
         term_kernel(count, added, added, *refs)
@@ -477,7 +474,6 @@
             ],
         ),
         out_shape=jax.ShapeDtypeStruct((rows, BLOCK), BF16),
-        input_output_aliases=aliases,
         compiler_params=pltpu.CompilerParams(vmem_limit_bytes=VMEM_LIMIT),
         cost_estimate=pl.CostEstimate(
             flops=(count + 1) * 7 * 10**8, bytes_accessed=2 * 10**6, transcendentals=0
@@ -487,7 +483,7 @@
         jnp.stack(list(places) + list(blocks)).astype(jnp.int32),
         *[piece for piece in pieces for _ in range(2)],
         low,
-        *more,
+        *sent,
     )
 
 
@@ -652,18 +648,14 @@
     theirs, theirs_y = 2 * y_lo + 1 - core, 2 * (1 - y_lo) + 1 - core
 
     theirs_early = terms(places[:-1], (theirs_y, theirs), early, low)
+    theirs_early, partner_far = lax.optimization_barrier((theirs_early, partner_far))
     sent_early = lax.ppermute(theirs_early, "blk", swap(1))
-    partner_far, _ = lax.optimization_barrier((partner_far, theirs_early))
     last = [jnp.concatenate(partner_far, axis=0)]
     sent_last = lax.ppermute(terms(places[-1:], (theirs_y, theirs), last, low), "blk", swap(1))
-    both = terms(places[:-1], (mine_y, mine), early, low, sent_early)
-    both = terms(places[-1:], (mine_y, mine), last, low, sent_last, base=both)
+    both = terms(places, (mine_y, mine), early + last, low, (sent_early, sent_last))
     plane = lax.psum_scatter(
         both, "blk", scatter_dimension=0, tiled=True, axis_index_groups=by_z
     )
-    given = lax.ppermute(plane[:CHANNELS], "blk", swap(2))
-    weight_grad = finish(plane, given, norm_scale)
-
     rows, _ = lax.optimization_barrier((rows, both))
     cot, gain_grad, pull = products(
         jnp.stack(places).astype(jnp.int32),
@@ -679,6 +671,9 @@
     summed = jnp.concatenate([small, gain_grad.reshape(8, LANES)], axis=0)
     for bit in (1, 2, 4, 8, 16):
         summed = summed + lax.ppermute(summed, "blk", swap(bit))
+    plane, summed = lax.optimization_barrier((plane, summed))
+    given = lax.ppermute(plane[:CHANNELS], "blk", swap(2))
+    weight_grad = finish(plane, given, norm_scale)
     summed = summed * norm_scale
     return (
         dx,

time: 253 us -> 157 us (0.62)
  waiting for transfers between devices: 118 us -> 30.4 us
  Pallas kernels: 65.5 us -> 62.8 us
  local copies, waits for them, and re-layouts: 24.5 us -> 21.9 us
    reduce_scatter x1, waiting for transfers between devices: 68.9 us -> 0.02 us  [shards(): lax.psum_scatter(both, 'blk', scatter_dimension=0, tiled=True, axis_index...]
    all_gather x1, waiting for transfers between devices: 32.9 us -> 11.1 us  [shards(): rows = lax.all_gather(out_proj, 'blk', axis=0, tiled=True)]
    ppermute x2, waiting for transfers between devices: 4.88 us -> 0.01 us  [beyond(): top = lax.ppermute(before[:half], 'tp', along_x(1))]
    ppermute x1, waiting for transfers between devices: 0.01 us -> 4.04 us  [shards(): given = lax.ppermute(plane[:CHANNELS], 'blk', swap(2))]
    ppermute x5, waiting for transfers between devices: 6.02 us -> 9.07 us  [shards(): summed = summed + lax.ppermute(summed, 'blk', swap(bit))]
    pallas_call x4 -> x3, Pallas kernels: 19.8 us -> 17.1 us  [terms(): pl.pallas_call(kernel, grid_spec=pltpu.PrefetchScalarGridSpec(num_scalar_...]
    ppermute x2, waiting for transfers between devices: 4 us -> 1.46 us  [beyond(): low = lax.ppermute(after[half:], 'tp', along_x(-1))]
  transfers between devices with their start and end apart: 19 -> 19, of which waited for: 10 -> 11; matrix products, arithmetic and copies ran while one was open for 9% -> 13% of each run, Pallas kernels for 22% -> 39%
where the time goes in v2:
time: 157 us; the launch traced here: 156 us
  Pallas kernels  62.8 us (40%)
  waiting for transfers between devices  30.4 us (19%)
  starting transfers between devices  22.4 us (14%)
  local copies, waits for them, and re-layouts  21.9 us (14%)
  between operations  15.7 us (10%)
  other arithmetic  3.04 us (2%)
    pallas_call x1, Pallas kernels, scan_backward(): pl.pallas_call(backward_kernel, grid=(PAIRS,), in_specs=[by_pair(TOKENS),...  18.1 us
    pallas_call x3, Pallas kernels, terms(): pl.pallas_call(kernel, grid_spec=pltpu.PrefetchScalarGridSpec(num_scalar_...  17.1 us
    pallas_call x1, Pallas kernels, scan_forward(): pl.pallas_call(forward_kernel, grid=(PAIRS,), in_specs=[by_pair(TOKENS),...  14.1 us
    pallas_call x1, Pallas kernels, products(): pl.pallas_call(product_kernel, grid_spec=pltpu.PrefetchScalarGridSpec(num...  11.4 us
    all_gather x1, waiting for transfers between devices, shards(): rows = lax.all_gather(out_proj, 'blk', axis=0, tiled=True)  11.1 us
    ppermute x5, waiting for transfers between devices, shards(): summed = summed + lax.ppermute(summed, 'blk', swap(bit))  9.07 us
    ppermute x5, starting transfers between devices, shards(): summed = summed + lax.ppermute(summed, 'blk', swap(bit))  8.48 us
    unnamed x28, local copies, waits for them, and re-layouts  8.32 us
  transfers between devices with their start and end apart: 19, of which 11 were waited for; matrix products, arithmetic and copies ran while one was open for 13% of the time, Pallas kernels for 39%

profile of v2, /device:TPU:6, one launch (start us, length us, event | category | flops | bytes accessed | tf_op | source)
XLA Modules:
  0.0 156.3 jit_solution(11219686529534545064)
XLA Ops:
  8.1 0.7 all-gather.2.cloned.1.call-update
  8.8 3.3 %collective-permute-start = (bf16[512,512]{1,0:T(8,128)(2,1)}, bf16[512,512]{1,0:T(8,128)(2,1)}, u32[]{:S(2)}, u32[]{:S(2)}) collective-permute-start(bf16[512,512]{1,0:T(8,128)(2,1)} %refs_0_.1), channel_id=1, source_target_pairs={{0,1},{1,0},{2,3},{3,2},{4,5},{5,4},{6,7},{7,6},{8,9},{9,8},{10,11... | collective-permute-start | bytes 1572872 | tf_op jit(solution)/shard_map/ppermute | solution.py:624
  12.6 1.5 collective-permute-start.2
  14.1 2.1 %fusion.1 = (bf16[512,1,256]{2,1,0:T(2,128)(2,1)S(1)}, bf16[512,1,256]{2,1,0:T(2,128)(2,1)S(1)}) fusion(bf16[512,2,256]{2,1,0:T(2,128)(2,1)} %param.12), kind=kLoop, calls=%fused_computation.17 | loop fusion | bytes 1048576 | tf_op jit(solution)/shard_map/slice | solution.py:633
  16.2 1.3 copy.33
  17.5 0.8 copy.21
  18.4 0.7 broadcast_in_dim.3
  19.1 0.7 reshape_reshape.3.skip_ref
  19.8 1.3 copy.24.bias_t_ref
  21.1 1.3 copy.25.rate_t_ref
  22.4 0.7 pad.11.raw_ref
  24.3 0.9 copy_bitcast_fusion
  25.7 1.4 collective-permute-done.2.refs_5_.refs_6_.refs_2_
  27.5 1.7 %collective-permute-start.4 = (bf16[512,512]{1,0:T(8,128)(2,1)}, bf16[512,512]{1,0:T(8,128)(2,1)S(1)}, u32[]{:S(2)}, u32[]{:S(2)}) collective-permute-start(bf16[512,512]{1,0:T(8,128)(2,1)} %collective-permute-done.refs_9_.refs_10_.refs_4_), channel_id=1, source_target_pairs={{0,6},{1,7},{2,0},{3,1},{4,2},{5,3},{6,4},{7,5},{8,14},{9,15},{10,... | collective-permute-start | bytes 1572872 | tf_op jit(solution)/shard_map/ppermute | solution.py:576
  29.2 1.6 %collective-permute-start.5 = (bf16[256,512]{1,0:T(8,128)(2,1)S(1)}, bf16[256,512]{1,0:T(8,128)(2,1)S(1)}, u32[]{:S(2)}, u32[]{:S(2)}) collective-permute-start(bf16[256,512]{1,0:T(8,128)(2,1)S(1)} %slice.33), channel_id=1, source_target_pairs={{0,2},{1,3},{2,4},{3,5},{4,6},{5,7},{6,0},{7,1},{8,10},{9,11},{10,... | collective-permute-start | bytes 786440 | tf_op jit(solution)/shard_map/ppermute | solution.py:581
  31.4 14.1 %scan_forward.1 = (bf16[1024,512]{1,0:T(8,128)(2,1)}, f32[512,1024]{1,0:T(8,128)}, f32[512,1024]{1,0:T(8,128)}, f32[8,3,256,128]{3,2,1,0:T(8,128)}, f32[512,128]{1,0:T(8,128)}) custom-call(bf16[512,1024]{1,0:T(8,128)(2,1)} %x_ref.1, bf16[512,1024]{1,0:T(8,128)(2,1)} %g_ref.3, bf16[512,256]{1,0:T(8,128)(2,1)} %get-tuple-element.82.b_ref, ...), custom_call_target="tpu_custom_call" | custom-call | flops 16000000000 | bytes 10000000 | tf_op jit(solution)/shard_map/scan_forward/pallas_call | solution.py:335
  45.5 1.2 collective-permute-done.6
  46.7 1.7 %collective-permute-start.7 = (bf16[256,512]{1,0:T(8,128)(2,1)S(1)}, bf16[256,512]{1,0:T(8,128)(2,1)S(1)}, u32[]{:S(2)}, u32[]{:S(2)}) collective-permute-start(bf16[256,512]{1,0:T(8,128)(2,1)S(1)} %slice.37), channel_id=1, source_target_pairs={{0,2},{1,3},{2,4},{3,5},{4,6},{5,7},{6,0},{7,1},{8,10},{9,11},{10,... | collective-permute-start | bytes 786440 | tf_op jit(solution)/shard_map/ppermute | solution.py:581
  48.4 0.7 collective-permute-start.8
  49.2 0.8 copy-done.5
  50.0 6.0 %terms.2 = bf16[14336,128]{1,0:T(8,128)(2,1)} custom-call(s32[9]{0:T(128)} %stack.86.refs_0_, bf16[512,512]{1,0:T(8,128)(2,1)} %refs_0_.1, bf16[512,512]{1,0:T(8,128)(2,1)} %refs_0_.1, bf16[512,512]{1,0:T(8,128)(2,1)} %copy-done.1, bf16[512,512]{1,0:T(8,128)(2,1)} %copy-done.1, bf16[512,512]{1,0:T(8,128)(2,1)} %copy-done.2, bf16[512,512]{1,0:T(8,128)(2,1)} %copy-done.2, ...), custom_call_target="tpu_custom_call" | custom-call | flops 5600000000 | bytes 2000000 | tf_op jit(solution)/shard_map/terms/pallas_call | solution.py:464
  56.9 0.8 copy-done.6
  57.8 3.3 %terms.3 = bf16[2048,128]{1,0:T(8,128)(2,1)} custom-call(s32[3]{0:T(128)} %pad_add_fusion.refs_0_, bf16[512,512]{1,0:T(8,128)(2,1)} %copy-done.6, bf16[512,512]{1,0:T(8,128)(2,1)} %copy-done.6, bf16[1024,512]{1,0:T(8,128)(2,1)} %get-tuple-element.47.refs_15_.refs_3_.refs_17_), custom_call_target="tpu_custom_call" | custom-call | flops 1400000000 | bytes 2000000 | tf_op jit(solution)/shard_map/terms/pallas_call | solution.py:464
  62.3 2.1 %collective-permute-done.10.refs_19_ = bf16[2048,128]{1,0:T(8,128)(2,1)S(1)} collective-permute-done((bf16[2048,128]{1,0:T(8,128)(2,1)}, bf16[2048,128]{1,0:T(8,128)(2,1)S(1)}, u32[]{:S(2)}, u32[]{:S(2)}) %collective-permute-start.10) | collective-permute-done | bytes 524320 | tf_op jit(solution)/shard_map/ppermute | solution.py:654
  64.4 0.8 copy-done.10
  65.2 7.7 %terms_added.1 = bf16[16384,128]{1,0:T(8,128)(2,1)} custom-call(s32[10]{0:T(128)} %stack.89.refs_0_, bf16[512,512]{1,0:T(8,128)(2,1)} %refs_0_.1, bf16[512,512]{1,0:T(8,128)(2,1)} %refs_0_.1, bf16[512,512]{1,0:T(8,128)(2,1)} %copy-done.1, bf16[512,512]{1,0:T(8,128)(2,1)} %copy-done.1, bf16[512,512]{1,0:T(8,128)(2,1)} %copy-done.2, ...), custom_call_target="tpu_custom_call" | custom-call | flops 6300000256 | bytes 2000000 | tf_op jit(solution)/shard_map/terms_added/pallas_call | solution.py:464
  73.6 1.3 copy.32
  74.9 11.1 %all-gather.2.cloned.1.call-done.refs_8_ = bf16[4096,1024]{1,0:T(8,128)(2,1)} async-done(((bf16[128,1024]{1,0:T(8,128)(2,1)}), bf16[4096,1024]{1,0:T(8,128)(2,1)}) %all-gather.2.cloned.1.call-update) | async-done | bytes 8388624 | tf_op jit(solution)/shard_map/all_gather | solution.py:622
  86.0 11.4 %products.1 = (f32[512,1024]{1,0:T(8,128)}, f32[1,1024]{1,0:T(1,128)}, f32[512,128]{1,0:T(8,128)}) custom-call(s32[8]{0:T(128)} %stack.83.places, bf16[512,512]{1,0:T(8,128)(2,1)} %refs_0_.1, bf16[512,512]{1,0:T(8,128)(2,1)} %copy-done.1, bf16[512,512]{1,0:T(8,128)(2,1)} %copy-done.2, bf16[512,512]{1,0:T(8,128)(2,1)} %copy-done.5, ...), custom_call_target="tpu_custom_call" | custom-call | flops 12000000000 | bytes 16000000 | tf_op jit(solution)/shard_map/products/pallas_call | solution.py:539
  97.4 18.1 %scan_backward.1 = (bf16[512,1024]{1,0:T(8,128)(2,1)}, bf16[512,1024]{1,0:T(8,128)(2,1)}, bf16[512,256]{1,0:T(8,128)(2,1)}, bf16[512,256]{1,0:T(8,128)(2,1)}, f32[512,16]{1,0:T(8,128)}, /*index=5*/f32[8,128]{1,0:T(8,128)}) custom-call(bf16[512,1024]{1,0:T(8,128)(2,1)} %x_ref.1, bf16[512,1024]{1,0:T(8,128)(2,1)} %g_ref.3, ...), custom_call_target="tpu_custom_call" | custom-call | flops 20000000000 | bytes 10000000 | tf_op jit(solution)/shard_map/scan_backward/pallas_call | solution.py:368
  115.6 0.7 pad_maximum_fusion.1
  116.5 0.9 collective-permute-done.11
  117.5 0.7 fusion
  118.1 1.6 %collective-permute-start.12 = (f32[16,128]{1,0:T(8,128)S(1)}, f32[16,128]{1,0:T(8,128)S(1)}, u32[]{:S(2)}, u32[]{:S(2)}) collective-permute-start(f32[16,128]{1,0:T(8,128)S(1)} %fusion), channel_id=1, source_target_pairs={{0,16},{8,24},{16,0},{24,8},{32,48},{40,56},{48,32},{56,40},{64,80... | collective-permute-start | bytes 24584 | tf_op jit(solution)/shard_map/ppermute | solution.py:673
  119.7 2.1 %collective-permute-done.12 = f32[16,128]{1,0:T(8,128)S(1)} collective-permute-done((f32[16,128]{1,0:T(8,128)S(1)}, f32[16,128]{1,0:T(8,128)S(1)}, u32[]{:S(2)}, u32[]{:S(2)}) %collective-permute-start.12) | collective-permute-done | bytes 8224 | tf_op jit(solution)/shard_map/ppermute | solution.py:673
  121.8 0.7 collective-permute-start.13
  122.5 3.3 %collective-permute-done.13 = f32[16,128]{1,0:T(8,128)S(1)} collective-permute-done((f32[16,128]{1,0:T(8,128)S(1)}, f32[16,128]{1,0:T(8,128)S(1)}, u32[]{:S(2)}, u32[]{:S(2)}) %collective-permute-start.13) | collective-permute-done | bytes 8224 | tf_op jit(solution)/shard_map/ppermute | solution.py:673
  125.8 1.7 %collective-permute-start.14 = (f32[16,128]{1,0:T(8,128)S(1)}, f32[16,128]{1,0:T(8,128)S(1)}, u32[]{:S(2)}, u32[]{:S(2)}) collective-permute-start(f32[16,128]{1,0:T(8,128)S(1)} %add.123), channel_id=1, source_target_pairs={{0,64},{8,72},{16,80},{24,88},{32,96},{40,104},{48,112},{56,120},{... | collective-permute-start | bytes 24584 | tf_op jit(solution)/shard_map/ppermute | solution.py:673
  127.5 2.8 %collective-permute-done.14 = f32[16,128]{1,0:T(8,128)S(1)} collective-permute-done((f32[16,128]{1,0:T(8,128)S(1)}, f32[16,128]{1,0:T(8,128)S(1)}, u32[]{:S(2)}, u32[]{:S(2)}) %collective-permute-start.14) | collective-permute-done | bytes 8224 | tf_op jit(solution)/shard_map/ppermute | solution.py:673
  130.3 4.2 %collective-permute-start.15 = (f32[16,128]{1,0:T(8,128)S(1)}, f32[16,128]{1,0:T(8,128)S(1)}, u32[]{:S(2)}, u32[]{:S(2)}) collective-permute-start(f32[16,128]{1,0:T(8,128)S(1)} %add.124), channel_id=1, source_target_pairs={{0,128},{8,136},{16,144},{24,152},{32,160},{40,168},{48,176},{56,1... | collective-permute-start | bytes 24584 | tf_op jit(solution)/shard_map/ppermute | solution.py:673
  134.5 1.1 pad_maximum_fusion
  135.6 1.3 copy.29
  136.9 1.7 %copy.30 = f32[512,16]{0,1:T(8,128)} copy(f32[512,16]{1,0:T(8,128)} %get-tuple-element.70) | data formatting | bytes 65536
  138.6 1.0 slice.39
  139.6 1.3 collective-permute-start.16
  142.0 4.0 %collective-permute-done.16.refs_1_ = bf16[1024,128]{1,0:T(8,128)(2,1)S(1)} collective-permute-done((bf16[1024,128]{1,0:T(8,128)(2,1)S(1)}, bf16[1024,128]{1,0:T(8,128)(2,1)S(1)}, u32[]{:S(2)}, u32[]{:S(2)}) %collective-permute-start.16) | collective-permute-done | bytes 262176 | tf_op jit(solution)/shard_map/ppermute | solution.py:675
  146.1 0.7 copy-done
  146.8 2.0 %finish.1 = f32[128,1024]{1,0:T(8,128)} custom-call(bf16[2048,128]{1,0:T(8,128)(2,1)} %reduce-scatter.2.cloned.1.call-done.refs_0_, bf16[1024,128]{1,0:T(8,128)(2,1)} %copy-done), custom_call_target="tpu_custom_call" | custom-call | tf_op jit(solution)/shard_map/finish/pallas_call | solution.py:496
  (57 shorter events, 7.4 us)
Async XLA Ops:
  8.0 15.7 %copy-start.9 = (f32[16]{0:T(128)S(1)}, f32[16]{0:T(128)}, u32[]{:S(2)}) copy-start(f32[16]{0:T(128)} %param.15) | copy-start | bytes 196
  8.0 15.7 %copy-start.8 = (f32[16]{0:T(128)S(1)}, f32[16]{0:T(128)}, u32[]{:S(2)}) copy-start(f32[16]{0:T(128)} %param.14) | copy-start | bytes 196
  8.0 78.0 %all-gather.2.cloned.1.call-start = ((), (), s32[]{:S(2)}) async-start(), calls=%async_computation.1 | async-start | bytes 8650752 | tf_op jit(solution)/shard_map/all_gather | solution.py:622
  8.8 129.9 %reduce-scatter.2.cloned.1.call-start = ((), (), s32[]{:S(2)}) async-start(), calls=%async_computation.2 | async-start | bytes 4718592 | tf_op jit(solution)/shard_map/reduce_scatter | solution.py:656
  8.8 16.3 %collective-permute-start = (bf16[512,512]{1,0:T(8,128)(2,1)}, bf16[512,512]{1,0:T(8,128)(2,1)}, u32[]{:S(2)}, u32[]{:S(2)}) collective-permute-start(bf16[512,512]{1,0:T(8,128)(2,1)} %refs_0_.1), channel_id=1, source_target_pairs={{0,1},{1,0},{2,3},{3,2},{4,5},{5,4},{6,7},{7,6},{8,9},{9,8},{10,11... | collective-permute-start | bytes 1572872 | tf_op jit(solution)/shard_map/ppermute | solution.py:624
  12.1 13.6 %collective-permute-start.1 = (bf16[512,512]{1,0:T(8,128)(2,1)}, bf16[512,512]{1,0:T(8,128)(2,1)S(1)}, u32[]{:S(2)}, u32[]{:S(2)}) collective-permute-start(bf16[512,512]{1,0:T(8,128)(2,1)} %refs_0_.1), channel_id=1, source_target_pairs={{0,2},{1,3},{2,4},{3,5},{4,6},{5,7},{6,0},{7,1},{8,10},{9,11},{10,... | collective-permute-start | bytes 1572872 | tf_op jit(solution)/shard_map/ppermute | solution.py:576
  12.6 14.5 %collective-permute-start.2 = (bf16[512,512]{1,0:T(8,128)(2,1)}, bf16[512,512]{1,0:T(8,128)(2,1)S(1)}, u32[]{:S(2)}, u32[]{:S(2)}) collective-permute-start(bf16[512,512]{1,0:T(8,128)(2,1)} %refs_0_.1), channel_id=1, source_target_pairs={{0,6},{1,7},{2,0},{3,1},{4,2},{5,3},{6,4},{7,5},{8,14},{9,15},{10,... | collective-permute-start | bytes 1572872 | tf_op jit(solution)/shard_map/ppermute | solution.py:576
  25.7 19.7 %copy-start.1 = (bf16[512,512]{1,0:T(8,128)(2,1)}, bf16[512,512]{1,0:T(8,128)(2,1)S(1)}, u32[]{:S(2)}) copy-start(bf16[512,512]{1,0:T(8,128)(2,1)S(1)} %collective-permute-done.1.refs_3_.refs_4_.refs_1_) | copy-start | bytes 1572868
  27.1 18.3 %copy-start.2 = (bf16[512,512]{1,0:T(8,128)(2,1)}, bf16[512,512]{1,0:T(8,128)(2,1)S(1)}, u32[]{:S(2)}) copy-start(bf16[512,512]{1,0:T(8,128)(2,1)S(1)} %collective-permute-done.2.refs_5_.refs_6_.refs_2_) | copy-start | bytes 1572868
  27.1 19.6 %collective-permute-start.3 = (bf16[512,512]{1,0:T(8,128)(2,1)}, bf16[512,512]{1,0:T(8,128)(2,1)S(1)}, u32[]{:S(2)}, u32[]{:S(2)}) collective-permute-start(bf16[512,512]{1,0:T(8,128)(2,1)} %collective-permute-done.refs_9_.refs_10_.refs_4_), channel_id=1, source_target_pairs={{0,2},{1,3},{2,4},{3,5},{4,6},{5,7},{6,0},{7,1},{8,10},{9,11},{10,... | collective-permute-start | bytes 1572872 | tf_op jit(solution)/shard_map/ppermute | solution.py:576
  27.5 19.2 %collective-permute-start.4 = (bf16[512,512]{1,0:T(8,128)(2,1)}, bf16[512,512]{1,0:T(8,128)(2,1)S(1)}, u32[]{:S(2)}, u32[]{:S(2)}) collective-permute-start(bf16[512,512]{1,0:T(8,128)(2,1)} %collective-permute-done.refs_9_.refs_10_.refs_4_), channel_id=1, source_target_pairs={{0,6},{1,7},{2,0},{3,1},{4,2},{5,3},{6,4},{7,5},{8,14},{9,15},{10,... | collective-permute-start | bytes 1572872 | tf_op jit(solution)/shard_map/ppermute | solution.py:576
  29.2 16.3 %collective-permute-start.5 = (bf16[256,512]{1,0:T(8,128)(2,1)S(1)}, bf16[256,512]{1,0:T(8,128)(2,1)S(1)}, u32[]{:S(2)}, u32[]{:S(2)}) collective-permute-start(bf16[256,512]{1,0:T(8,128)(2,1)S(1)} %slice.33), channel_id=1, source_target_pairs={{0,2},{1,3},{2,4},{3,5},{4,6},{5,7},{6,0},{7,1},{8,10},{9,11},{10,... | collective-permute-start | bytes 786440 | tf_op jit(solution)/shard_map/ppermute | solution.py:581
  30.8 15.9 %collective-permute-start.6 = (bf16[256,512]{1,0:T(8,128)(2,1)S(1)}, bf16[256,512]{1,0:T(8,128)(2,1)S(1)}, u32[]{:S(2)}, u32[]{:S(2)}) collective-permute-start(bf16[256,512]{1,0:T(8,128)(2,1)S(1)} %slice.34), channel_id=1, source_target_pairs={{0,6},{1,7},{2,0},{3,1},{4,2},{5,3},{6,4},{7,5},{8,14},{9,15},{10,... | collective-permute-start | bytes 786440 | tf_op jit(solution)/shard_map/ppermute | solution.py:582
  46.7 2.5 %copy-start.3 = (bf16[512,512]{1,0:T(8,128)(2,1)}, bf16[512,512]{1,0:T(8,128)(2,1)S(1)}, u32[]{:S(2)}) copy-start(bf16[512,512]{1,0:T(8,128)(2,1)S(1)} %collective-permute-done.3.refs_11_.refs_12_.refs_5_) | copy-start | bytes 1572868
  46.7 2.5 %copy-start.4 = (bf16[512,512]{1,0:T(8,128)(2,1)}, bf16[512,512]{1,0:T(8,128)(2,1)S(1)}, u32[]{:S(2)}) copy-start(bf16[512,512]{1,0:T(8,128)(2,1)S(1)} %collective-permute-done.4.refs_13_.refs_14_.refs_6_) | copy-start | bytes 1572868
  46.7 9.3 %collective-permute-start.7 = (bf16[256,512]{1,0:T(8,128)(2,1)S(1)}, bf16[256,512]{1,0:T(8,128)(2,1)S(1)}, u32[]{:S(2)}, u32[]{:S(2)}) collective-permute-start(bf16[256,512]{1,0:T(8,128)(2,1)S(1)} %slice.37), channel_id=1, source_target_pairs={{0,2},{1,3},{2,4},{3,5},{4,6},{5,7},{6,0},{7,1},{8,10},{9,11},{10,... | collective-permute-start | bytes 786440 | tf_op jit(solution)/shard_map/ppermute | solution.py:581
  48.4 7.8 %collective-permute-start.8 = (bf16[256,512]{1,0:T(8,128)(2,1)S(1)}, bf16[256,512]{1,0:T(8,128)(2,1)S(1)}, u32[]{:S(2)}, u32[]{:S(2)}) collective-permute-start(bf16[256,512]{1,0:T(8,128)(2,1)S(1)} %slice.38), channel_id=1, source_target_pairs={{0,6},{1,7},{2,0},{3,1},{4,2},{5,3},{6,4},{7,5},{8,14},{9,15},{10,... | collective-permute-start | bytes 786440 | tf_op jit(solution)/shard_map/ppermute | solution.py:582
  49.2 0.8 copy-start.5
  56.3 8.1 %collective-permute-start.9 = (bf16[14336,128]{1,0:T(8,128)(2,1)}, bf16[14336,128]{1,0:T(8,128)(2,1)}, u32[]{:S(2)}, u32[]{:S(2)}) collective-permute-start(bf16[14336,128]{1,0:T(8,128)(2,1)} %terms.2), channel_id=1, source_target_pairs={{0,8},{8,0},{16,24},{24,16},{32,40},{40,32},{48,56},{56,48},{64,72... | collective-permute-start | bytes 11010056 | tf_op jit(solution)/shard_map/ppermute | solution.py:652
  56.9 0.8 copy-start.6
  61.1 3.3 %collective-permute-start.10 = (bf16[2048,128]{1,0:T(8,128)(2,1)}, bf16[2048,128]{1,0:T(8,128)(2,1)S(1)}, u32[]{:S(2)}, u32[]{:S(2)}) collective-permute-start(bf16[2048,128]{1,0:T(8,128)(2,1)} %terms.3), channel_id=1, source_target_pairs={{0,8},{8,0},{16,24},{24,16},{32,40},{40,32},{48,56},{56,48},{64,72... | collective-permute-start | bytes 1572872 | tf_op jit(solution)/shard_map/ppermute | solution.py:654
  64.4 0.8 copy-start.10
  97.4 18.2 %copy-start.7 = (f32[1,1024]{1,0:T(1,128)S(1)}, f32[1,1024]{1,0:T(1,128)}, u32[]{:S(2)}) copy-start(f32[1,1024]{1,0:T(1,128)} %get-tuple-element.64) | copy-start | bytes 12292
  116.3 1.2 collective-permute-start.11
  118.1 3.7 %collective-permute-start.12 = (f32[16,128]{1,0:T(8,128)S(1)}, f32[16,128]{1,0:T(8,128)S(1)}, u32[]{:S(2)}, u32[]{:S(2)}) collective-permute-start(f32[16,128]{1,0:T(8,128)S(1)} %fusion), channel_id=1, source_target_pairs={{0,16},{8,24},{16,0},{24,8},{32,48},{40,56},{48,32},{56,40},{64,80... | collective-permute-start | bytes 24584 | tf_op jit(solution)/shard_map/ppermute | solution.py:673
  121.8 4.0 %collective-permute-start.13 = (f32[16,128]{1,0:T(8,128)S(1)}, f32[16,128]{1,0:T(8,128)S(1)}, u32[]{:S(2)}, u32[]{:S(2)}) collective-permute-start(f32[16,128]{1,0:T(8,128)S(1)} %add.122), channel_id=1, source_target_pairs={{0,32},{8,40},{16,48},{24,56},{32,0},{40,8},{48,16},{56,24},{64,96... | collective-permute-start | bytes 24584 | tf_op jit(solution)/shard_map/ppermute | solution.py:673
  125.8 4.6 %collective-permute-start.14 = (f32[16,128]{1,0:T(8,128)S(1)}, f32[16,128]{1,0:T(8,128)S(1)}, u32[]{:S(2)}, u32[]{:S(2)}) collective-permute-start(f32[16,128]{1,0:T(8,128)S(1)} %add.123), channel_id=1, source_target_pairs={{0,64},{8,72},{16,80},{24,88},{32,96},{40,104},{48,112},{56,120},{... | collective-permute-start | bytes 24584 | tf_op jit(solution)/shard_map/ppermute | solution.py:673
  130.3 8.3 %collective-permute-start.15 = (f32[16,128]{1,0:T(8,128)S(1)}, f32[16,128]{1,0:T(8,128)S(1)}, u32[]{:S(2)}, u32[]{:S(2)}) collective-permute-start(f32[16,128]{1,0:T(8,128)S(1)} %add.124), channel_id=1, source_target_pairs={{0,128},{8,136},{16,144},{24,152},{32,160},{40,168},{48,176},{56,1... | collective-permute-start | bytes 24584 | tf_op jit(solution)/shard_map/ppermute | solution.py:673
  139.6 6.5 %collective-permute-start.16 = (bf16[1024,128]{1,0:T(8,128)(2,1)S(1)}, bf16[1024,128]{1,0:T(8,128)(2,1)S(1)}, u32[]{:S(2)}, u32[]{:S(2)}) collective-permute-start(bf16[1024,128]{1,0:T(8,128)(2,1)S(1)} %slice.39), channel_id=1, source_target_pairs={{0,16},{8,24},{16,0},{24,8},{32,48},{40,56},{48,32},{56,40},{64,80... | collective-permute-start | bytes 786440 | tf_op jit(solution)/shard_map/ppermute | solution.py:675
  146.1 0.7 copy-start
Sparse Core Ops, SparseCore 0:
  10.7 75.2 all-gather.1
Sparse Core Ops, SparseCore 1:
  73.0 55.9 reduce-scatter.1

commit v3 on v2

--- a/solution.py
+++ b/solution.py
@@ -37,7 +37,7 @@
 
 def packed(v):
     hi, mid, low = three_parts(v)
-    return (hi + pltpu.roll(mid, HEADS, 1) + pltpu.roll(low, 2 * HEADS, 1)).astype(BF16)
+    return hi + pltpu.roll(mid, HEADS, 1) + pltpu.roll(low, 2 * HEADS, 1)
 
 
 def halves(v):
@@ -56,11 +56,14 @@
     return i >= j if lower else i <= j
 
 
-def picker(pair, width):
-    row = lax.broadcasted_iota(jnp.int32, (LANES, 2 * width), 0)
-    col = lax.broadcasted_iota(jnp.int32, (LANES, 2 * width), 1)
-    head = 2 * pair + col // width
-    return jnp.where((row % HEADS == head) & (row < 3 * HEADS), 1.0, 0.0).astype(BF16)
+def picker(pair):
+    row = lax.broadcasted_iota(jnp.int32, (LANES, 4 * LANES), 0)
+    col = lax.broadcasted_iota(jnp.int32, (LANES, 4 * LANES), 1)
+    narrow = col < 2 * LANES
+    head = 2 * pair + jnp.where(narrow, (col % LANES) // WIDTH, col // CHUNK - 2)
+    first = jnp.where(col < LANES, 0, 3 * HEADS)
+    hit = (row % HEADS == head) & (row >= first) & (row < first + 3 * HEADS)
+    return jnp.where(hit, 1.0, 0.0).astype(BF16)
 
 
 def softplus(v):
@@ -77,12 +80,12 @@
 
 
 def prepare(raw_ref, raw_t_ref, bias_ref, rate_ref, bias_t_ref, rate_t_ref, b_ref, c_ref,
-            step_pack, run_pack, run_rows, step_rows, overlap):
+            pack, run_rows, step_rows, overlap):
     step, decay = steps_of(raw_ref, bias_ref, rate_ref)
-    step_pack[...] = packed(step)
+    step_pack = packed(step)
     lower = jnp.where(triangle(True), 1.0, 0.0).astype(BF16)
     upper = jnp.where(triangle(False), 1.0, 0.0).astype(BF16)
-    decay_pack = packed(decay)
+    decay_pack = packed(decay).astype(BF16)
     keep = lax.broadcasted_iota(jnp.int32, (CHUNK, LANES), 1) < HEADS
     step_t = softplus(raw_t_ref[...].astype(F32) + bias_t_ref[...])
     decay_t = three_parts(-step_t * jnp.exp(rate_t_ref[...]))
@@ -92,7 +95,8 @@
         rows = slice(c * CHUNK, (c + 1) * CHUNK)
         total = dot(lower, decay_pack[rows])
         total = total + pltpu.roll(total, LANES - HEADS, 1) + pltpu.roll(total, LANES - 2 * HEADS, 1)
-        run_pack[rows, :] = packed(jnp.where(keep, total, 0.0))
+        run_pack = pltpu.roll(packed(jnp.where(keep, total, 0.0)), 3 * HEADS, 1)
+        pack[rows, :] = (step_pack[rows] + run_pack).astype(BF16)
         across = sum(dot(part[:, rows].astype(BF16), upper) for part in decay_t)
         for pair in range(PAIRS):
             run_rows[pair, :, rows] = across[2 * pair : 2 * pair + 2, :]
@@ -119,32 +123,37 @@
 def forward_kernel(x_ref, g_ref, b_ref, bt_ref, c_ref, raw_ref, raw_t_ref, bias_ref, rate_ref,
                    bias_t_ref, rate_t_ref, skip_ref, gain_ref,
                    low_ref, scan_ref, gated_ref, state_ref, scale_ref,
-                   step_pack, run_pack, run_rows, step_rows, overlap, squares):
+                   pack, run_rows, step_rows, overlap, spread, squares):
     pair = pl.program_id(0)
 
     @pl.when(pair == 0)
     def _():
         prepare(raw_ref, raw_t_ref, bias_ref, rate_ref, bias_t_ref, rate_t_ref, b_ref, c_ref,
-                step_pack, run_pack, run_rows, step_rows, overlap)
+                pack, run_rows, step_rows, overlap)
         squares[...] = jnp.zeros_like(squares)
 
-    narrow, wide = picker(pair, WIDTH), picker(pair, CHUNK)
+    spread[...] = dot(pack[...], picker(pair))
     skip = skip_ref[:, pl.ds(pl.multiple_of(pair * LANES, LANES), LANES)]
     state = None
     for c in range(CHUNKS):
         rows = slice(c * CHUNK, (c + 1) * CHUNK)
         x = x_ref[rows, :].astype(F32)
-        step = dot(step_pack[rows, :], narrow)
-        run = dot(run_pack[rows, :], narrow)
-        columns = dot(run_pack[rows, :], wide)
+        step, run = spread[rows, :LANES], spread[rows, LANES : 2 * LANES]
+        columns = spread[rows, 2 * LANES :]
         weights = []
         for h, one in enumerate(decays(columns, run_rows, pair, rows)):
             weights.append(halves(one * overlap[c] * step_rows[pair, h : h + 1, rows]))
-        x_apart = apart(x)
         y = dot(
-            jnp.concatenate([weights[h][part] for part in range(2) for h in range(2)], axis=1),
-            jnp.concatenate([x_apart, x_apart], axis=0),
+            jnp.concatenate(
+                [
+                    jnp.concatenate([weights[h][part] for h in range(2)], axis=1)
+                    for part in range(2)
+                ],
+                axis=0,
+            ),
+            apart(x),
         )
+        y = y[:CHUNK] + y[CHUNK:]
         if c > 0:
             state_ref[0, c - 1] = state
             held = jnp.concatenate(halves(state), axis=1)
@@ -174,17 +183,17 @@
                     b_ref, c_ref, ct_ref, raw_ref, raw_t_ref, bias_ref, rate_ref,
                     bias_t_ref, rate_t_ref, skip_ref, gain_ref,
                     dx_ref, dg_ref, db_ref, dc_ref, step_ref, small_ref,
-                    step_pack, run_pack, run_rows, step_rows, overlap, d_overlap, d_b, d_c, flow, direct, lanes):
+                    pack, run_rows, step_rows, overlap, spread, d_overlap, d_b, d_c, flow, direct, lanes):
     pair = pl.program_id(0)
 
     @pl.when(pair == 0)
     def _():
         prepare(raw_ref, raw_t_ref, bias_ref, rate_ref, bias_t_ref, rate_t_ref, b_ref, c_ref,
-                step_pack, run_pack, run_rows, step_rows, overlap)
+                pack, run_rows, step_rows, overlap)
         for held in (d_overlap, d_b, d_c, flow, direct, lanes):
             held[...] = jnp.zeros_like(held)
 
-    narrow, wide = picker(pair, WIDTH), picker(pair, CHUNK)
+    spread[...] = dot(pack[...], picker(pair))
     here = pl.ds(pl.multiple_of(pair * LANES, LANES), LANES)
     skip, gain = skip_ref[:, here], gain_ref[:, here]
     first = first_half()
@@ -210,9 +219,8 @@
         dg_ref[rows, :] = (d_gated * out * (sig + silu * (1.0 - sig))).astype(BF16)
         skip_sum = skip_sum + jnp.sum(dy * x, axis=0, keepdims=True)
 
-        step = dot(step_pack[rows, :], narrow)
-        run = dot(run_pack[rows, :], narrow)
-        columns = dot(run_pack[rows, :], wide)
+        step, run = spread[rows, :LANES], spread[rows, LANES : 2 * LANES]
+        columns = spread[rows, 2 * LANES :]
         driven = x * step
         dy_hi, dy_low = (apart(part.astype(F32)) for part in halves(dy))
         factor = decays(columns, run_rows, pair, rows)
@@ -226,10 +234,9 @@
             factor[0] * products[:CHUNK] * step_row[:1] + factor[1] * products[CHUNK:] * step_row[1:]
         )
         weights = [halves(one * overlap[c]) for one in factor]
-        weights_hi = jnp.concatenate([one[0] for one in weights], axis=0)
-        weights_low = jnp.concatenate([one[1] for one in weights], axis=0)
-        d_driven = folded(dot(weights_hi, jnp.concatenate([dy_hi, dy_low], axis=1), (0, 0)))
-        d_driven = d_driven + dot(weights_low, dy_hi, (0, 0))
+        weights = jnp.concatenate([jnp.concatenate(one, axis=1) for one in weights], axis=0)
+        both = dot(weights, jnp.concatenate([dy_hi, dy_low], axis=1), (0, 0))
+        d_driven = folded(both[:CHUNK]) + both[CHUNK:, :LANES]
         entering_hi, entering_low = halves(dy * jnp.exp(run))
         entering = jnp.concatenate([entering_hi, entering_low], axis=1)
         end = run[CHUNK - 1 :, :]
@@ -313,10 +320,10 @@
 
 TABLES = [
     pltpu.VMEM((TOKENS, LANES), BF16),
-    pltpu.VMEM((TOKENS, LANES), BF16),
     pltpu.VMEM((PAIRS, 2, TOKENS), F32),
     pltpu.VMEM((PAIRS, 2, TOKENS), F32),
     pltpu.VMEM((CHUNKS, CHUNK, CHUNK), F32),
+    pltpu.VMEM((TOKENS, 4 * LANES), F32),
 ]
 
 PARAMETERS = [
@@ -669,12 +676,12 @@
         scan_input, gate_input, cot, scan, states, scale, pull, b, c, c.T, parameters
     )
     summed = jnp.concatenate([small, gain_grad.reshape(8, LANES)], axis=0)
-    for bit in (1, 2, 4, 8, 16):
+    for bit in (1, 4, 8, 16):
         summed = summed + lax.ppermute(summed, "blk", swap(bit))
     plane, summed = lax.optimization_barrier((plane, summed))
     given = lax.ppermute(plane[:CHANNELS], "blk", swap(2))
     weight_grad = finish(plane, given, norm_scale)
-    summed = summed * norm_scale
+    summed = (summed + lax.ppermute(summed, "blk", swap(2))) * norm_scale
     return (
         dx,
         dg,

time: 157 us -> 158 us (level)
  waiting for transfers between devices: 30.4 us -> 33.6 us
    ppermute x5 -> x4, waiting for transfers between devices: 9.07 us -> 10.7 us  [shards(): summed = summed + lax.ppermute(summed, 'blk', swap(bit))]
    ppermute x5 -> x4, starting transfers between devices: 8.48 us -> 7.02 us  [shards(): summed = summed + lax.ppermute(summed, 'blk', swap(bit))]
  transfers between devices with their start and end apart: 19 -> 19, of which waited for: 11 -> 11; matrix products, arithmetic and copies ran while one was open for 13% -> 14% of each run, Pallas kernels for 39% -> 38%
where the time goes in v3:
time: 158 us
  Pallas kernels  61.6 us (39%)
  waiting for transfers between devices  33.6 us (21%)
  local copies, waits for them, and re-layouts  21.9 us (14%)
  starting transfers between devices  21.8 us (14%)
  between operations  15.7 us (10%)
  other arithmetic  3.04 us (2%)
    pallas_call x1, Pallas kernels, scan_backward(): pl.pallas_call(backward_kernel, grid=(PAIRS,), in_specs=[by_pair(TOKENS),...  18 us
    pallas_call x3, Pallas kernels, terms(): pl.pallas_call(kernel, grid_spec=pltpu.PrefetchScalarGridSpec(num_scalar_...  17.1 us
    pallas_call x1, Pallas kernels, scan_forward(): pl.pallas_call(forward_kernel, grid=(PAIRS,), in_specs=[by_pair(TOKENS),...  13.1 us
    pallas_call x1, Pallas kernels, products(): pl.pallas_call(product_kernel, grid_spec=pltpu.PrefetchScalarGridSpec(num...  11.4 us
    all_gather x1, waiting for transfers between devices, shards(): rows = lax.all_gather(out_proj, 'blk', axis=0, tiled=True)  11.2 us
    ppermute x4, waiting for transfers between devices, shards(): summed = summed + lax.ppermute(summed, 'blk', swap(bit))  10.7 us
    unnamed x28, local copies, waits for them, and re-layouts  8.32 us
    ppermute x4, starting transfers between devices, shards(): summed = summed + lax.ppermute(summed, 'blk', swap(bit))  7.02 us
  transfers between devices with their start and end apart: 19, of which 11 were waited for; matrix products, arithmetic and copies ran while one was open for 14% of the time, Pallas kernels for 38%

profile of v3, /device:TPU:6, one launch (start us, length us, event | category | flops | bytes accessed | tf_op | source)
XLA Modules:
  0.0 157.7 jit_solution(17249982823155306905)
XLA Ops:
  8.1 0.7 all-gather.2.cloned.1.call-update
  8.8 3.3 %collective-permute-start = (bf16[512,512]{1,0:T(8,128)(2,1)}, bf16[512,512]{1,0:T(8,128)(2,1)}, u32[]{:S(2)}, u32[]{:S(2)}) collective-permute-start(bf16[512,512]{1,0:T(8,128)(2,1)} %refs_0_.1), channel_id=1, source_target_pairs={{0,1},{1,0},{2,3},{3,2},{4,5},{5,4},{6,7},{7,6},{8,9},{9,8},{10,11... | collective-permute-start | bytes 1572872 | tf_op jit(solution)/shard_map/ppermute | solution.py:631
  12.6 1.5 collective-permute-start.2
  14.1 2.1 %fusion.1 = (bf16[512,1,256]{2,1,0:T(2,128)(2,1)S(1)}, bf16[512,1,256]{2,1,0:T(2,128)(2,1)S(1)}) fusion(bf16[512,2,256]{2,1,0:T(2,128)(2,1)} %param.12), kind=kLoop, calls=%fused_computation.17 | loop fusion | bytes 1048576 | tf_op jit(solution)/shard_map/slice | solution.py:640
  16.2 1.3 copy.33
  17.5 0.8 copy.21
  18.4 0.7 broadcast_in_dim.3
  19.1 0.7 reshape_reshape.3.skip_ref
  19.8 1.3 copy.24.bias_t_ref
  21.1 1.3 copy.25.rate_t_ref
  22.4 0.7 pad.11.raw_ref
  24.3 0.9 copy_bitcast_fusion
  25.7 1.4 collective-permute-done.2.refs_5_.refs_6_.refs_2_
  27.5 1.7 %collective-permute-start.4 = (bf16[512,512]{1,0:T(8,128)(2,1)}, bf16[512,512]{1,0:T(8,128)(2,1)S(1)}, u32[]{:S(2)}, u32[]{:S(2)}) collective-permute-start(bf16[512,512]{1,0:T(8,128)(2,1)} %collective-permute-done.refs_9_.refs_10_.refs_4_), channel_id=1, source_target_pairs={{0,6},{1,7},{2,0},{3,1},{4,2},{5,3},{6,4},{7,5},{8,14},{9,15},{10,... | collective-permute-start | bytes 1572872 | tf_op jit(solution)/shard_map/ppermute | solution.py:583
  29.2 1.6 %collective-permute-start.5 = (bf16[256,512]{1,0:T(8,128)(2,1)S(1)}, bf16[256,512]{1,0:T(8,128)(2,1)S(1)}, u32[]{:S(2)}, u32[]{:S(2)}) collective-permute-start(bf16[256,512]{1,0:T(8,128)(2,1)S(1)} %slice.33), channel_id=1, source_target_pairs={{0,2},{1,3},{2,4},{3,5},{4,6},{5,7},{6,0},{7,1},{8,10},{9,11},{10,... | collective-permute-start | bytes 786440 | tf_op jit(solution)/shard_map/ppermute | solution.py:588
  31.4 13.1 %scan_forward.1 = (bf16[1024,512]{1,0:T(8,128)(2,1)}, f32[512,1024]{1,0:T(8,128)}, f32[512,1024]{1,0:T(8,128)}, f32[8,3,256,128]{3,2,1,0:T(8,128)}, f32[512,128]{1,0:T(8,128)}) custom-call(bf16[512,1024]{1,0:T(8,128)(2,1)} %x_ref.1, bf16[512,1024]{1,0:T(8,128)(2,1)} %g_ref.3, bf16[512,256]{1,0:T(8,128)(2,1)} %get-tuple-element.82.b_ref, ...), custom_call_target="tpu_custom_call" | custom-call | flops 16000000000 | bytes 10000000 | tf_op jit(solution)/shard_map/scan_forward/pallas_call | solution.py:342
  45.1 1.6 %collective-permute-done.6 = bf16[256,512]{1,0:T(8,128)(2,1)S(1)} collective-permute-done((bf16[256,512]{1,0:T(8,128)(2,1)S(1)}, bf16[256,512]{1,0:T(8,128)(2,1)S(1)}, u32[]{:S(2)}, u32[]{:S(2)}) %collective-permute-start.6) | collective-permute-done | bytes 262176 | tf_op jit(solution)/shard_map/ppermute | solution.py:589
  46.7 0.7 collective-permute-start.7
  47.5 1.6 %collective-permute-start.8 = (bf16[256,512]{1,0:T(8,128)(2,1)S(1)}, bf16[256,512]{1,0:T(8,128)(2,1)S(1)}, u32[]{:S(2)}, u32[]{:S(2)}) collective-permute-start(bf16[256,512]{1,0:T(8,128)(2,1)S(1)} %slice.38), channel_id=1, source_target_pairs={{0,6},{1,7},{2,0},{3,1},{4,2},{5,3},{6,4},{7,5},{8,14},{9,15},{10,... | collective-permute-start | bytes 786440 | tf_op jit(solution)/shard_map/ppermute | solution.py:589
  49.2 0.8 copy-done.5
  50.0 6.0 %terms.2 = bf16[14336,128]{1,0:T(8,128)(2,1)} custom-call(s32[9]{0:T(128)} %stack.86.refs_0_, bf16[512,512]{1,0:T(8,128)(2,1)} %refs_0_.1, bf16[512,512]{1,0:T(8,128)(2,1)} %refs_0_.1, bf16[512,512]{1,0:T(8,128)(2,1)} %copy-done.1, bf16[512,512]{1,0:T(8,128)(2,1)} %copy-done.1, bf16[512,512]{1,0:T(8,128)(2,1)} %copy-done.2, bf16[512,512]{1,0:T(8,128)(2,1)} %copy-done.2, ...), custom_call_target="tpu_custom_call" | custom-call | flops 5600000000 | bytes 2000000 | tf_op jit(solution)/shard_map/terms/pallas_call | solution.py:471
  56.8 0.8 copy-done.6
  57.6 3.3 %terms.3 = bf16[2048,128]{1,0:T(8,128)(2,1)} custom-call(s32[3]{0:T(128)} %pad_add_fusion.refs_0_, bf16[512,512]{1,0:T(8,128)(2,1)} %copy-done.6, bf16[512,512]{1,0:T(8,128)(2,1)} %copy-done.6, bf16[1024,512]{1,0:T(8,128)(2,1)} %get-tuple-element.47.refs_15_.refs_3_.refs_17_), custom_call_target="tpu_custom_call" | custom-call | flops 1400000000 | bytes 2000000 | tf_op jit(solution)/shard_map/terms/pallas_call | solution.py:471
  62.2 2.2 %collective-permute-done.10.refs_19_ = bf16[2048,128]{1,0:T(8,128)(2,1)S(1)} collective-permute-done((bf16[2048,128]{1,0:T(8,128)(2,1)}, bf16[2048,128]{1,0:T(8,128)(2,1)S(1)}, u32[]{:S(2)}, u32[]{:S(2)}) %collective-permute-start.10) | collective-permute-done | bytes 524320 | tf_op jit(solution)/shard_map/ppermute | solution.py:661
  64.4 0.8 copy-done.10
  65.2 7.7 %terms_added.1 = bf16[16384,128]{1,0:T(8,128)(2,1)} custom-call(s32[10]{0:T(128)} %stack.89.refs_0_, bf16[512,512]{1,0:T(8,128)(2,1)} %refs_0_.1, bf16[512,512]{1,0:T(8,128)(2,1)} %refs_0_.1, bf16[512,512]{1,0:T(8,128)(2,1)} %copy-done.1, bf16[512,512]{1,0:T(8,128)(2,1)} %copy-done.1, bf16[512,512]{1,0:T(8,128)(2,1)} %copy-done.2, ...), custom_call_target="tpu_custom_call" | custom-call | flops 6300000256 | bytes 2000000 | tf_op jit(solution)/shard_map/terms_added/pallas_call | solution.py:471
  73.6 1.3 copy.32
  74.9 11.2 %all-gather.2.cloned.1.call-done.refs_8_ = bf16[4096,1024]{1,0:T(8,128)(2,1)} async-done(((bf16[128,1024]{1,0:T(8,128)(2,1)}), bf16[4096,1024]{1,0:T(8,128)(2,1)}) %all-gather.2.cloned.1.call-update) | async-done | bytes 8388624 | tf_op jit(solution)/shard_map/all_gather | solution.py:629
  86.1 11.4 %products.1 = (f32[512,1024]{1,0:T(8,128)}, f32[1,1024]{1,0:T(1,128)}, f32[512,128]{1,0:T(8,128)}) custom-call(s32[8]{0:T(128)} %stack.83.places, bf16[512,512]{1,0:T(8,128)(2,1)} %refs_0_.1, bf16[512,512]{1,0:T(8,128)(2,1)} %copy-done.1, bf16[512,512]{1,0:T(8,128)(2,1)} %copy-done.2, bf16[512,512]{1,0:T(8,128)(2,1)} %copy-done.5, ...), custom_call_target="tpu_custom_call" | custom-call | flops 12000000000 | bytes 16000000 | tf_op jit(solution)/shard_map/products/pallas_call | solution.py:546
  97.6 18.0 %scan_backward.1 = (bf16[512,1024]{1,0:T(8,128)(2,1)}, bf16[512,1024]{1,0:T(8,128)(2,1)}, bf16[512,256]{1,0:T(8,128)(2,1)}, bf16[512,256]{1,0:T(8,128)(2,1)}, f32[512,16]{1,0:T(8,128)}, /*index=5*/f32[8,128]{1,0:T(8,128)}) custom-call(bf16[512,1024]{1,0:T(8,128)(2,1)} %x_ref.1, bf16[512,1024]{1,0:T(8,128)(2,1)} %g_ref.3, ...), custom_call_target="tpu_custom_call" | custom-call | flops 20000000000 | bytes 10000000 | tf_op jit(solution)/shard_map/scan_backward/pallas_call | solution.py:375
  115.6 0.7 pad_maximum_fusion.1
  116.5 0.9 collective-permute-done.11
  117.4 0.7 fusion
  118.1 0.7 collective-permute-start.12
  118.8 3.3 %collective-permute-done.12 = f32[16,128]{1,0:T(8,128)S(1)} collective-permute-done((f32[16,128]{1,0:T(8,128)S(1)}, f32[16,128]{1,0:T(8,128)S(1)}, u32[]{:S(2)}, u32[]{:S(2)}) %collective-permute-start.12) | collective-permute-done | bytes 8224 | tf_op jit(solution)/shard_map/ppermute | solution.py:680
  122.1 2.0 %collective-permute-start.13 = (f32[16,128]{1,0:T(8,128)S(1)}, f32[16,128]{1,0:T(8,128)S(1)}, u32[]{:S(2)}, u32[]{:S(2)}) collective-permute-start(f32[16,128]{1,0:T(8,128)S(1)} %add.122), channel_id=1, source_target_pairs={{0,64},{8,72},{16,80},{24,88},{32,96},{40,104},{48,112},{56,120},{... | collective-permute-start | bytes 24584 | tf_op jit(solution)/shard_map/ppermute | solution.py:680
  124.1 2.9 %collective-permute-done.13 = f32[16,128]{1,0:T(8,128)S(1)} collective-permute-done((f32[16,128]{1,0:T(8,128)S(1)}, f32[16,128]{1,0:T(8,128)S(1)}, u32[]{:S(2)}, u32[]{:S(2)}) %collective-permute-start.13) | collective-permute-done | bytes 8224 | tf_op jit(solution)/shard_map/ppermute | solution.py:680
  127.1 4.1 %collective-permute-start.14 = (f32[16,128]{1,0:T(8,128)S(1)}, f32[16,128]{1,0:T(8,128)S(1)}, u32[]{:S(2)}, u32[]{:S(2)}) collective-permute-start(f32[16,128]{1,0:T(8,128)S(1)} %add.123), channel_id=1, source_target_pairs={{0,128},{8,136},{16,144},{24,152},{32,160},{40,168},{48,176},{56,1... | collective-permute-start | bytes 24584 | tf_op jit(solution)/shard_map/ppermute | solution.py:680
  131.1 3.5 %collective-permute-done.14 = f32[16,128]{1,0:T(8,128)S(1)} collective-permute-done((f32[16,128]{1,0:T(8,128)S(1)}, f32[16,128]{1,0:T(8,128)S(1)}, u32[]{:S(2)}, u32[]{:S(2)}) %collective-permute-start.14) | collective-permute-done | bytes 8224 | tf_op jit(solution)/shard_map/ppermute | solution.py:680
  134.6 1.4 collective-permute-start.16
  136.0 1.1 pad_maximum_fusion
  137.1 1.3 copy.29
  138.4 1.7 %copy.30 = f32[512,16]{0,1:T(8,128)} copy(f32[512,16]{1,0:T(8,128)} %get-tuple-element.70) | data formatting | bytes 65536
  140.1 1.0 slice.39
  141.1 0.7 collective-permute-start.15
  142.9 4.6 %collective-permute-done.15.refs_1_ = bf16[1024,128]{1,0:T(8,128)(2,1)S(1)} collective-permute-done((bf16[1024,128]{1,0:T(8,128)(2,1)S(1)}, bf16[1024,128]{1,0:T(8,128)(2,1)S(1)}, u32[]{:S(2)}, u32[]{:S(2)}) %collective-permute-start.15) | collective-permute-done | bytes 262176 | tf_op jit(solution)/shard_map/ppermute | solution.py:682
  147.5 0.7 copy-done
  148.2 2.0 %finish.1 = f32[128,1024]{1,0:T(8,128)} custom-call(bf16[2048,128]{1,0:T(8,128)(2,1)} %reduce-scatter.2.cloned.1.call-done.refs_0_, bf16[1024,128]{1,0:T(8,128)(2,1)} %copy-done), custom_call_target="tpu_custom_call" | custom-call | tf_op jit(solution)/shard_map/finish/pallas_call | solution.py:503
  (56 shorter events, 7.8 us)
Async XLA Ops:
  8.0 15.7 %copy-start.9 = (f32[16]{0:T(128)S(1)}, f32[16]{0:T(128)}, u32[]{:S(2)}) copy-start(f32[16]{0:T(128)} %param.15) | copy-start | bytes 196
  8.0 15.7 %copy-start.8 = (f32[16]{0:T(128)S(1)}, f32[16]{0:T(128)}, u32[]{:S(2)}) copy-start(f32[16]{0:T(128)} %param.14) | copy-start | bytes 196
  8.0 78.1 %all-gather.2.cloned.1.call-start = ((), (), s32[]{:S(2)}) async-start(), calls=%async_computation.1 | async-start | bytes 8650752 | tf_op jit(solution)/shard_map/all_gather | solution.py:629
  8.8 125.9 %reduce-scatter.2.cloned.1.call-start = ((), (), s32[]{:S(2)}) async-start(), calls=%async_computation.2 | async-start | bytes 4718592 | tf_op jit(solution)/shard_map/reduce_scatter | solution.py:663
  8.8 16.3 %collective-permute-start = (bf16[512,512]{1,0:T(8,128)(2,1)}, bf16[512,512]{1,0:T(8,128)(2,1)}, u32[]{:S(2)}, u32[]{:S(2)}) collective-permute-start(bf16[512,512]{1,0:T(8,128)(2,1)} %refs_0_.1), channel_id=1, source_target_pairs={{0,1},{1,0},{2,3},{3,2},{4,5},{5,4},{6,7},{7,6},{8,9},{9,8},{10,11... | collective-permute-start | bytes 1572872 | tf_op jit(solution)/shard_map/ppermute | solution.py:631
  12.1 13.6 %collective-permute-start.1 = (bf16[512,512]{1,0:T(8,128)(2,1)}, bf16[512,512]{1,0:T(8,128)(2,1)S(1)}, u32[]{:S(2)}, u32[]{:S(2)}) collective-permute-start(bf16[512,512]{1,0:T(8,128)(2,1)} %refs_0_.1), channel_id=1, source_target_pairs={{0,2},{1,3},{2,4},{3,5},{4,6},{5,7},{6,0},{7,1},{8,10},{9,11},{10,... | collective-permute-start | bytes 1572872 | tf_op jit(solution)/shard_map/ppermute | solution.py:583
  12.6 14.5 %collective-permute-start.2 = (bf16[512,512]{1,0:T(8,128)(2,1)}, bf16[512,512]{1,0:T(8,128)(2,1)S(1)}, u32[]{:S(2)}, u32[]{:S(2)}) collective-permute-start(bf16[512,512]{1,0:T(8,128)(2,1)} %refs_0_.1), channel_id=1, source_target_pairs={{0,6},{1,7},{2,0},{3,1},{4,2},{5,3},{6,4},{7,5},{8,14},{9,15},{10,... | collective-permute-start | bytes 1572872 | tf_op jit(solution)/shard_map/ppermute | solution.py:583
  25.7 18.8 %copy-start.1 = (bf16[512,512]{1,0:T(8,128)(2,1)}, bf16[512,512]{1,0:T(8,128)(2,1)S(1)}, u32[]{:S(2)}) copy-start(bf16[512,512]{1,0:T(8,128)(2,1)S(1)} %collective-permute-done.1.refs_3_.refs_4_.refs_1_) | copy-start | bytes 1572868
  27.1 17.4 %copy-start.2 = (bf16[512,512]{1,0:T(8,128)(2,1)}, bf16[512,512]{1,0:T(8,128)(2,1)S(1)}, u32[]{:S(2)}) copy-start(bf16[512,512]{1,0:T(8,128)(2,1)S(1)} %collective-permute-done.2.refs_5_.refs_6_.refs_2_) | copy-start | bytes 1572868
  27.1 19.6 %collective-permute-start.3 = (bf16[512,512]{1,0:T(8,128)(2,1)}, bf16[512,512]{1,0:T(8,128)(2,1)S(1)}, u32[]{:S(2)}, u32[]{:S(2)}) collective-permute-start(bf16[512,512]{1,0:T(8,128)(2,1)} %collective-permute-done.refs_9_.refs_10_.refs_4_), channel_id=1, source_target_pairs={{0,2},{1,3},{2,4},{3,5},{4,6},{5,7},{6,0},{7,1},{8,10},{9,11},{10,... | collective-permute-start | bytes 1572872 | tf_op jit(solution)/shard_map/ppermute | solution.py:583
  27.5 19.2 %collective-permute-start.4 = (bf16[512,512]{1,0:T(8,128)(2,1)}, bf16[512,512]{1,0:T(8,128)(2,1)S(1)}, u32[]{:S(2)}, u32[]{:S(2)}) collective-permute-start(bf16[512,512]{1,0:T(8,128)(2,1)} %collective-permute-done.refs_9_.refs_10_.refs_4_), channel_id=1, source_target_pairs={{0,6},{1,7},{2,0},{3,1},{4,2},{5,3},{6,4},{7,5},{8,14},{9,15},{10,... | collective-permute-start | bytes 1572872 | tf_op jit(solution)/shard_map/ppermute | solution.py:583
  29.2 16.0 %collective-permute-start.5 = (bf16[256,512]{1,0:T(8,128)(2,1)S(1)}, bf16[256,512]{1,0:T(8,128)(2,1)S(1)}, u32[]{:S(2)}, u32[]{:S(2)}) collective-permute-start(bf16[256,512]{1,0:T(8,128)(2,1)S(1)} %slice.33), channel_id=1, source_target_pairs={{0,2},{1,3},{2,4},{3,5},{4,6},{5,7},{6,0},{7,1},{8,10},{9,11},{10,... | collective-permute-start | bytes 786440 | tf_op jit(solution)/shard_map/ppermute | solution.py:588
  30.8 15.9 %collective-permute-start.6 = (bf16[256,512]{1,0:T(8,128)(2,1)S(1)}, bf16[256,512]{1,0:T(8,128)(2,1)S(1)}, u32[]{:S(2)}, u32[]{:S(2)}) collective-permute-start(bf16[256,512]{1,0:T(8,128)(2,1)S(1)} %slice.34), channel_id=1, source_target_pairs={{0,6},{1,7},{2,0},{3,1},{4,2},{5,3},{6,4},{7,5},{8,14},{9,15},{10,... | collective-permute-start | bytes 786440 | tf_op jit(solution)/shard_map/ppermute | solution.py:589
  46.7 2.5 %copy-start.3 = (bf16[512,512]{1,0:T(8,128)(2,1)}, bf16[512,512]{1,0:T(8,128)(2,1)S(1)}, u32[]{:S(2)}) copy-start(bf16[512,512]{1,0:T(8,128)(2,1)S(1)} %collective-permute-done.3.refs_11_.refs_12_.refs_5_) | copy-start | bytes 1572868
  46.7 2.5 %copy-start.4 = (bf16[512,512]{1,0:T(8,128)(2,1)}, bf16[512,512]{1,0:T(8,128)(2,1)S(1)}, u32[]{:S(2)}) copy-start(bf16[512,512]{1,0:T(8,128)(2,1)S(1)} %collective-permute-done.4.refs_13_.refs_14_.refs_6_) | copy-start | bytes 1572868
  46.7 9.3 %collective-permute-start.7 = (bf16[256,512]{1,0:T(8,128)(2,1)S(1)}, bf16[256,512]{1,0:T(8,128)(2,1)S(1)}, u32[]{:S(2)}, u32[]{:S(2)}) collective-permute-start(bf16[256,512]{1,0:T(8,128)(2,1)S(1)} %slice.37), channel_id=1, source_target_pairs={{0,2},{1,3},{2,4},{3,5},{4,6},{5,7},{6,0},{7,1},{8,10},{9,11},{10,... | collective-permute-start | bytes 786440 | tf_op jit(solution)/shard_map/ppermute | solution.py:588
  47.5 8.6 %collective-permute-start.8 = (bf16[256,512]{1,0:T(8,128)(2,1)S(1)}, bf16[256,512]{1,0:T(8,128)(2,1)S(1)}, u32[]{:S(2)}, u32[]{:S(2)}) collective-permute-start(bf16[256,512]{1,0:T(8,128)(2,1)S(1)} %slice.38), channel_id=1, source_target_pairs={{0,6},{1,7},{2,0},{3,1},{4,2},{5,3},{6,4},{7,5},{8,14},{9,15},{10,... | collective-permute-start | bytes 786440 | tf_op jit(solution)/shard_map/ppermute | solution.py:589
  49.2 0.8 copy-start.5
  56.1 8.3 %collective-permute-start.9 = (bf16[14336,128]{1,0:T(8,128)(2,1)}, bf16[14336,128]{1,0:T(8,128)(2,1)}, u32[]{:S(2)}, u32[]{:S(2)}) collective-permute-start(bf16[14336,128]{1,0:T(8,128)(2,1)} %terms.2), channel_id=1, source_target_pairs={{0,8},{8,0},{16,24},{24,16},{32,40},{40,32},{48,56},{56,48},{64,72... | collective-permute-start | bytes 11010056 | tf_op jit(solution)/shard_map/ppermute | solution.py:659
  56.8 0.8 copy-start.6
  61.0 3.4 %collective-permute-start.10 = (bf16[2048,128]{1,0:T(8,128)(2,1)}, bf16[2048,128]{1,0:T(8,128)(2,1)S(1)}, u32[]{:S(2)}, u32[]{:S(2)}) collective-permute-start(bf16[2048,128]{1,0:T(8,128)(2,1)} %terms.3), channel_id=1, source_target_pairs={{0,8},{8,0},{16,24},{24,16},{32,40},{40,32},{48,56},{56,48},{64,72... | collective-permute-start | bytes 1572872 | tf_op jit(solution)/shard_map/ppermute | solution.py:661
  64.4 0.8 copy-start.10
  97.6 18.0 %copy-start.7 = (f32[1,1024]{1,0:T(1,128)S(1)}, f32[1,1024]{1,0:T(1,128)}, u32[]{:S(2)}) copy-start(f32[1,1024]{1,0:T(1,128)} %get-tuple-element.64) | copy-start | bytes 12292
  116.2 1.2 collective-permute-start.11
  118.1 4.0 %collective-permute-start.12 = (f32[16,128]{1,0:T(8,128)S(1)}, f32[16,128]{1,0:T(8,128)S(1)}, u32[]{:S(2)}, u32[]{:S(2)}) collective-permute-start(f32[16,128]{1,0:T(8,128)S(1)} %fusion), channel_id=1, source_target_pairs={{0,32},{8,40},{16,48},{24,56},{32,0},{40,8},{48,16},{56,24},{64,96... | collective-permute-start | bytes 24584 | tf_op jit(solution)/shard_map/ppermute | solution.py:680
  122.1 5.0 %collective-permute-start.13 = (f32[16,128]{1,0:T(8,128)S(1)}, f32[16,128]{1,0:T(8,128)S(1)}, u32[]{:S(2)}, u32[]{:S(2)}) collective-permute-start(f32[16,128]{1,0:T(8,128)S(1)} %add.122), channel_id=1, source_target_pairs={{0,64},{8,72},{16,80},{24,88},{32,96},{40,104},{48,112},{56,120},{... | collective-permute-start | bytes 24584 | tf_op jit(solution)/shard_map/ppermute | solution.py:680
  127.1 7.6 %collective-permute-start.14 = (f32[16,128]{1,0:T(8,128)S(1)}, f32[16,128]{1,0:T(8,128)S(1)}, u32[]{:S(2)}, u32[]{:S(2)}) collective-permute-start(f32[16,128]{1,0:T(8,128)S(1)} %add.123), channel_id=1, source_target_pairs={{0,128},{8,136},{16,144},{24,152},{32,160},{40,168},{48,176},{56,1... | collective-permute-start | bytes 24584 | tf_op jit(solution)/shard_map/ppermute | solution.py:680
  134.6 7.2 %collective-permute-start.16 = (f32[16,128]{1,0:T(8,128)S(1)}, f32[16,128]{1,0:T(8,128)S(1)}, u32[]{:S(2)}, u32[]{:S(2)}) collective-permute-start(f32[16,128]{1,0:T(8,128)S(1)} %add.124), channel_id=1, source_target_pairs={{0,16},{8,24},{16,0},{24,8},{32,48},{40,56},{48,32},{56,40},{64,80... | collective-permute-start | bytes 24584 | tf_op jit(solution)/shard_map/ppermute | solution.py:684
  141.1 6.5 %collective-permute-start.15 = (bf16[1024,128]{1,0:T(8,128)(2,1)S(1)}, bf16[1024,128]{1,0:T(8,128)(2,1)S(1)}, u32[]{:S(2)}, u32[]{:S(2)}) collective-permute-start(bf16[1024,128]{1,0:T(8,128)(2,1)S(1)} %slice.39), channel_id=1, source_target_pairs={{0,16},{8,24},{16,0},{24,8},{32,48},{40,56},{48,32},{56,40},{64,80... | collective-permute-start | bytes 786440 | tf_op jit(solution)/shard_map/ppermute | solution.py:682
  147.5 0.7 copy-start
Sparse Core Ops, SparseCore 0:
  10.7 75.3 all-gather.1
Sparse Core Ops, SparseCore 1:
  73.0 55.8 reduce-scatter.1

commit v4 on v3

--- a/solution.py
+++ b/solution.py
@@ -74,33 +74,40 @@
     return lax.broadcasted_iota(jnp.int32, (TOKENS, LANES), 1) < HEADS
 
 
-def steps_of(raw_ref, bias_ref, rate_ref):
-    step = jnp.where(head_lanes(), softplus(raw_ref[...].astype(F32) + bias_ref[...]), 0.0)
+def steps_of(raw, bias_ref, rate_ref):
+    step = jnp.where(head_lanes(), softplus(raw[...] + bias_ref[...]), 0.0)
     return step, -step * jnp.exp(rate_ref[...])
 
 
-def prepare(raw_ref, raw_t_ref, bias_ref, rate_ref, bias_t_ref, rate_t_ref, b_ref, c_ref,
-            pack, run_rows, step_rows, overlap):
-    step, decay = steps_of(raw_ref, bias_ref, rate_ref)
+def prepare(raw_t_ref, bias_ref, rate_ref, bc_ref, turned, source,
+            raw, pack, run_rows, step_rows, overlap):
+    empty = jnp.zeros((CHUNK - HEADS, CHUNK), F32)
+    for c in range(CHUNKS):
+        rows = slice(c * CHUNK, (c + 1) * CHUNK)
+        wide = jnp.concatenate([raw_t_ref[:, rows].astype(F32), empty], axis=0)
+        raw[rows, :] = wide.T
+        turned[:, rows] = bc_ref[rows, source : source + STATE].astype(F32).T.astype(BF16)
+    step, decay = steps_of(raw, bias_ref, rate_ref)
     step_pack = packed(step)
     lower = jnp.where(triangle(True), 1.0, 0.0).astype(BF16)
     upper = jnp.where(triangle(False), 1.0, 0.0).astype(BF16)
     decay_pack = packed(decay).astype(BF16)
     keep = lax.broadcasted_iota(jnp.int32, (CHUNK, LANES), 1) < HEADS
-    step_t = softplus(raw_t_ref[...].astype(F32) + bias_t_ref[...])
-    decay_t = three_parts(-step_t * jnp.exp(rate_t_ref[...]))
-    for pair in range(PAIRS):
-        step_rows[pair] = step_t[2 * pair : 2 * pair + 2, :]
     for c in range(CHUNKS):
         rows = slice(c * CHUNK, (c + 1) * CHUNK)
         total = dot(lower, decay_pack[rows])
         total = total + pltpu.roll(total, LANES - HEADS, 1) + pltpu.roll(total, LANES - 2 * HEADS, 1)
         run_pack = pltpu.roll(packed(jnp.where(keep, total, 0.0)), 3 * HEADS, 1)
         pack[rows, :] = (step_pack[rows] + run_pack).astype(BF16)
-        across = sum(dot(part[:, rows].astype(BF16), upper) for part in decay_t)
+        step_t = step[rows].T
+        decay_t = three_parts(decay[rows].T[:HEADS])
+        across = sum(dot(part.astype(BF16), upper) for part in decay_t)
         for pair in range(PAIRS):
-            run_rows[pair, :, rows] = across[2 * pair : 2 * pair + 2, :]
-        overlap[c] = jnp.where(triangle(True), dot(c_ref[rows, :], b_ref[rows, :], (1, 1)), 0.0)
+            heads = slice(2 * pair, 2 * pair + 2)
+            run_rows[pair, :, rows] = across[heads, :]
+            step_rows[pair, :, rows] = step_t[heads, :]
+        b, c_low = bc_ref[rows, :STATE], bc_ref[rows, STATE:]
+        overlap[c] = jnp.where(triangle(True), dot(c_low, b, (1, 1)), 0.0)
 
 
 def first_half():
@@ -120,16 +127,15 @@
     return out
 
 
-def forward_kernel(x_ref, g_ref, b_ref, bt_ref, c_ref, raw_ref, raw_t_ref, bias_ref, rate_ref,
-                   bias_t_ref, rate_t_ref, skip_ref, gain_ref,
+def forward_kernel(x_ref, g_ref, bc_ref, raw_t_ref, bias_ref, rate_ref, skip_ref, gain_ref,
                    low_ref, scan_ref, gated_ref, state_ref, scale_ref,
-                   pack, run_rows, step_rows, overlap, spread, squares):
+                   raw, pack, run_rows, step_rows, overlap, spread, turned, squares):
     pair = pl.program_id(0)
 
     @pl.when(pair == 0)
     def _():
-        prepare(raw_ref, raw_t_ref, bias_ref, rate_ref, bias_t_ref, rate_t_ref, b_ref, c_ref,
-                pack, run_rows, step_rows, overlap)
+        prepare(raw_t_ref, bias_ref, rate_ref, bc_ref, turned, 0,
+                raw, pack, run_rows, step_rows, overlap)
         squares[...] = jnp.zeros_like(squares)
 
     spread[...] = dot(pack[...], picker(pair))
@@ -157,11 +163,11 @@
         if c > 0:
             state_ref[0, c - 1] = state
             held = jnp.concatenate(halves(state), axis=1)
-            y = y + jnp.exp(run) * folded(dot(c_ref[rows, :], held))
+            y = y + jnp.exp(run) * folded(dot(bc_ref[rows, STATE:], held))
         if c < CHUNKS - 1:
             end = run[CHUNK - 1 :, :]
             fresh = jnp.concatenate(halves(x * step * jnp.exp(end - run)), axis=1)
-            local = folded(dot(bt_ref[:, rows], fresh))
+            local = folded(dot(turned[:, rows], fresh))
             state = local if c == 0 else jnp.exp(end) * state + local
         scan_ref[rows, :] = y
         g = g_ref[rows, :].astype(F32)
@@ -180,16 +186,15 @@
 
 
 def backward_kernel(x_ref, g_ref, cot_ref, scan_ref, state_ref, scale_ref, pull_ref,
-                    b_ref, c_ref, ct_ref, raw_ref, raw_t_ref, bias_ref, rate_ref,
-                    bias_t_ref, rate_t_ref, skip_ref, gain_ref,
+                    bc_ref, raw_t_ref, bias_ref, rate_ref, skip_ref, gain_ref,
                     dx_ref, dg_ref, db_ref, dc_ref, step_ref, small_ref,
-                    pack, run_rows, step_rows, overlap, spread, d_overlap, d_b, d_c, flow, direct, lanes):
+                    raw, pack, run_rows, step_rows, overlap, spread, turned, d_overlap, d_b, d_c, flow, direct, lanes):
     pair = pl.program_id(0)
 
     @pl.when(pair == 0)
     def _():
-        prepare(raw_ref, raw_t_ref, bias_ref, rate_ref, bias_t_ref, rate_t_ref, b_ref, c_ref,
-                pack, run_rows, step_rows, overlap)
+        prepare(raw_t_ref, bias_ref, rate_ref, bc_ref, turned, STATE,
+                raw, pack, run_rows, step_rows, overlap)
         for held in (d_overlap, d_b, d_c, flow, direct, lanes):
             held[...] = jnp.zeros_like(held)
 
@@ -250,7 +255,7 @@
             to_end = jnp.exp(end - run)
             d_hi, d_low = halves(d_state)
             from_state = to_end * folded(
-                dot(b_ref[rows, :], jnp.concatenate([d_hi, d_low], axis=1))
+                dot(bc_ref[rows, :STATE], jnp.concatenate([d_hi, d_low], axis=1))
             )
             fresh_hi, fresh_low = halves(driven * to_end)
             d_b[rows, :] += dot(
@@ -265,7 +270,7 @@
             lanes[c : c + 1, here] = crossing
             d_driven = d_driven + from_state
         if c > 0:
-            back = folded(dot(ct_ref[:, rows], entering))
+            back = folded(dot(turned[:, rows], entering))
             d_state = back if d_state is None else jnp.exp(end) * d_state + back
         flow[rows, :] += by_head(dy * scan - driven * d_driven)
         direct[rows, :] += by_head(x * d_driven)
@@ -278,7 +283,7 @@
         head = lax.broadcasted_iota(jnp.int32, (CHANNELS, LANES), 1)
         gather = jnp.where(channel == head, 1.0, 0.0).astype(BF16)
         heads = sum(dot(part.astype(BF16), gather) for part in three_parts(lanes[...]))
-        step_all, decay_all = steps_of(raw_ref, bias_ref, rate_ref)
+        step_all, decay_all = steps_of(raw, bias_ref, rate_ref)
         rate = jnp.exp(rate_ref[...])
         upper = jnp.where(triangle(False), 1.0, 0.0).astype(BF16)
         keep = lane < HEADS
@@ -289,19 +294,21 @@
             d_decay = sum(dot(upper, part.astype(BF16)) for part in three_parts(flow[rows, :]))
             d_decay = d_decay + heads[c : c + 1, :]
             d_step = direct[rows, :] - d_decay * rate
-            before = raw_ref[rows, :].astype(F32) + bias_ref[...]
+            before = raw[rows, :] + bias_ref[...]
             d_raw = jnp.where(keep, d_step / (1.0 + jnp.exp(-before)), 0.0)
-            step_ref[rows, :] = d_raw[:, :HEADS]
+            step_ref[:, rows] = d_raw.T[:HEADS, :]
             bias_sum = bias_sum + jnp.sum(d_raw, axis=0, keepdims=True)
             rate_sum = rate_sum + jnp.sum(
                 jnp.where(keep, d_decay * decay_all[rows], 0.0), axis=0, keepdims=True
             )
             d_hi, d_low = halves(jnp.where(triangle(True), d_overlap[c], 0.0))
             dc_ref[rows, :] = (
-                d_c[rows, :] + dot(d_hi, b_ref[rows, :]) + dot(d_low, b_ref[rows, :])
+                d_c[rows, :] + dot(d_hi, bc_ref[rows, :STATE]) + dot(d_low, bc_ref[rows, :STATE])
             ).astype(BF16)
             db_ref[rows, :] = (
-                d_b[rows, :] + dot(d_hi, c_ref[rows, :], (0, 0)) + dot(d_low, c_ref[rows, :], (0, 0))
+                d_b[rows, :]
+                + dot(d_hi, bc_ref[rows, STATE:], (0, 0))
+                + dot(d_low, bc_ref[rows, STATE:], (0, 0))
             ).astype(BF16)
         small_ref[...] = jnp.concatenate(
             [rate_sum, bias_sum, heads[CHUNKS : CHUNKS + 1, :], jnp.zeros((5, LANES), F32)], axis=0
@@ -319,35 +326,32 @@
 VMEM_LIMIT = 56 * 1024 * 1024
 
 TABLES = [
+    pltpu.VMEM((TOKENS, LANES), F32),
     pltpu.VMEM((TOKENS, LANES), BF16),
     pltpu.VMEM((PAIRS, 2, TOKENS), F32),
     pltpu.VMEM((PAIRS, 2, TOKENS), F32),
     pltpu.VMEM((CHUNKS, CHUNK, CHUNK), F32),
     pltpu.VMEM((TOKENS, 4 * LANES), F32),
+    pltpu.VMEM((STATE, TOKENS), BF16),
 ]
 
 PARAMETERS = [
-    whole((TOKENS, LANES)),
+    whole((TOKENS, 2 * STATE)),
     whole((HEADS, TOKENS)),
     whole((1, LANES)),
     whole((1, LANES)),
-    whole((HEADS, 1)),
-    whole((HEADS, 1)),
     whole((1, CHANNELS)),
     whole((1, CHANNELS)),
 ]
 
 
-def scan_forward(x, g, b, bt, c, parameters):
+def scan_forward(x, g, parameters):
     return pl.pallas_call(
         forward_kernel,
         grid=(PAIRS,),
         in_specs=[
             by_pair(TOKENS),
             by_pair(TOKENS),
-            whole((TOKENS, STATE)),
-            whole((STATE, TOKENS)),
-            whole((TOKENS, STATE)),
         ]
         + PARAMETERS,
         out_specs=[
@@ -368,10 +372,10 @@
         compiler_params=pltpu.CompilerParams(vmem_limit_bytes=VMEM_LIMIT),
         cost_estimate=pl.CostEstimate(flops=16 * 10**9, bytes_accessed=10**7, transcendentals=0),
         name="scan_forward",
-    )(x, g, b, bt, c, *parameters)
-
-
-def scan_backward(x, g, cot, scan, states, scale, pull, b, c, ct, parameters):
+    )(x, g, *parameters)
+
+
+def scan_backward(x, g, cot, scan, states, scale, pull, parameters):
     return pl.pallas_call(
         backward_kernel,
         grid=(PAIRS,),
@@ -383,9 +387,6 @@
             pl.BlockSpec((1, CHUNKS - 1, STATE, LANES), lambda p: (p, 0, 0, 0)),
             whole((TOKENS, LANES)),
             whole((TOKENS, LANES)),
-            whole((TOKENS, STATE)),
-            whole((TOKENS, STATE)),
-            whole((STATE, TOKENS)),
         ]
         + PARAMETERS,
         out_specs=[
@@ -393,7 +394,7 @@
             by_pair(TOKENS),
             whole((TOKENS, STATE)),
             whole((TOKENS, STATE)),
-            whole((TOKENS, HEADS)),
+            whole((HEADS, TOKENS)),
             whole((8, LANES)),
         ],
         out_shape=[
@@ -401,7 +402,7 @@
             jax.ShapeDtypeStruct((TOKENS, CHANNELS), BF16),
             jax.ShapeDtypeStruct((TOKENS, STATE), BF16),
             jax.ShapeDtypeStruct((TOKENS, STATE), BF16),
-            jax.ShapeDtypeStruct((TOKENS, HEADS), F32),
+            jax.ShapeDtypeStruct((HEADS, TOKENS), F32),
             jax.ShapeDtypeStruct((8, LANES), F32),
         ],
         scratch_shapes=TABLES
@@ -416,7 +417,7 @@
         compiler_params=pltpu.CompilerParams(vmem_limit_bytes=VMEM_LIMIT),
         cost_estimate=pl.CostEstimate(flops=20 * 10**9, bytes_accessed=10**7, transcendentals=0),
         name="scan_backward",
-    )(x, g, cot, scan, states, scale, pull, b, c, ct, *parameters)
+    )(x, g, cot, scan, states, scale, pull, *parameters)
 
 
 FEATURES = 512
@@ -506,6 +507,7 @@
         in_specs=[pl.BlockSpec((CHANNELS, BLOCK), lambda _: (1, 0)), whole((CHANNELS, BLOCK))],
         out_specs=whole((BLOCK, CHANNELS)),
         out_shape=jax.ShapeDtypeStruct((BLOCK, CHANNELS), F32),
+        cost_estimate=pl.CostEstimate(flops=4 * 10**9, bytes_accessed=10**6, transcendentals=0),
         name="finish",
     )(plane, given)
 
@@ -594,17 +596,15 @@
     return [(b, b ^ bit) for b in range(32)]
 
 
-def local_parameters(step_raw, log_rate, step_bias, skip_gain, norm_gain):
+def local_parameters(state_proj, step_raw, log_rate, step_bias, skip_gain, norm_gain):
     def padded(v):
         return jnp.pad(v, (0, LANES - HEADS)).reshape(1, LANES)
 
     return (
-        jnp.pad(step_raw, ((0, 0), (0, LANES - HEADS))),
+        state_proj.reshape(TOKENS, 2 * STATE),
         step_raw.T,
         padded(step_bias),
         padded(log_rate),
-        step_bias.reshape(HEADS, 1),
-        log_rate.reshape(HEADS, 1),
         jnp.repeat(skip_gain, WIDTH).reshape(1, CHANNELS),
         norm_gain.reshape(1, CHANNELS),
     )
@@ -636,11 +636,10 @@
     partner_before, partner_after = beside(partner)
     far_parts = beyond(before, after)
 
-    parameters = local_parameters(step_raw, log_rate, step_bias, skip_gain, norm_gain)
-    b, c = state_proj[:, 0, :], state_proj[:, 1, :]
-    low, scan, gated, states, scale = scan_forward(
-        scan_input, gate_input, b, b.T, c, parameters
-    )
+    parameters = local_parameters(
+        state_proj, step_raw, log_rate, step_bias, skip_gain, norm_gain
+    )
+    low, scan, gated, states, scale = scan_forward(scan_input, gate_input, parameters)
     partner_before, partner_after, far_parts, low = lax.optimization_barrier(
         (partner_before, partner_after, far_parts, low)
     )
@@ -673,20 +672,23 @@
         parameters[-1],
     )
     dx, dg, db, dc, step_grad, small = scan_backward(
-        scan_input, gate_input, cot, scan, states, scale, pull, b, c, c.T, parameters
+        scan_input, gate_input, cot, scan, states, scale, pull, parameters
     )
     summed = jnp.concatenate([small, gain_grad.reshape(8, LANES)], axis=0)
-    for bit in (1, 4, 8, 16):
+    for bit in (1, 4, 8):
         summed = summed + lax.ppermute(summed, "blk", swap(bit))
-    plane, summed = lax.optimization_barrier((plane, summed))
+    state_grad = jnp.stack([db, dc], axis=1)
+    plane, summed, state_grad = lax.optimization_barrier((plane, summed, state_grad))
     given = lax.ppermute(plane[:CHANNELS], "blk", swap(2))
+    summed = summed + lax.ppermute(summed, "blk", swap(16))
+    given, summed = lax.optimization_barrier((given, summed))
     weight_grad = finish(plane, given, norm_scale)
     summed = (summed + lax.ppermute(summed, "blk", swap(2))) * norm_scale
     return (
         dx,
         dg,
-        jnp.stack([db, dc], axis=1),
-        step_grad,
+        state_grad,
+        step_grad.T,
         weight_grad,
         summed[0, :HEADS],
         summed[1, :HEADS],

time: 158 us -> 152 us (0.962)
  local copies, waits for them, and re-layouts: 21.9 us -> 12.4 us
  waiting for transfers between devices: 33.6 us -> 35.5 us
    ppermute x4 -> x3, waiting for transfers between devices: 10.7 us -> 5.29 us  [shards(): summed = summed + lax.ppermute(summed, 'blk', swap(bit))]
    ppermute x1, waiting for transfers between devices: 0.01 us -> 5.03 us  [shards(): partner = lax.ppermute(own, 'tp', [(t, t ^ 1) for t in range(8)])]
    ppermute x1, waiting for transfers between devices: 4.6 us -> 0.01 us  [shards(): given = lax.ppermute(plane[:CHANNELS], 'blk', swap(2))]
    ppermute x4 -> x3, starting transfers between devices: 7.02 us -> 3.34 us  [shards(): summed = summed + lax.ppermute(summed, 'blk', swap(bit))]
    ppermute x0 -> x1, starting transfers between devices: none -> 3.38 us  [shards(): summed = summed + lax.ppermute(summed, 'blk', swap(16))]
    ppermute x0 -> x1, waiting for transfers between devices: none -> 2.84 us  [shards(): summed = summed + lax.ppermute(summed, 'blk', swap(16))]
    reshape x2 -> x0, local copies, waits for them, and re-layouts: 2.65 us -> none  [the longest x1 1.33 us: local_parameters(): step_bias.reshape(HEADS, 1)]
    unnamed x28 -> x24, local copies, waits for them, and re-layouts: 8.32 us -> 5.7 us
  transfers between devices with their start and end apart: 19 -> 19, of which waited for: 11 -> 13; matrix products, arithmetic and copies ran while one was open for 14% -> 7% of each run, Pallas kernels for 38% -> 42%
where the time goes in v4:
time: 152 us; the launch traced here: 151 us
  Pallas kernels  62.8 us (41%)
  waiting for transfers between devices  35.5 us (23%)
  starting transfers between devices  21.4 us (14%)
  between operations  15.7 us (10%)
  local copies, waits for them, and re-layouts  12.4 us (8%)
  other arithmetic  3.12 us (2%)
    pallas_call x1, Pallas kernels, scan_backward(): pl.pallas_call(backward_kernel, grid=(PAIRS,), in_specs=[by_pair(TOKENS),...  18.5 us
    pallas_call x3, Pallas kernels, terms(): pl.pallas_call(kernel, grid_spec=pltpu.PrefetchScalarGridSpec(num_scalar_...  17 us
    pallas_call x1, Pallas kernels, scan_forward(): pl.pallas_call(forward_kernel, grid=(PAIRS,), in_specs=[by_pair(TOKENS),...  13.8 us
    all_gather x1, waiting for transfers between devices, shards(): rows = lax.all_gather(out_proj, 'blk', axis=0, tiled=True)  12.9 us
    pallas_call x1, Pallas kernels, products(): pl.pallas_call(product_kernel, grid_spec=pltpu.PrefetchScalarGridSpec(num...  11.5 us
    unnamed x24, local copies, waits for them, and re-layouts  5.7 us
    ppermute x3, waiting for transfers between devices, shards(): summed = summed + lax.ppermute(summed, 'blk', swap(bit))  5.29 us
    ppermute x1, waiting for transfers between devices, shards(): partner = lax.ppermute(own, 'tp', [(t, t ^ 1) for t in range(8)])  5.03 us
  transfers between devices with their start and end apart: 19, of which 13 were waited for; matrix products, arithmetic and copies ran while one was open for 7% of the time, Pallas kernels for 42%

profile of v4, /device:TPU:6, one launch (start us, length us, event | category | flops | bytes accessed | tf_op | source)
XLA Modules:
  0.0 150.9 jit_solution(3605519396456208053)
XLA Ops:
  8.1 0.7 all-gather.2.cloned.1.call-update
  8.8 3.3 %collective-permute-start = (bf16[512,512]{1,0:T(8,128)(2,1)}, bf16[512,512]{1,0:T(8,128)(2,1)S(1)}, u32[]{:S(2)}, u32[]{:S(2)}) collective-permute-start(bf16[512,512]{1,0:T(8,128)(2,1)} %refs_0_.1), channel_id=1, source_target_pairs={{0,1},{1,0},{2,3},{3,2},{4,5},{5,4},{6,7},{7,6},{8,9},{9,8},{10,11... | collective-permute-start | bytes 1572872 | tf_op jit(solution)/shard_map/ppermute | solution.py:631
  12.6 1.5 %collective-permute-start.2 = (bf16[512,512]{1,0:T(8,128)(2,1)}, bf16[512,512]{1,0:T(8,128)(2,1)S(1)}, u32[]{:S(2)}, u32[]{:S(2)}) collective-permute-start(bf16[512,512]{1,0:T(8,128)(2,1)} %refs_0_.1), channel_id=1, source_target_pairs={{0,6},{1,7},{2,0},{3,1},{4,2},{5,3},{6,4},{7,5},{8,14},{9,15},{10,... | collective-permute-start | bytes 1572872 | tf_op jit(solution)/shard_map/ppermute | solution.py:585
  14.1 1.9 %copy.20 = bf16[64,8,2,256]{3,1,2,0:T(8,128)(2,1)} copy(bf16[64,8,2,256]{3,2,1,0:T(2,128)(2,1)} %bitcast.32) | data formatting | bytes 1048576
  16.0 0.7 broadcast_in_dim.3
  16.7 0.7 reshape_reshape.3.skip_ref
  17.4 0.6 stack.86.refs_0_
  18.0 1.2 pad_bitcast_fusion
  19.2 5.0 %collective-permute-done.refs_9_.refs_10_.refs_4_ = bf16[512,512]{1,0:T(8,128)(2,1)S(1)} collective-permute-done((bf16[512,512]{1,0:T(8,128)(2,1)}, bf16[512,512]{1,0:T(8,128)(2,1)S(1)}, u32[]{:S(2)}, u32[]{:S(2)}) %collective-permute-start) | collective-permute-done | bytes 524320 | tf_op jit(solution)/shard_map/ppermute | solution.py:631
  24.3 1.4 collective-permute-done.1.refs_3_.refs_4_.refs_1_
  25.7 1.4 collective-permute-done.2.refs_5_.refs_6_.refs_2_
  27.4 1.7 %collective-permute-start.4 = (bf16[512,512]{1,0:T(8,128)(2,1)S(1)}, bf16[512,512]{1,0:T(8,128)(2,1)S(1)}, u32[]{:S(2)}, u32[]{:S(2)}) collective-permute-start(bf16[512,512]{1,0:T(8,128)(2,1)S(1)} %collective-permute-done.refs_9_.refs_10_.refs_4_), channel_id=1, source_target_pairs={{0,6},{1,7},{2,0},{3,1},{4,2},{5,3},{6,4},{7,5},{8,14},{9,15},{10,... | collective-permute-start | bytes 1572872 | tf_op jit(solution)/shard_map/ppermute | solution.py:585
  29.1 1.6 %collective-permute-start.5 = (bf16[256,512]{1,0:T(8,128)(2,1)S(1)}, bf16[256,512]{1,0:T(8,128)(2,1)S(1)}, u32[]{:S(2)}, u32[]{:S(2)}) collective-permute-start(bf16[256,512]{1,0:T(8,128)(2,1)S(1)} %slice.27), channel_id=1, source_target_pairs={{0,2},{1,3},{2,4},{3,5},{4,6},{5,7},{6,0},{7,1},{8,10},{9,11},{10,... | collective-permute-start | bytes 786440 | tf_op jit(solution)/shard_map/ppermute | solution.py:590
  31.3 13.8 %scan_forward.1 = (bf16[1024,512]{1,0:T(8,128)(2,1)}, f32[512,1024]{1,0:T(8,128)}, f32[512,1024]{1,0:T(8,128)}, f32[8,3,256,128]{3,2,1,0:T(8,128)}, f32[512,128]{1,0:T(8,128)}) custom-call(bf16[512,1024]{1,0:T(8,128)(2,1)} %x_ref.1, bf16[512,1024]{1,0:T(8,128)(2,1)} %g_ref.3, bf16[512,512]{1,0:T(8,128)(2,1)} %bitcast.33, bf16[16,512]{1,0:T(8,128)(2,1)} %bitcast.39, ...), custom_call_target="tpu_custom_call" | custom-call | flops 16000000000 | bytes 10000000 | tf_op jit(solution)/shard_map/scan_forward/pallas_call | solution.py:349
  45.2 1.3 collective-permute-done.6
  46.5 1.6 %collective-permute-start.7 = (bf16[256,512]{1,0:T(8,128)(2,1)S(1)}, bf16[256,512]{1,0:T(8,128)(2,1)S(1)}, u32[]{:S(2)}, u32[]{:S(2)}) collective-permute-start(bf16[256,512]{1,0:T(8,128)(2,1)S(1)} %slice.29), channel_id=1, source_target_pairs={{0,2},{1,3},{2,4},{3,5},{4,6},{5,7},{6,0},{7,1},{8,10},{9,11},{10,... | collective-permute-start | bytes 786440 | tf_op jit(solution)/shard_map/ppermute | solution.py:590
  48.1 0.6 collective-permute-start.8
  48.8 0.8 copy-done.4
  49.6 6.0 %terms.2 = bf16[14336,128]{1,0:T(8,128)(2,1)} custom-call(s32[9]{0:T(128)} %stack.86.refs_0_, bf16[512,512]{1,0:T(8,128)(2,1)} %refs_0_.1, bf16[512,512]{1,0:T(8,128)(2,1)} %refs_0_.1, bf16[512,512]{1,0:T(8,128)(2,1)} %copy-done, bf16[512,512]{1,0:T(8,128)(2,1)} %copy-done, bf16[512,512]{1,0:T(8,128)(2,1)} %copy-done.1, bf16[512,512]{1,0:T(8,128)(2,1)} %copy-done.1, ...), custom_call_target="tpu_custom_call" | custom-call | flops 5600000000 | bytes 2000000 | tf_op jit(solution)/shard_map/terms/pallas_call | solution.py:472
  55.9 0.7 pad_add_fusion.refs_0_
  56.6 0.8 copy-done.5
  57.4 3.3 %terms.3 = bf16[2048,128]{1,0:T(8,128)(2,1)} custom-call(s32[3]{0:T(128)} %pad_add_fusion.refs_0_, bf16[512,512]{1,0:T(8,128)(2,1)} %copy-done.5, bf16[512,512]{1,0:T(8,128)(2,1)} %copy-done.5, bf16[1024,512]{1,0:T(8,128)(2,1)} %get-tuple-element.50.refs_15_.refs_3_.refs_17_), custom_call_target="tpu_custom_call" | custom-call | flops 1400000000 | bytes 2000000 | tf_op jit(solution)/shard_map/terms/pallas_call | solution.py:472
  61.3 0.7 stack.89.refs_0_
  62.0 2.1 %collective-permute-done.10.refs_19_ = bf16[2048,128]{1,0:T(8,128)(2,1)S(1)} collective-permute-done((bf16[2048,128]{1,0:T(8,128)(2,1)}, bf16[2048,128]{1,0:T(8,128)(2,1)S(1)}, u32[]{:S(2)}, u32[]{:S(2)}) %collective-permute-start.10) | collective-permute-done | bytes 524320 | tf_op jit(solution)/shard_map/ppermute | solution.py:660
  64.1 0.8 copy-done.8
  64.9 7.7 %terms_added.1 = bf16[16384,128]{1,0:T(8,128)(2,1)} custom-call(s32[10]{0:T(128)} %stack.89.refs_0_, bf16[512,512]{1,0:T(8,128)(2,1)} %refs_0_.1, bf16[512,512]{1,0:T(8,128)(2,1)} %refs_0_.1, bf16[512,512]{1,0:T(8,128)(2,1)} %copy-done, bf16[512,512]{1,0:T(8,128)(2,1)} %copy-done, bf16[512,512]{1,0:T(8,128)(2,1)} %copy-done.1, bf16[512,512]{1,0:T(8,128)(2,1)} %copy-done.1, ...), custom_call_target="tpu_custom_call" | custom-call | flops 6300000256 | bytes 2000000 | tf_op jit(solution)/shard_map/terms_added/pallas_call | solution.py:472
  72.6 0.6 stack.83.places
  73.2 12.9 %all-gather.2.cloned.1.call-done.refs_8_ = bf16[4096,1024]{1,0:T(8,128)(2,1)} async-done(((bf16[128,1024]{1,0:T(8,128)(2,1)}), bf16[4096,1024]{1,0:T(8,128)(2,1)}) %all-gather.2.cloned.1.call-update) | async-done | bytes 8388624 | tf_op jit(solution)/shard_map/all_gather | solution.py:629
  86.1 11.5 %products.1 = (f32[512,1024]{1,0:T(8,128)}, f32[1,1024]{1,0:T(1,128)}, f32[512,128]{1,0:T(8,128)}) custom-call(s32[8]{0:T(128)} %stack.83.places, bf16[512,512]{1,0:T(8,128)(2,1)} %refs_0_.1, bf16[512,512]{1,0:T(8,128)(2,1)} %copy-done, bf16[512,512]{1,0:T(8,128)(2,1)} %copy-done.1, bf16[512,512]{1,0:T(8,128)(2,1)} %copy-done.4, bf16[512,512]{1,0:T(8,128)(2,1)} %copy-done.7, ...), custom_call_target="tpu_custom_call" | custom-call | flops 12000000000 | bytes 16000000 | tf_op jit(solution)/shard_map/products/pallas_call | solution.py:548
  97.6 18.5 %scan_backward.1 = (bf16[512,1024]{1,0:T(8,128)(2,1)}, bf16[512,1024]{1,0:T(8,128)(2,1)}, bf16[512,256]{1,0:T(8,128)(2,1)}, bf16[512,256]{1,0:T(8,128)(2,1)}, f32[16,512]{1,0:T(8,128)}, /*index=5*/f32[8,128]{1,0:T(8,128)}) custom-call(bf16[512,1024]{1,0:T(8,128)(2,1)} %x_ref.1, bf16[512,1024]{1,0:T(8,128)(2,1)} %g_ref.3, ...), custom_call_target="tpu_custom_call" | custom-call | flops 20000000000 | bytes 10000000 | tf_op jit(solution)/shard_map/scan_backward/pallas_call | solution.py:379
  116.1 0.7 pad_maximum_fusion.1
  117.0 0.9 collective-permute-done.11
  117.9 0.7 fusion
  118.6 1.2 collective-permute-start.12
  119.8 2.8 %collective-permute-done.12 = f32[16,128]{1,0:T(8,128)S(1)} collective-permute-done((f32[16,128]{1,0:T(8,128)S(1)}, f32[16,128]{1,0:T(8,128)S(1)}, u32[]{:S(2)}, u32[]{:S(2)}) %collective-permute-start.12) | collective-permute-done | bytes 8224 | tf_op jit(solution)/shard_map/ppermute | solution.py:679
  122.6 1.9 %collective-permute-start.13 = (f32[16,128]{1,0:T(8,128)S(1)}, f32[16,128]{1,0:T(8,128)S(1)}, u32[]{:S(2)}, u32[]{:S(2)}) collective-permute-start(f32[16,128]{1,0:T(8,128)S(1)} %add.120), channel_id=1, source_target_pairs={{0,64},{8,72},{16,80},{24,88},{32,96},{40,104},{48,112},{56,120},{... | collective-permute-start | bytes 24584 | tf_op jit(solution)/shard_map/ppermute | solution.py:679
  124.5 1.1 pad_maximum_fusion
  125.6 1.6 %collective-permute-done.13 = f32[16,128]{1,0:T(8,128)S(1)} collective-permute-done((f32[16,128]{1,0:T(8,128)S(1)}, f32[16,128]{1,0:T(8,128)S(1)}, u32[]{:S(2)}, u32[]{:S(2)}) %collective-permute-start.13) | collective-permute-done | bytes 8224 | tf_op jit(solution)/shard_map/ppermute | solution.py:679
  127.2 1.3 reduce-scatter.2.cloned.1.call-done.refs_0_
  128.5 1.0 slice.31
  129.5 1.6 %collective-permute-start.14 = (bf16[1024,128]{1,0:T(8,128)(2,1)S(1)}, bf16[1024,128]{1,0:T(8,128)(2,1)S(1)}, u32[]{:S(2)}, u32[]{:S(2)}) collective-permute-start(bf16[1024,128]{1,0:T(8,128)(2,1)S(1)} %slice.31), channel_id=1, source_target_pairs={{0,16},{8,24},{16,0},{24,8},{32,48},{40,56},{48,32},{56,40},{64,80... | collective-permute-start | bytes 786440 | tf_op jit(solution)/shard_map/ppermute | solution.py:682
  131.0 3.4 %collective-permute-start.15 = (f32[16,128]{1,0:T(8,128)S(1)}, f32[16,128]{1,0:T(8,128)S(1)}, u32[]{:S(2)}, u32[]{:S(2)}) collective-permute-start(f32[16,128]{1,0:T(8,128)S(1)} %add.121), channel_id=1, source_target_pairs={{0,128},{8,136},{16,144},{24,152},{32,160},{40,168},{48,176},{56,1... | collective-permute-start | bytes 24584 | tf_op jit(solution)/shard_map/ppermute | solution.py:683
  134.4 1.3 copy.19
  135.7 2.8 %collective-permute-done.15 = f32[16,128]{1,0:T(8,128)S(1)} collective-permute-done((f32[16,128]{1,0:T(8,128)S(1)}, f32[16,128]{1,0:T(8,128)S(1)}, u32[]{:S(2)}, u32[]{:S(2)}) %collective-permute-start.15) | collective-permute-done | bytes 8224 | tf_op jit(solution)/shard_map/ppermute | solution.py:683
  138.6 0.6 collective-permute-start.16
  139.3 2.0 %finish.1 = f32[128,1024]{1,0:T(8,128)} custom-call(bf16[2048,128]{1,0:T(8,128)(2,1)} %reduce-scatter.2.cloned.1.call-done.refs_0_, bf16[1024,128]{1,0:T(8,128)(2,1)} %copy-done.9), custom_call_target="tpu_custom_call" | custom-call | flops 4000000000 | bytes 1000000 | tf_op jit(solution)/shard_map/finish/pallas_call | solution.py:504
  141.3 1.0 collective-permute-done.16
  142.3 0.6 slice_bitcast_fusion
  (46 shorter events, 3.4 us)
Async XLA Ops:
  8.0 78.1 %all-gather.2.cloned.1.call-start = ((), (), s32[]{:S(2)}) async-start(), calls=%async_computation.1 | async-start | bytes 8650752 | tf_op jit(solution)/shard_map/all_gather | solution.py:629
  8.7 119.7 %reduce-scatter.2.cloned.1.call-start = ((), (), s32[]{:S(2)}) async-start(), calls=%async_computation.2 | async-start | bytes 4718592 | tf_op jit(solution)/shard_map/reduce_scatter | solution.py:662
  8.8 15.5 %collective-permute-start = (bf16[512,512]{1,0:T(8,128)(2,1)}, bf16[512,512]{1,0:T(8,128)(2,1)S(1)}, u32[]{:S(2)}, u32[]{:S(2)}) collective-permute-start(bf16[512,512]{1,0:T(8,128)(2,1)} %refs_0_.1), channel_id=1, source_target_pairs={{0,1},{1,0},{2,3},{3,2},{4,5},{5,4},{6,7},{7,6},{8,9},{9,8},{10,11... | collective-permute-start | bytes 1572872 | tf_op jit(solution)/shard_map/ppermute | solution.py:631
  12.1 13.6 %collective-permute-start.1 = (bf16[512,512]{1,0:T(8,128)(2,1)}, bf16[512,512]{1,0:T(8,128)(2,1)S(1)}, u32[]{:S(2)}, u32[]{:S(2)}) collective-permute-start(bf16[512,512]{1,0:T(8,128)(2,1)} %refs_0_.1), channel_id=1, source_target_pairs={{0,2},{1,3},{2,4},{3,5},{4,6},{5,7},{6,0},{7,1},{8,10},{9,11},{10,... | collective-permute-start | bytes 1572872 | tf_op jit(solution)/shard_map/ppermute | solution.py:585
  12.6 14.5 %collective-permute-start.2 = (bf16[512,512]{1,0:T(8,128)(2,1)}, bf16[512,512]{1,0:T(8,128)(2,1)S(1)}, u32[]{:S(2)}, u32[]{:S(2)}) collective-permute-start(bf16[512,512]{1,0:T(8,128)(2,1)} %refs_0_.1), channel_id=1, source_target_pairs={{0,6},{1,7},{2,0},{3,1},{4,2},{5,3},{6,4},{7,5},{8,14},{9,15},{10,... | collective-permute-start | bytes 1572872 | tf_op jit(solution)/shard_map/ppermute | solution.py:585
  24.3 20.9 %copy-start.7 = (bf16[512,512]{1,0:T(8,128)(2,1)}, bf16[512,512]{1,0:T(8,128)(2,1)S(1)}, u32[]{:S(2)}) copy-start(bf16[512,512]{1,0:T(8,128)(2,1)S(1)} %collective-permute-done.refs_9_.refs_10_.refs_4_) | copy-start | bytes 1572868
  25.7 19.5 %copy-start = (bf16[512,512]{1,0:T(8,128)(2,1)}, bf16[512,512]{1,0:T(8,128)(2,1)S(1)}, u32[]{:S(2)}) copy-start(bf16[512,512]{1,0:T(8,128)(2,1)S(1)} %collective-permute-done.1.refs_3_.refs_4_.refs_1_) | copy-start | bytes 1572868
  27.1 18.1 %copy-start.1 = (bf16[512,512]{1,0:T(8,128)(2,1)}, bf16[512,512]{1,0:T(8,128)(2,1)S(1)}, u32[]{:S(2)}) copy-start(bf16[512,512]{1,0:T(8,128)(2,1)S(1)} %collective-permute-done.2.refs_5_.refs_6_.refs_2_) | copy-start | bytes 1572868
  27.1 19.4 %collective-permute-start.3 = (bf16[512,512]{1,0:T(8,128)(2,1)S(1)}, bf16[512,512]{1,0:T(8,128)(2,1)S(1)}, u32[]{:S(2)}, u32[]{:S(2)}) collective-permute-start(bf16[512,512]{1,0:T(8,128)(2,1)S(1)} %collective-permute-done.refs_9_.refs_10_.refs_4_), channel_id=1, source_target_pairs={{0,2},{1,3},{2,4},{3,5},{4,6},{5,7},{6,0},{7,1},{8,10},{9,11},{10,... | collective-permute-start | bytes 1572872 | tf_op jit(solution)/shard_map/ppermute | solution.py:585
  27.4 19.0 %collective-permute-start.4 = (bf16[512,512]{1,0:T(8,128)(2,1)S(1)}, bf16[512,512]{1,0:T(8,128)(2,1)S(1)}, u32[]{:S(2)}, u32[]{:S(2)}) collective-permute-start(bf16[512,512]{1,0:T(8,128)(2,1)S(1)} %collective-permute-done.refs_9_.refs_10_.refs_4_), channel_id=1, source_target_pairs={{0,6},{1,7},{2,0},{3,1},{4,2},{5,3},{6,4},{7,5},{8,14},{9,15},{10,... | collective-permute-start | bytes 1572872 | tf_op jit(solution)/shard_map/ppermute | solution.py:585
  29.1 16.0 %collective-permute-start.5 = (bf16[256,512]{1,0:T(8,128)(2,1)S(1)}, bf16[256,512]{1,0:T(8,128)(2,1)S(1)}, u32[]{:S(2)}, u32[]{:S(2)}) collective-permute-start(bf16[256,512]{1,0:T(8,128)(2,1)S(1)} %slice.27), channel_id=1, source_target_pairs={{0,2},{1,3},{2,4},{3,5},{4,6},{5,7},{6,0},{7,1},{8,10},{9,11},{10,... | collective-permute-start | bytes 786440 | tf_op jit(solution)/shard_map/ppermute | solution.py:590
  30.8 15.7 %collective-permute-start.6 = (bf16[256,512]{1,0:T(8,128)(2,1)S(1)}, bf16[256,512]{1,0:T(8,128)(2,1)S(1)}, u32[]{:S(2)}, u32[]{:S(2)}) collective-permute-start(bf16[256,512]{1,0:T(8,128)(2,1)S(1)} %slice.28), channel_id=1, source_target_pairs={{0,6},{1,7},{2,0},{3,1},{4,2},{5,3},{6,4},{7,5},{8,14},{9,15},{10,... | collective-permute-start | bytes 786440 | tf_op jit(solution)/shard_map/ppermute | solution.py:591
  46.5 2.3 %copy-start.2 = (bf16[512,512]{1,0:T(8,128)(2,1)}, bf16[512,512]{1,0:T(8,128)(2,1)S(1)}, u32[]{:S(2)}) copy-start(bf16[512,512]{1,0:T(8,128)(2,1)S(1)} %collective-permute-done.3.refs_11_.refs_12_.refs_5_) | copy-start | bytes 1572868
  46.5 2.3 %copy-start.3 = (bf16[512,512]{1,0:T(8,128)(2,1)}, bf16[512,512]{1,0:T(8,128)(2,1)S(1)}, u32[]{:S(2)}) copy-start(bf16[512,512]{1,0:T(8,128)(2,1)S(1)} %collective-permute-done.4.refs_13_.refs_14_.refs_6_) | copy-start | bytes 1572868
  46.5 9.1 %collective-permute-start.7 = (bf16[256,512]{1,0:T(8,128)(2,1)S(1)}, bf16[256,512]{1,0:T(8,128)(2,1)S(1)}, u32[]{:S(2)}, u32[]{:S(2)}) collective-permute-start(bf16[256,512]{1,0:T(8,128)(2,1)S(1)} %slice.29), channel_id=1, source_target_pairs={{0,2},{1,3},{2,4},{3,5},{4,6},{5,7},{6,0},{7,1},{8,10},{9,11},{10,... | collective-permute-start | bytes 786440 | tf_op jit(solution)/shard_map/ppermute | solution.py:590
  48.1 7.7 %collective-permute-start.8 = (bf16[256,512]{1,0:T(8,128)(2,1)S(1)}, bf16[256,512]{1,0:T(8,128)(2,1)S(1)}, u32[]{:S(2)}, u32[]{:S(2)}) collective-permute-start(bf16[256,512]{1,0:T(8,128)(2,1)S(1)} %slice.30), channel_id=1, source_target_pairs={{0,6},{1,7},{2,0},{3,1},{4,2},{5,3},{6,4},{7,5},{8,14},{9,15},{10,... | collective-permute-start | bytes 786440 | tf_op jit(solution)/shard_map/ppermute | solution.py:591
  48.8 0.8 copy-start.4
  55.8 8.3 %collective-permute-start.9 = (bf16[14336,128]{1,0:T(8,128)(2,1)}, bf16[14336,128]{1,0:T(8,128)(2,1)}, u32[]{:S(2)}, u32[]{:S(2)}) collective-permute-start(bf16[14336,128]{1,0:T(8,128)(2,1)} %terms.2), channel_id=1, source_target_pairs={{0,8},{8,0},{16,24},{24,16},{32,40},{40,32},{48,56},{56,48},{64,72... | collective-permute-start | bytes 11010056 | tf_op jit(solution)/shard_map/ppermute | solution.py:658
  56.6 0.8 copy-start.5
  60.7 3.3 %collective-permute-start.10 = (bf16[2048,128]{1,0:T(8,128)(2,1)}, bf16[2048,128]{1,0:T(8,128)(2,1)S(1)}, u32[]{:S(2)}, u32[]{:S(2)}) collective-permute-start(bf16[2048,128]{1,0:T(8,128)(2,1)} %terms.3), channel_id=1, source_target_pairs={{0,8},{8,0},{16,24},{24,16},{32,40},{40,32},{48,56},{56,48},{64,72... | collective-permute-start | bytes 1572872 | tf_op jit(solution)/shard_map/ppermute | solution.py:660
  64.1 0.8 copy-start.8
  97.6 18.5 %copy-start.6 = (f32[1,1024]{1,0:T(1,128)S(1)}, f32[1,1024]{1,0:T(1,128)}, u32[]{:S(2)}) copy-start(f32[1,1024]{1,0:T(1,128)} %get-tuple-element.64) | copy-start | bytes 12292
  116.8 1.2 collective-permute-start.11
  118.6 4.0 %collective-permute-start.12 = (f32[16,128]{1,0:T(8,128)S(1)}, f32[16,128]{1,0:T(8,128)S(1)}, u32[]{:S(2)}, u32[]{:S(2)}) collective-permute-start(f32[16,128]{1,0:T(8,128)S(1)} %fusion), channel_id=1, source_target_pairs={{0,32},{8,40},{16,48},{24,56},{32,0},{40,8},{48,16},{56,24},{64,96... | collective-permute-start | bytes 24584 | tf_op jit(solution)/shard_map/ppermute | solution.py:679
  122.6 4.5 %collective-permute-start.13 = (f32[16,128]{1,0:T(8,128)S(1)}, f32[16,128]{1,0:T(8,128)S(1)}, u32[]{:S(2)}, u32[]{:S(2)}) collective-permute-start(f32[16,128]{1,0:T(8,128)S(1)} %add.120), channel_id=1, source_target_pairs={{0,64},{8,72},{16,80},{24,88},{32,96},{40,104},{48,112},{56,120},{... | collective-permute-start | bytes 24584 | tf_op jit(solution)/shard_map/ppermute | solution.py:679
  129.5 9.1 %collective-permute-start.14 = (bf16[1024,128]{1,0:T(8,128)(2,1)S(1)}, bf16[1024,128]{1,0:T(8,128)(2,1)S(1)}, u32[]{:S(2)}, u32[]{:S(2)}) collective-permute-start(bf16[1024,128]{1,0:T(8,128)(2,1)S(1)} %slice.31), channel_id=1, source_target_pairs={{0,16},{8,24},{16,0},{24,8},{32,48},{40,56},{48,32},{56,40},{64,80... | collective-permute-start | bytes 786440 | tf_op jit(solution)/shard_map/ppermute | solution.py:682
  131.0 7.6 %collective-permute-start.15 = (f32[16,128]{1,0:T(8,128)S(1)}, f32[16,128]{1,0:T(8,128)S(1)}, u32[]{:S(2)}, u32[]{:S(2)}) collective-permute-start(f32[16,128]{1,0:T(8,128)S(1)} %add.121), channel_id=1, source_target_pairs={{0,128},{8,136},{16,144},{24,152},{32,160},{40,168},{48,176},{56,1... | collective-permute-start | bytes 24584 | tf_op jit(solution)/shard_map/ppermute | solution.py:683
  138.6 0.7 copy-start.9
  138.6 3.7 %collective-permute-start.16 = (f32[16,128]{1,0:T(8,128)S(1)}, f32[16,128]{1,0:T(8,128)S(1)}, u32[]{:S(2)}, u32[]{:S(2)}) collective-permute-start(f32[16,128]{1,0:T(8,128)S(1)} %add.122), channel_id=1, source_target_pairs={{0,16},{8,24},{16,0},{24,8},{32,48},{40,56},{48,32},{56,40},{64,80... | collective-permute-start | bytes 24584 | tf_op jit(solution)/shard_map/ppermute | solution.py:686
Sparse Core Ops, SparseCore 0:
  10.7 75.3 all-gather.1
Sparse Core Ops, SparseCore 1:
  72.7 55.8 reduce-scatter.1

commit v5 on v4

--- a/solution.py
+++ b/solution.py
@@ -427,22 +427,31 @@
 
 def term_kernel(count, added, placed, places, *refs):
     pieces, low_ref = refs[: 2 * count], refs[2 * count]
-    sent_refs = refs[2 * count + 1 : -3]
-    out_ref, held, done = refs[-3:]
     per = 2 * CHANNELS
-    sent = [
-        ref.at[start : start + per] for ref in sent_refs for start in range(0, ref.shape[0], per)
-    ]
-    copies = []
+    copies, arrivals = [], []
+    if added:
+        out_ref, held, done, sent, come = refs[-5:]
+        parts = [
+            ref.at[start : start + per]
+            for ref in refs[2 * count + 1 : -5]
+            for start in range(0, ref.shape[0], per)
+        ]
+        for k, part in enumerate(parts):
+            arrivals.append(pltpu.make_async_copy(part, sent.at[k], come.at[k]))
+            arrivals[-1].start()
+    else:
+        out_ref, held, done = refs[-3:]
     for k in range(count):
         blocks = [piece[...] for piece in pieces[2 * k : 2 * k + 2]]
         term = dot(low_ref[...], jnp.concatenate(blocks, axis=1))
+        if added:
+            arrivals[k].wait()
         for slot in range(2):
             n = 2 * k + slot
             here = slice(n * CHANNELS, (n + 1) * CHANNELS)
             part = term[:, slot * BLOCK : (slot + 1) * BLOCK]
             if added:
-                part = part + sent[k][slot * CHANNELS : (slot + 1) * CHANNELS, :].astype(F32)
+                part = part + sent[k, slot * CHANNELS : (slot + 1) * CHANNELS, :].astype(F32)
             held[here, :] = part.astype(BF16)
             start = n * CHANNELS
             if placed:
@@ -461,7 +470,16 @@
     count = len(pieces)
     added = len(sent) > 0
     rows = 2 * CHANNELS * count
-    specs = [whole(part.shape) for part in sent]
+    specs = [pl.BlockSpec(memory_space=pl.ANY) for _ in sent]
+    scratch = [
+        pltpu.VMEM((2 * count * CHANNELS, BLOCK), BF16),
+        pltpu.SemaphoreType.DMA((2 * count,)),
+    ]
+    if added:
+        scratch += [
+            pltpu.VMEM((count, 2 * CHANNELS, BLOCK), BF16),
+            pltpu.SemaphoreType.DMA((count,)),
+        ]
 
     def kernel(*refs):
         term_kernel(count, added, added, *refs)
@@ -476,10 +494,7 @@
             grid=(1,),
             in_specs=[lanes(0), lanes(1)] * count + [whole((CHANNELS, TOKENS))] + specs,
             out_specs=pl.BlockSpec(memory_space=pl.ANY),
-            scratch_shapes=[
-                pltpu.VMEM((2 * count * CHANNELS, BLOCK), BF16),
-                pltpu.SemaphoreType.DMA((2 * count,)),
-            ],
+            scratch_shapes=scratch,
         ),
         out_shape=jax.ShapeDtypeStruct((rows, BLOCK), BF16),
         compiler_params=pltpu.CompilerParams(vmem_limit_bytes=VMEM_LIMIT),

time: 152 us -> 154 us (1.013)
  Pallas kernels: 62.8 us -> 65.9 us
    all_gather x1, waiting for transfers between devices: 12.9 us -> 10.1 us  [shards(): rows = lax.all_gather(out_proj, 'blk', axis=0, tiled=True)]
    pallas_call x3, Pallas kernels: 17 us -> 19.9 us  [terms(): pl.pallas_call(kernel, grid_spec=pltpu.PrefetchScalarGridSpec(num_scalar_...]
    reduce_scatter x1, waiting for transfers between devices: 1.32 us -> 3.49 us  [shards(): lax.psum_scatter(both, 'blk', scatter_dimension=0, tiled=True, axis_index...]
  transfers between devices with their start and end apart: 19 -> 19, of which waited for: 13 -> 13; matrix products, arithmetic and copies ran while one was open for 7% -> 7% of each run, Pallas kernels for 42% -> 43%
where the time goes in v5:
time: 154 us
  Pallas kernels  65.9 us (43%)
  waiting for transfers between devices  34.7 us (23%)
  starting transfers between devices  21.8 us (14%)
  between operations  15.7 us (10%)
  local copies, waits for them, and re-layouts  12.4 us (8%)
  other arithmetic  3.12 us (2%)
    pallas_call x3, Pallas kernels, terms(): pl.pallas_call(kernel, grid_spec=pltpu.PrefetchScalarGridSpec(num_scalar_...  19.9 us
    pallas_call x1, Pallas kernels, scan_backward(): pl.pallas_call(backward_kernel, grid=(PAIRS,), in_specs=[by_pair(TOKENS),...  18.5 us
    pallas_call x1, Pallas kernels, scan_forward(): pl.pallas_call(forward_kernel, grid=(PAIRS,), in_specs=[by_pair(TOKENS),...  13.8 us
    pallas_call x1, Pallas kernels, products(): pl.pallas_call(product_kernel, grid_spec=pltpu.PrefetchScalarGridSpec(num...  11.8 us
    all_gather x1, waiting for transfers between devices, shards(): rows = lax.all_gather(out_proj, 'blk', axis=0, tiled=True)  10.1 us
    unnamed x24, local copies, waits for them, and re-layouts  5.7 us
    ppermute x3, waiting for transfers between devices, shards(): summed = summed + lax.ppermute(summed, 'blk', swap(bit))  5.28 us
    ppermute x1, waiting for transfers between devices, shards(): partner = lax.ppermute(own, 'tp', [(t, t ^ 1) for t in range(8)])  5.03 us
  transfers between devices with their start and end apart: 19, of which 13 were waited for; matrix products, arithmetic and copies ran while one was open for 7% of the time, Pallas kernels for 43%

profile of v5, /device:TPU:6, one launch (start us, length us, event | category | flops | bytes accessed | tf_op | source)
XLA Modules:
  0.0 153.7 jit_solution(13001878860082787895)
XLA Ops:
  8.1 0.7 all-gather.2.cloned.1.call-update
  8.8 3.3 %collective-permute-start = (bf16[512,512]{1,0:T(8,128)(2,1)}, bf16[512,512]{1,0:T(8,128)(2,1)S(1)}, u32[]{:S(2)}, u32[]{:S(2)}) collective-permute-start(bf16[512,512]{1,0:T(8,128)(2,1)} %refs_0_.1), channel_id=1, source_target_pairs={{0,1},{1,0},{2,3},{3,2},{4,5},{5,4},{6,7},{7,6},{8,9},{9,8},{10,11... | collective-permute-start | bytes 1572872 | tf_op jit(solution)/shard_map/ppermute | solution.py:646
  12.6 1.5 %collective-permute-start.2 = (bf16[512,512]{1,0:T(8,128)(2,1)}, bf16[512,512]{1,0:T(8,128)(2,1)S(1)}, u32[]{:S(2)}, u32[]{:S(2)}) collective-permute-start(bf16[512,512]{1,0:T(8,128)(2,1)} %refs_0_.1), channel_id=1, source_target_pairs={{0,6},{1,7},{2,0},{3,1},{4,2},{5,3},{6,4},{7,5},{8,14},{9,15},{10,... | collective-permute-start | bytes 1572872 | tf_op jit(solution)/shard_map/ppermute | solution.py:600
  14.1 1.9 %copy.20 = bf16[64,8,2,256]{3,1,2,0:T(8,128)(2,1)} copy(bf16[64,8,2,256]{3,2,1,0:T(2,128)(2,1)} %bitcast.32) | data formatting | bytes 1048576
  16.0 0.7 broadcast_in_dim.3
  16.7 0.7 reshape_reshape.3.skip_ref
  17.4 0.6 stack.86.refs_0_
  18.0 1.2 pad_bitcast_fusion
  19.2 5.0 %collective-permute-done.refs_9_.refs_10_.refs_4_ = bf16[512,512]{1,0:T(8,128)(2,1)S(1)} collective-permute-done((bf16[512,512]{1,0:T(8,128)(2,1)}, bf16[512,512]{1,0:T(8,128)(2,1)S(1)}, u32[]{:S(2)}, u32[]{:S(2)}) %collective-permute-start) | collective-permute-done | bytes 524320 | tf_op jit(solution)/shard_map/ppermute | solution.py:646
  24.3 1.4 collective-permute-done.1.refs_3_.refs_4_.refs_1_
  25.7 1.4 collective-permute-done.2.refs_5_.refs_6_.refs_2_
  27.4 1.7 %collective-permute-start.4 = (bf16[512,512]{1,0:T(8,128)(2,1)S(1)}, bf16[512,512]{1,0:T(8,128)(2,1)S(1)}, u32[]{:S(2)}, u32[]{:S(2)}) collective-permute-start(bf16[512,512]{1,0:T(8,128)(2,1)S(1)} %collective-permute-done.refs_9_.refs_10_.refs_4_), channel_id=1, source_target_pairs={{0,6},{1,7},{2,0},{3,1},{4,2},{5,3},{6,4},{7,5},{8,14},{9,15},{10,... | collective-permute-start | bytes 1572872 | tf_op jit(solution)/shard_map/ppermute | solution.py:600
  29.1 1.6 %collective-permute-start.5 = (bf16[256,512]{1,0:T(8,128)(2,1)S(1)}, bf16[256,512]{1,0:T(8,128)(2,1)S(1)}, u32[]{:S(2)}, u32[]{:S(2)}) collective-permute-start(bf16[256,512]{1,0:T(8,128)(2,1)S(1)} %slice.27), channel_id=1, source_target_pairs={{0,2},{1,3},{2,4},{3,5},{4,6},{5,7},{6,0},{7,1},{8,10},{9,11},{10,... | collective-permute-start | bytes 786440 | tf_op jit(solution)/shard_map/ppermute | solution.py:605
  31.3 13.8 %scan_forward.1 = (bf16[1024,512]{1,0:T(8,128)(2,1)}, f32[512,1024]{1,0:T(8,128)}, f32[512,1024]{1,0:T(8,128)}, f32[8,3,256,128]{3,2,1,0:T(8,128)}, f32[512,128]{1,0:T(8,128)}) custom-call(bf16[512,1024]{1,0:T(8,128)(2,1)} %x_ref.1, bf16[512,1024]{1,0:T(8,128)(2,1)} %g_ref.3, bf16[512,512]{1,0:T(8,128)(2,1)} %bitcast.33, bf16[16,512]{1,0:T(8,128)(2,1)} %bitcast.39, ...), custom_call_target="tpu_custom_call" | custom-call | flops 16000000000 | bytes 10000000 | tf_op jit(solution)/shard_map/scan_forward/pallas_call | solution.py:349
  45.2 1.3 collective-permute-done.6
  46.5 1.6 %collective-permute-start.7 = (bf16[256,512]{1,0:T(8,128)(2,1)S(1)}, bf16[256,512]{1,0:T(8,128)(2,1)S(1)}, u32[]{:S(2)}, u32[]{:S(2)}) collective-permute-start(bf16[256,512]{1,0:T(8,128)(2,1)S(1)} %slice.29), channel_id=1, source_target_pairs={{0,2},{1,3},{2,4},{3,5},{4,6},{5,7},{6,0},{7,1},{8,10},{9,11},{10,... | collective-permute-start | bytes 786440 | tf_op jit(solution)/shard_map/ppermute | solution.py:605
  48.1 0.6 collective-permute-start.8
  48.8 0.8 copy-done.4
  49.6 6.0 %terms.2 = bf16[14336,128]{1,0:T(8,128)(2,1)} custom-call(s32[9]{0:T(128)} %stack.86.refs_0_, bf16[512,512]{1,0:T(8,128)(2,1)} %refs_0_.1, bf16[512,512]{1,0:T(8,128)(2,1)} %refs_0_.1, bf16[512,512]{1,0:T(8,128)(2,1)} %copy-done, bf16[512,512]{1,0:T(8,128)(2,1)} %copy-done, bf16[512,512]{1,0:T(8,128)(2,1)} %copy-done.1, bf16[512,512]{1,0:T(8,128)(2,1)} %copy-done.1, ...), custom_call_target="tpu_custom_call" | custom-call | flops 5600000000 | bytes 2000000 | tf_op jit(solution)/shard_map/terms/pallas_call | solution.py:490
  55.9 0.7 pad_add_fusion.refs_0_
  56.6 0.8 copy-done.5
  57.4 3.3 %terms.3 = bf16[2048,128]{1,0:T(8,128)(2,1)} custom-call(s32[3]{0:T(128)} %pad_add_fusion.refs_0_, bf16[512,512]{1,0:T(8,128)(2,1)} %copy-done.5, bf16[512,512]{1,0:T(8,128)(2,1)} %copy-done.5, bf16[1024,512]{1,0:T(8,128)(2,1)} %get-tuple-element.50.refs_15_.refs_3_.refs_17_), custom_call_target="tpu_custom_call" | custom-call | flops 1400000000 | bytes 2000000 | tf_op jit(solution)/shard_map/terms/pallas_call | solution.py:490
  61.3 0.7 stack.89.refs_0_
  62.0 2.1 %collective-permute-done.10.refs_19_ = bf16[2048,128]{1,0:T(8,128)(2,1)S(1)} collective-permute-done((bf16[2048,128]{1,0:T(8,128)(2,1)}, bf16[2048,128]{1,0:T(8,128)(2,1)S(1)}, u32[]{:S(2)}, u32[]{:S(2)}) %collective-permute-start.10) | collective-permute-done | bytes 524320 | tf_op jit(solution)/shard_map/ppermute | solution.py:675
  64.1 0.8 copy-done.8
  64.9 10.5 %terms_added.1 = bf16[16384,128]{1,0:T(8,128)(2,1)} custom-call(s32[10]{0:T(128)} %stack.89.refs_0_, bf16[512,512]{1,0:T(8,128)(2,1)} %refs_0_.1, bf16[512,512]{1,0:T(8,128)(2,1)} %refs_0_.1, bf16[512,512]{1,0:T(8,128)(2,1)} %copy-done, bf16[512,512]{1,0:T(8,128)(2,1)} %copy-done, bf16[512,512]{1,0:T(8,128)(2,1)} %copy-done.1, bf16[512,512]{1,0:T(8,128)(2,1)} %copy-done.1, ...), custom_call_target="tpu_custom_call" | custom-call | flops 6300000256 | bytes 2000000 | tf_op jit(solution)/shard_map/terms_added/pallas_call | solution.py:490
  75.4 0.6 stack.83.places
  76.0 10.1 %all-gather.2.cloned.1.call-done.refs_8_ = bf16[4096,1024]{1,0:T(8,128)(2,1)} async-done(((bf16[128,1024]{1,0:T(8,128)(2,1)}), bf16[4096,1024]{1,0:T(8,128)(2,1)}) %all-gather.2.cloned.1.call-update) | async-done | bytes 8388624 | tf_op jit(solution)/shard_map/all_gather | solution.py:644
  86.1 11.8 %products.1 = (f32[512,1024]{1,0:T(8,128)}, f32[1,1024]{1,0:T(1,128)}, f32[512,128]{1,0:T(8,128)}) custom-call(s32[8]{0:T(128)} %stack.83.places, bf16[512,512]{1,0:T(8,128)(2,1)} %refs_0_.1, bf16[512,512]{1,0:T(8,128)(2,1)} %copy-done, bf16[512,512]{1,0:T(8,128)(2,1)} %copy-done.1, bf16[512,512]{1,0:T(8,128)(2,1)} %copy-done.4, bf16[512,512]{1,0:T(8,128)(2,1)} %copy-done.7, ...), custom_call_target="tpu_custom_call" | custom-call | flops 12000000000 | bytes 16000000 | tf_op jit(solution)/shard_map/products/pallas_call | solution.py:563
  97.9 18.5 %scan_backward.1 = (bf16[512,1024]{1,0:T(8,128)(2,1)}, bf16[512,1024]{1,0:T(8,128)(2,1)}, bf16[512,256]{1,0:T(8,128)(2,1)}, bf16[512,256]{1,0:T(8,128)(2,1)}, f32[16,512]{1,0:T(8,128)}, /*index=5*/f32[8,128]{1,0:T(8,128)}) custom-call(bf16[512,1024]{1,0:T(8,128)(2,1)} %x_ref.1, bf16[512,1024]{1,0:T(8,128)(2,1)} %g_ref.3, ...), custom_call_target="tpu_custom_call" | custom-call | flops 20000000000 | bytes 10000000 | tf_op jit(solution)/shard_map/scan_backward/pallas_call | solution.py:379
  116.4 0.7 pad_maximum_fusion.1
  117.3 0.9 collective-permute-done.11
  118.2 0.7 fusion
  118.9 1.3 collective-permute-start.12
  120.2 2.7 %collective-permute-done.12 = f32[16,128]{1,0:T(8,128)S(1)} collective-permute-done((f32[16,128]{1,0:T(8,128)S(1)}, f32[16,128]{1,0:T(8,128)S(1)}, u32[]{:S(2)}, u32[]{:S(2)}) %collective-permute-start.12) | collective-permute-done | bytes 8224 | tf_op jit(solution)/shard_map/ppermute | solution.py:694
  122.9 2.2 %collective-permute-start.13 = (f32[16,128]{1,0:T(8,128)S(1)}, f32[16,128]{1,0:T(8,128)S(1)}, u32[]{:S(2)}, u32[]{:S(2)}) collective-permute-start(f32[16,128]{1,0:T(8,128)S(1)} %add.120), channel_id=1, source_target_pairs={{0,64},{8,72},{16,80},{24,88},{32,96},{40,104},{48,112},{56,120},{... | collective-permute-start | bytes 24584 | tf_op jit(solution)/shard_map/ppermute | solution.py:694
  125.1 1.1 pad_maximum_fusion
  126.2 1.6 %collective-permute-done.13 = f32[16,128]{1,0:T(8,128)S(1)} collective-permute-done((f32[16,128]{1,0:T(8,128)S(1)}, f32[16,128]{1,0:T(8,128)S(1)}, u32[]{:S(2)}, u32[]{:S(2)}) %collective-permute-start.13) | collective-permute-done | bytes 8224 | tf_op jit(solution)/shard_map/ppermute | solution.py:694
  127.8 3.5 %reduce-scatter.2.cloned.1.call-done.refs_0_ = bf16[2048,128]{1,0:T(8,128)(2,1)} async-done(((bf16[16384,128]{1,0:T(8,128)(2,1)}), bf16[2048,128]{1,0:T(8,128)(2,1)}) %reduce-scatter.2.cloned.1.call-update) | async-done | bytes 524304 | tf_op jit(solution)/shard_map/reduce_scatter | solution.py:677
  131.3 1.0 slice.31
  132.3 1.6 %collective-permute-start.14 = (bf16[1024,128]{1,0:T(8,128)(2,1)S(1)}, bf16[1024,128]{1,0:T(8,128)(2,1)S(1)}, u32[]{:S(2)}, u32[]{:S(2)}) collective-permute-start(bf16[1024,128]{1,0:T(8,128)(2,1)S(1)} %slice.31), channel_id=1, source_target_pairs={{0,16},{8,24},{16,0},{24,8},{32,48},{40,56},{48,32},{56,40},{64,80... | collective-permute-start | bytes 786440 | tf_op jit(solution)/shard_map/ppermute | solution.py:697
  133.8 3.4 %collective-permute-start.15 = (f32[16,128]{1,0:T(8,128)S(1)}, f32[16,128]{1,0:T(8,128)S(1)}, u32[]{:S(2)}, u32[]{:S(2)}) collective-permute-start(f32[16,128]{1,0:T(8,128)S(1)} %add.121), channel_id=1, source_target_pairs={{0,128},{8,136},{16,144},{24,152},{32,160},{40,168},{48,176},{56,1... | collective-permute-start | bytes 24584 | tf_op jit(solution)/shard_map/ppermute | solution.py:698
  137.3 1.3 copy.19
  138.6 2.8 %collective-permute-done.15 = f32[16,128]{1,0:T(8,128)S(1)} collective-permute-done((f32[16,128]{1,0:T(8,128)S(1)}, f32[16,128]{1,0:T(8,128)S(1)}, u32[]{:S(2)}, u32[]{:S(2)}) %collective-permute-start.15) | collective-permute-done | bytes 8224 | tf_op jit(solution)/shard_map/ppermute | solution.py:698
  141.4 0.6 collective-permute-start.16
  142.1 2.0 %finish.1 = f32[128,1024]{1,0:T(8,128)} custom-call(bf16[2048,128]{1,0:T(8,128)(2,1)} %reduce-scatter.2.cloned.1.call-done.refs_0_, bf16[1024,128]{1,0:T(8,128)(2,1)} %copy-done.9), custom_call_target="tpu_custom_call" | custom-call | flops 4000000000 | bytes 1000000 | tf_op jit(solution)/shard_map/finish/pallas_call | solution.py:519
  144.1 1.0 collective-permute-done.16
  145.1 0.6 slice_bitcast_fusion
  (46 shorter events, 3.4 us)
Async XLA Ops:
  8.0 78.1 %all-gather.2.cloned.1.call-start = ((), (), s32[]{:S(2)}) async-start(), calls=%async_computation.1 | async-start | bytes 8650752 | tf_op jit(solution)/shard_map/all_gather | solution.py:644
  8.7 122.5 %reduce-scatter.2.cloned.1.call-start = ((), (), s32[]{:S(2)}) async-start(), calls=%async_computation.2 | async-start | bytes 4718592 | tf_op jit(solution)/shard_map/reduce_scatter | solution.py:677
  8.8 15.5 %collective-permute-start = (bf16[512,512]{1,0:T(8,128)(2,1)}, bf16[512,512]{1,0:T(8,128)(2,1)S(1)}, u32[]{:S(2)}, u32[]{:S(2)}) collective-permute-start(bf16[512,512]{1,0:T(8,128)(2,1)} %refs_0_.1), channel_id=1, source_target_pairs={{0,1},{1,0},{2,3},{3,2},{4,5},{5,4},{6,7},{7,6},{8,9},{9,8},{10,11... | collective-permute-start | bytes 1572872 | tf_op jit(solution)/shard_map/ppermute | solution.py:646
  12.1 13.6 %collective-permute-start.1 = (bf16[512,512]{1,0:T(8,128)(2,1)}, bf16[512,512]{1,0:T(8,128)(2,1)S(1)}, u32[]{:S(2)}, u32[]{:S(2)}) collective-permute-start(bf16[512,512]{1,0:T(8,128)(2,1)} %refs_0_.1), channel_id=1, source_target_pairs={{0,2},{1,3},{2,4},{3,5},{4,6},{5,7},{6,0},{7,1},{8,10},{9,11},{10,... | collective-permute-start | bytes 1572872 | tf_op jit(solution)/shard_map/ppermute | solution.py:600
  12.6 14.5 %collective-permute-start.2 = (bf16[512,512]{1,0:T(8,128)(2,1)}, bf16[512,512]{1,0:T(8,128)(2,1)S(1)}, u32[]{:S(2)}, u32[]{:S(2)}) collective-permute-start(bf16[512,512]{1,0:T(8,128)(2,1)} %refs_0_.1), channel_id=1, source_target_pairs={{0,6},{1,7},{2,0},{3,1},{4,2},{5,3},{6,4},{7,5},{8,14},{9,15},{10,... | collective-permute-start | bytes 1572872 | tf_op jit(solution)/shard_map/ppermute | solution.py:600
  24.3 20.9 %copy-start.7 = (bf16[512,512]{1,0:T(8,128)(2,1)}, bf16[512,512]{1,0:T(8,128)(2,1)S(1)}, u32[]{:S(2)}) copy-start(bf16[512,512]{1,0:T(8,128)(2,1)S(1)} %collective-permute-done.refs_9_.refs_10_.refs_4_) | copy-start | bytes 1572868
  25.7 19.5 %copy-start = (bf16[512,512]{1,0:T(8,128)(2,1)}, bf16[512,512]{1,0:T(8,128)(2,1)S(1)}, u32[]{:S(2)}) copy-start(bf16[512,512]{1,0:T(8,128)(2,1)S(1)} %collective-permute-done.1.refs_3_.refs_4_.refs_1_) | copy-start | bytes 1572868
  27.1 18.1 %copy-start.1 = (bf16[512,512]{1,0:T(8,128)(2,1)}, bf16[512,512]{1,0:T(8,128)(2,1)S(1)}, u32[]{:S(2)}) copy-start(bf16[512,512]{1,0:T(8,128)(2,1)S(1)} %collective-permute-done.2.refs_5_.refs_6_.refs_2_) | copy-start | bytes 1572868
  27.1 19.4 %collective-permute-start.3 = (bf16[512,512]{1,0:T(8,128)(2,1)S(1)}, bf16[512,512]{1,0:T(8,128)(2,1)S(1)}, u32[]{:S(2)}, u32[]{:S(2)}) collective-permute-start(bf16[512,512]{1,0:T(8,128)(2,1)S(1)} %collective-permute-done.refs_9_.refs_10_.refs_4_), channel_id=1, source_target_pairs={{0,2},{1,3},{2,4},{3,5},{4,6},{5,7},{6,0},{7,1},{8,10},{9,11},{10,... | collective-permute-start | bytes 1572872 | tf_op jit(solution)/shard_map/ppermute | solution.py:600
  27.4 19.0 %collective-permute-start.4 = (bf16[512,512]{1,0:T(8,128)(2,1)S(1)}, bf16[512,512]{1,0:T(8,128)(2,1)S(1)}, u32[]{:S(2)}, u32[]{:S(2)}) collective-permute-start(bf16[512,512]{1,0:T(8,128)(2,1)S(1)} %collective-permute-done.refs_9_.refs_10_.refs_4_), channel_id=1, source_target_pairs={{0,6},{1,7},{2,0},{3,1},{4,2},{5,3},{6,4},{7,5},{8,14},{9,15},{10,... | collective-permute-start | bytes 1572872 | tf_op jit(solution)/shard_map/ppermute | solution.py:600
  29.1 16.0 %collective-permute-start.5 = (bf16[256,512]{1,0:T(8,128)(2,1)S(1)}, bf16[256,512]{1,0:T(8,128)(2,1)S(1)}, u32[]{:S(2)}, u32[]{:S(2)}) collective-permute-start(bf16[256,512]{1,0:T(8,128)(2,1)S(1)} %slice.27), channel_id=1, source_target_pairs={{0,2},{1,3},{2,4},{3,5},{4,6},{5,7},{6,0},{7,1},{8,10},{9,11},{10,... | collective-permute-start | bytes 786440 | tf_op jit(solution)/shard_map/ppermute | solution.py:605
  30.8 15.7 %collective-permute-start.6 = (bf16[256,512]{1,0:T(8,128)(2,1)S(1)}, bf16[256,512]{1,0:T(8,128)(2,1)S(1)}, u32[]{:S(2)}, u32[]{:S(2)}) collective-permute-start(bf16[256,512]{1,0:T(8,128)(2,1)S(1)} %slice.28), channel_id=1, source_target_pairs={{0,6},{1,7},{2,0},{3,1},{4,2},{5,3},{6,4},{7,5},{8,14},{9,15},{10,... | collective-permute-start | bytes 786440 | tf_op jit(solution)/shard_map/ppermute | solution.py:606
  46.5 2.3 %copy-start.2 = (bf16[512,512]{1,0:T(8,128)(2,1)}, bf16[512,512]{1,0:T(8,128)(2,1)S(1)}, u32[]{:S(2)}) copy-start(bf16[512,512]{1,0:T(8,128)(2,1)S(1)} %collective-permute-done.3.refs_11_.refs_12_.refs_5_) | copy-start | bytes 1572868
  46.5 2.3 %copy-start.3 = (bf16[512,512]{1,0:T(8,128)(2,1)}, bf16[512,512]{1,0:T(8,128)(2,1)S(1)}, u32[]{:S(2)}) copy-start(bf16[512,512]{1,0:T(8,128)(2,1)S(1)} %collective-permute-done.4.refs_13_.refs_14_.refs_6_) | copy-start | bytes 1572868
  46.5 9.1 %collective-permute-start.7 = (bf16[256,512]{1,0:T(8,128)(2,1)S(1)}, bf16[256,512]{1,0:T(8,128)(2,1)S(1)}, u32[]{:S(2)}, u32[]{:S(2)}) collective-permute-start(bf16[256,512]{1,0:T(8,128)(2,1)S(1)} %slice.29), channel_id=1, source_target_pairs={{0,2},{1,3},{2,4},{3,5},{4,6},{5,7},{6,0},{7,1},{8,10},{9,11},{10,... | collective-permute-start | bytes 786440 | tf_op jit(solution)/shard_map/ppermute | solution.py:605
  48.1 7.7 %collective-permute-start.8 = (bf16[256,512]{1,0:T(8,128)(2,1)S(1)}, bf16[256,512]{1,0:T(8,128)(2,1)S(1)}, u32[]{:S(2)}, u32[]{:S(2)}) collective-permute-start(bf16[256,512]{1,0:T(8,128)(2,1)S(1)} %slice.30), channel_id=1, source_target_pairs={{0,6},{1,7},{2,0},{3,1},{4,2},{5,3},{6,4},{7,5},{8,14},{9,15},{10,... | collective-permute-start | bytes 786440 | tf_op jit(solution)/shard_map/ppermute | solution.py:606
  48.8 0.8 copy-start.4
  55.8 8.3 %collective-permute-start.9 = (bf16[14336,128]{1,0:T(8,128)(2,1)}, bf16[14336,128]{1,0:T(8,128)(2,1)}, u32[]{:S(2)}, u32[]{:S(2)}) collective-permute-start(bf16[14336,128]{1,0:T(8,128)(2,1)} %terms.2), channel_id=1, source_target_pairs={{0,8},{8,0},{16,24},{24,16},{32,40},{40,32},{48,56},{56,48},{64,72... | collective-permute-start | bytes 11010056 | tf_op jit(solution)/shard_map/ppermute | solution.py:673
  56.6 0.8 copy-start.5
  60.7 3.3 %collective-permute-start.10 = (bf16[2048,128]{1,0:T(8,128)(2,1)}, bf16[2048,128]{1,0:T(8,128)(2,1)S(1)}, u32[]{:S(2)}, u32[]{:S(2)}) collective-permute-start(bf16[2048,128]{1,0:T(8,128)(2,1)} %terms.3), channel_id=1, source_target_pairs={{0,8},{8,0},{16,24},{24,16},{32,40},{40,32},{48,56},{56,48},{64,72... | collective-permute-start | bytes 1572872 | tf_op jit(solution)/shard_map/ppermute | solution.py:675
  64.1 0.8 copy-start.8
  97.9 18.5 %copy-start.6 = (f32[1,1024]{1,0:T(1,128)S(1)}, f32[1,1024]{1,0:T(1,128)}, u32[]{:S(2)}) copy-start(f32[1,1024]{1,0:T(1,128)} %get-tuple-element.64) | copy-start | bytes 12292
  117.1 1.2 collective-permute-start.11
  118.9 4.0 %collective-permute-start.12 = (f32[16,128]{1,0:T(8,128)S(1)}, f32[16,128]{1,0:T(8,128)S(1)}, u32[]{:S(2)}, u32[]{:S(2)}) collective-permute-start(f32[16,128]{1,0:T(8,128)S(1)} %fusion), channel_id=1, source_target_pairs={{0,32},{8,40},{16,48},{24,56},{32,0},{40,8},{48,16},{56,24},{64,96... | collective-permute-start | bytes 24584 | tf_op jit(solution)/shard_map/ppermute | solution.py:694
  122.9 4.9 %collective-permute-start.13 = (f32[16,128]{1,0:T(8,128)S(1)}, f32[16,128]{1,0:T(8,128)S(1)}, u32[]{:S(2)}, u32[]{:S(2)}) collective-permute-start(f32[16,128]{1,0:T(8,128)S(1)} %add.120), channel_id=1, source_target_pairs={{0,64},{8,72},{16,80},{24,88},{32,96},{40,104},{48,112},{56,120},{... | collective-permute-start | bytes 24584 | tf_op jit(solution)/shard_map/ppermute | solution.py:694
  132.3 9.1 %collective-permute-start.14 = (bf16[1024,128]{1,0:T(8,128)(2,1)S(1)}, bf16[1024,128]{1,0:T(8,128)(2,1)S(1)}, u32[]{:S(2)}, u32[]{:S(2)}) collective-permute-start(bf16[1024,128]{1,0:T(8,128)(2,1)S(1)} %slice.31), channel_id=1, source_target_pairs={{0,16},{8,24},{16,0},{24,8},{32,48},{40,56},{48,32},{56,40},{64,80... | collective-permute-start | bytes 786440 | tf_op jit(solution)/shard_map/ppermute | solution.py:697
  133.8 7.6 %collective-permute-start.15 = (f32[16,128]{1,0:T(8,128)S(1)}, f32[16,128]{1,0:T(8,128)S(1)}, u32[]{:S(2)}, u32[]{:S(2)}) collective-permute-start(f32[16,128]{1,0:T(8,128)S(1)} %add.121), channel_id=1, source_target_pairs={{0,128},{8,136},{16,144},{24,152},{32,160},{40,168},{48,176},{56,1... | collective-permute-start | bytes 24584 | tf_op jit(solution)/shard_map/ppermute | solution.py:698
  141.4 0.7 copy-start.9
  141.4 3.7 %collective-permute-start.16 = (f32[16,128]{1,0:T(8,128)S(1)}, f32[16,128]{1,0:T(8,128)S(1)}, u32[]{:S(2)}, u32[]{:S(2)}) collective-permute-start(f32[16,128]{1,0:T(8,128)S(1)} %add.122), channel_id=1, source_target_pairs={{0,16},{8,24},{16,0},{24,8},{32,48},{40,56},{48,32},{56,40},{64,80... | collective-permute-start | bytes 24584 | tf_op jit(solution)/shard_map/ppermute | solution.py:701
Sparse Core Ops, SparseCore 0:
  10.7 75.3 all-gather.1
Sparse Core Ops, SparseCore 1:
  75.5 55.7 reduce-scatter.1

commit v6 on v4

--- a/solution.py
+++ b/solution.py
@@ -187,14 +187,16 @@
 
 def backward_kernel(x_ref, g_ref, cot_ref, scan_ref, state_ref, scale_ref, pull_ref,
                     bc_ref, raw_t_ref, bias_ref, rate_ref, skip_ref, gain_ref,
+                    raw, pack, run_rows, step_rows, overlap,
                     dx_ref, dg_ref, db_ref, dc_ref, step_ref, small_ref,
-                    raw, pack, run_rows, step_rows, overlap, spread, turned, d_overlap, d_b, d_c, flow, direct, lanes):
+                    spread, turned, d_overlap, d_b, d_c, flow, direct, lanes):
     pair = pl.program_id(0)
 
     @pl.when(pair == 0)
     def _():
-        prepare(raw_t_ref, bias_ref, rate_ref, bc_ref, turned, STATE,
-                raw, pack, run_rows, step_rows, overlap)
+        for c in range(CHUNKS):
+            rows = slice(c * CHUNK, (c + 1) * CHUNK)
+            turned[:, rows] = bc_ref[rows, STATE:].astype(F32).T.astype(BF16)
         for held in (d_overlap, d_b, d_c, flow, direct, lanes):
             held[...] = jnp.zeros_like(held)
 
@@ -326,11 +328,14 @@
 VMEM_LIMIT = 56 * 1024 * 1024
 
 TABLES = [
-    pltpu.VMEM((TOKENS, LANES), F32),
-    pltpu.VMEM((TOKENS, LANES), BF16),
-    pltpu.VMEM((PAIRS, 2, TOKENS), F32),
-    pltpu.VMEM((PAIRS, 2, TOKENS), F32),
-    pltpu.VMEM((CHUNKS, CHUNK, CHUNK), F32),
+    jax.ShapeDtypeStruct((TOKENS, LANES), F32),
+    jax.ShapeDtypeStruct((TOKENS, LANES), BF16),
+    jax.ShapeDtypeStruct((PAIRS, 2, TOKENS), F32),
+    jax.ShapeDtypeStruct((PAIRS, 2, TOKENS), F32),
+    jax.ShapeDtypeStruct((CHUNKS, CHUNK, CHUNK), F32),
+]
+
+SCRATCH = [
     pltpu.VMEM((TOKENS, 4 * LANES), F32),
     pltpu.VMEM((STATE, TOKENS), BF16),
 ]
@@ -360,22 +365,24 @@
             whole((TOKENS, CHANNELS)),
             pl.BlockSpec((1, CHUNKS - 1, STATE, LANES), lambda p: (p, 0, 0, 0)),
             whole((TOKENS, LANES)),
-        ],
+        ]
+        + [whole(one.shape) for one in TABLES],
         out_shape=[
             jax.ShapeDtypeStruct((CHANNELS, TOKENS), BF16),
             jax.ShapeDtypeStruct((TOKENS, CHANNELS), F32),
             jax.ShapeDtypeStruct((TOKENS, CHANNELS), F32),
             jax.ShapeDtypeStruct((PAIRS, CHUNKS - 1, STATE, LANES), F32),
             jax.ShapeDtypeStruct((TOKENS, LANES), F32),
-        ],
-        scratch_shapes=TABLES + [pltpu.VMEM((TOKENS, LANES), F32)],
+        ]
+        + TABLES,
+        scratch_shapes=SCRATCH + [pltpu.VMEM((TOKENS, LANES), F32)],
         compiler_params=pltpu.CompilerParams(vmem_limit_bytes=VMEM_LIMIT),
         cost_estimate=pl.CostEstimate(flops=16 * 10**9, bytes_accessed=10**7, transcendentals=0),
         name="scan_forward",
     )(x, g, *parameters)
 
 
-def scan_backward(x, g, cot, scan, states, scale, pull, parameters):
+def scan_backward(x, g, cot, scan, states, scale, pull, parameters, tables):
     return pl.pallas_call(
         backward_kernel,
         grid=(PAIRS,),
@@ -388,7 +395,8 @@
             whole((TOKENS, LANES)),
             whole((TOKENS, LANES)),
         ]
-        + PARAMETERS,
+        + PARAMETERS
+        + [whole(one.shape) for one in TABLES],
         out_specs=[
             by_pair(TOKENS),
             by_pair(TOKENS),
@@ -405,7 +413,7 @@
             jax.ShapeDtypeStruct((HEADS, TOKENS), F32),
             jax.ShapeDtypeStruct((8, LANES), F32),
         ],
-        scratch_shapes=TABLES
+        scratch_shapes=SCRATCH
         + [
             pltpu.VMEM((CHUNKS, CHUNK, CHUNK), F32),
             pltpu.VMEM((TOKENS, STATE), F32),
@@ -417,7 +425,7 @@
         compiler_params=pltpu.CompilerParams(vmem_limit_bytes=VMEM_LIMIT),
         cost_estimate=pl.CostEstimate(flops=20 * 10**9, bytes_accessed=10**7, transcendentals=0),
         name="scan_backward",
-    )(x, g, cot, scan, states, scale, pull, *parameters)
+    )(x, g, cot, scan, states, scale, pull, *parameters, *tables)
 
 
 FEATURES = 512
@@ -639,7 +647,7 @@
     parameters = local_parameters(
         state_proj, step_raw, log_rate, step_bias, skip_gain, norm_gain
     )
-    low, scan, gated, states, scale = scan_forward(scan_input, gate_input, parameters)
+    low, scan, gated, states, scale, *tables = scan_forward(scan_input, gate_input, parameters)
     partner_before, partner_after, far_parts, low = lax.optimization_barrier(
         (partner_before, partner_after, far_parts, low)
     )
@@ -672,18 +680,18 @@
         parameters[-1],
     )
     dx, dg, db, dc, step_grad, small = scan_backward(
-        scan_input, gate_input, cot, scan, states, scale, pull, parameters
+        scan_input, gate_input, cot, scan, states, scale, pull, parameters, tables
     )
     summed = jnp.concatenate([small, gain_grad.reshape(8, LANES)], axis=0)
-    for bit in (1, 4, 8):
+    for bit in (1, 4, 8, 16):
         summed = summed + lax.ppermute(summed, "blk", swap(bit))
     state_grad = jnp.stack([db, dc], axis=1)
     plane, summed, state_grad = lax.optimization_barrier((plane, summed, state_grad))
     given = lax.ppermute(plane[:CHANNELS], "blk", swap(2))
-    summed = summed + lax.ppermute(summed, "blk", swap(16))
+    summed = summed + lax.ppermute(summed, "blk", swap(2))
     given, summed = lax.optimization_barrier((given, summed))
     weight_grad = finish(plane, given, norm_scale)
-    summed = (summed + lax.ppermute(summed, "blk", swap(2))) * norm_scale
+    summed = summed * norm_scale
     return (
         dx,
         dg,

time: 152 us -> 153 us (level)
  waiting for transfers between devices: 35.5 us -> 37.9 us
    ppermute x3 -> x4, waiting for transfers between devices: 5.29 us -> 9.96 us  [shards(): summed = summed + lax.ppermute(summed, 'blk', swap(bit))]
    ppermute x2 -> x1, starting transfers between devices: 4.02 us -> 0.69 us  [shards(): summed = summed + lax.ppermute(summed, 'blk', swap(2))]
    ppermute x3 -> x4, starting transfers between devices: 3.34 us -> 6.65 us  [shards(): summed = summed + lax.ppermute(summed, 'blk', swap(bit))]
    ppermute x2 -> x1, waiting for transfers between devices: 3.87 us -> 3.1 us  [shards(): summed = summed + lax.ppermute(summed, 'blk', swap(2))]
  transfers between devices with their start and end apart: 19 -> 19, of which waited for: 13 -> 12; matrix products, arithmetic and copies ran while one was open for 7% -> 7% of each run, Pallas kernels for 42% -> 39%
where the time goes in v6:
time: 153 us; the launch traced here: 152 us
  Pallas kernels  61.6 us (40%)
  waiting for transfers between devices  37.9 us (25%)
  starting transfers between devices  21.2 us (14%)
  between operations  15.7 us (10%)
  local copies, waits for them, and re-layouts  12.4 us (8%)
  other arithmetic  3.12 us (2%)
    pallas_call x3, Pallas kernels, terms(): pl.pallas_call(kernel, grid_spec=pltpu.PrefetchScalarGridSpec(num_scalar_...  17 us
    pallas_call x1, Pallas kernels, scan_backward(): pl.pallas_call(backward_kernel, grid=(PAIRS,), in_specs=[by_pair(TOKENS),...  17 us
    pallas_call x1, Pallas kernels, scan_forward(): pl.pallas_call(forward_kernel, grid=(PAIRS,), in_specs=[by_pair(TOKENS),...  14.1 us
    all_gather x1, waiting for transfers between devices, shards(): rows = lax.all_gather(out_proj, 'blk', axis=0, tiled=True)  12.8 us
    pallas_call x1, Pallas kernels, products(): pl.pallas_call(product_kernel, grid_spec=pltpu.PrefetchScalarGridSpec(num...  11.5 us
    ppermute x4, waiting for transfers between devices, shards(): summed = summed + lax.ppermute(summed, 'blk', swap(bit))  9.96 us
    ppermute x4, starting transfers between devices, shards(): summed = summed + lax.ppermute(summed, 'blk', swap(bit))  6.65 us
    unnamed x24, local copies, waits for them, and re-layouts  5.65 us
  transfers between devices with their start and end apart: 19, of which 12 were waited for; matrix products, arithmetic and copies ran while one was open for 7% of the time, Pallas kernels for 39%

profile of v6, /device:TPU:6, one launch (start us, length us, event | category | flops | bytes accessed | tf_op | source)
XLA Modules:
  0.0 151.9 jit_solution(15809651958806863253)
XLA Ops:
  8.1 0.7 all-gather.2.cloned.1.call-update
  8.8 3.3 %collective-permute-start = (bf16[512,512]{1,0:T(8,128)(2,1)}, bf16[512,512]{1,0:T(8,128)(2,1)S(1)}, u32[]{:S(2)}, u32[]{:S(2)}) collective-permute-start(bf16[512,512]{1,0:T(8,128)(2,1)} %refs_0_.1), channel_id=1, source_target_pairs={{0,1},{1,0},{2,3},{3,2},{4,5},{5,4},{6,7},{7,6},{8,9},{9,8},{10,11... | collective-permute-start | bytes 1572872 | tf_op jit(solution)/shard_map/ppermute | solution.py:639
  12.6 1.5 %collective-permute-start.2 = (bf16[512,512]{1,0:T(8,128)(2,1)}, bf16[512,512]{1,0:T(8,128)(2,1)S(1)}, u32[]{:S(2)}, u32[]{:S(2)}) collective-permute-start(bf16[512,512]{1,0:T(8,128)(2,1)} %refs_0_.1), channel_id=1, source_target_pairs={{0,6},{1,7},{2,0},{3,1},{4,2},{5,3},{6,4},{7,5},{8,14},{9,15},{10,... | collective-permute-start | bytes 1572872 | tf_op jit(solution)/shard_map/ppermute | solution.py:593
  14.1 1.9 %copy.20 = bf16[64,8,2,256]{3,1,2,0:T(8,128)(2,1)} copy(bf16[64,8,2,256]{3,2,1,0:T(2,128)(2,1)} %bitcast.32) | data formatting | bytes 1048576
  16.0 0.7 broadcast_in_dim.3
  16.7 0.7 reshape_reshape.3.skip_ref
  17.4 0.6 stack.86.refs_0_
  18.0 1.3 pad_bitcast_fusion
  19.3 5.0 %collective-permute-done.refs_9_.refs_10_.refs_4_ = bf16[512,512]{1,0:T(8,128)(2,1)S(1)} collective-permute-done((bf16[512,512]{1,0:T(8,128)(2,1)}, bf16[512,512]{1,0:T(8,128)(2,1)S(1)}, u32[]{:S(2)}, u32[]{:S(2)}) %collective-permute-start) | collective-permute-done | bytes 524320 | tf_op jit(solution)/shard_map/ppermute | solution.py:639
  24.3 1.4 collective-permute-done.1.refs_3_.refs_4_.refs_1_
  25.7 1.4 collective-permute-done.2.refs_5_.refs_6_.refs_2_
  27.4 1.7 %collective-permute-start.4 = (bf16[512,512]{1,0:T(8,128)(2,1)S(1)}, bf16[512,512]{1,0:T(8,128)(2,1)S(1)}, u32[]{:S(2)}, u32[]{:S(2)}) collective-permute-start(bf16[512,512]{1,0:T(8,128)(2,1)S(1)} %collective-permute-done.refs_9_.refs_10_.refs_4_), channel_id=1, source_target_pairs={{0,6},{1,7},{2,0},{3,1},{4,2},{5,3},{6,4},{7,5},{8,14},{9,15},{10,... | collective-permute-start | bytes 1572872 | tf_op jit(solution)/shard_map/ppermute | solution.py:593
  29.1 1.6 %collective-permute-start.5 = (bf16[256,512]{1,0:T(8,128)(2,1)S(1)}, bf16[256,512]{1,0:T(8,128)(2,1)S(1)}, u32[]{:S(2)}, u32[]{:S(2)}) collective-permute-start(bf16[256,512]{1,0:T(8,128)(2,1)S(1)} %slice.27), channel_id=1, source_target_pairs={{0,2},{1,3},{2,4},{3,5},{4,6},{5,7},{6,0},{7,1},{8,10},{9,11},{10,... | collective-permute-start | bytes 786440 | tf_op jit(solution)/shard_map/ppermute | solution.py:598
  30.8 0.5 collective-permute-start.6
  31.3 14.1 %scan_forward.1 = (bf16[1024,512]{1,0:T(8,128)(2,1)}, f32[512,1024]{1,0:T(8,128)}, f32[512,1024]{1,0:T(8,128)}, f32[8,3,256,128]{3,2,1,0:T(8,128)}, f32[512,128]...) custom-call(bf16[512,1024]{1,0:T(8,128)(2,1)} %x_ref.1, ...), custom_call_target="tpu_custom_call" | custom-call | flops 16000000000 | bytes 10000000 | tf_op jit(solution)/shard_map/scan_forward/pallas_call | solution.py:354
  45.4 1.0 collective-permute-done.6
  46.5 1.9 %collective-permute-start.7 = (bf16[256,512]{1,0:T(8,128)(2,1)S(1)}, bf16[256,512]{1,0:T(8,128)(2,1)S(1)}, u32[]{:S(2)}, u32[]{:S(2)}) collective-permute-start(bf16[256,512]{1,0:T(8,128)(2,1)S(1)} %slice.29), channel_id=1, source_target_pairs={{0,2},{1,3},{2,4},{3,5},{4,6},{5,7},{6,0},{7,1},{8,10},{9,11},{10,... | collective-permute-start | bytes 786440 | tf_op jit(solution)/shard_map/ppermute | solution.py:598
  48.8 0.8 copy-done.4
  49.6 6.0 %terms.2 = bf16[14336,128]{1,0:T(8,128)(2,1)} custom-call(s32[9]{0:T(128)} %stack.86.refs_0_, bf16[512,512]{1,0:T(8,128)(2,1)} %refs_0_.1, bf16[512,512]{1,0:T(8,128)(2,1)} %refs_0_.1, bf16[512,512]{1,0:T(8,128)(2,1)} %copy-done, bf16[512,512]{1,0:T(8,128)(2,1)} %copy-done, bf16[512,512]{1,0:T(8,128)(2,1)} %copy-done.1, bf16[512,512]{1,0:T(8,128)(2,1)} %copy-done.1, ...), custom_call_target="tpu_custom_call" | custom-call | flops 5600000000 | bytes 2000000 | tf_op jit(solution)/shard_map/terms/pallas_call | solution.py:480
  56.0 0.7 pad_add_fusion.refs_0_
  56.8 0.8 copy-done.5
  57.5 3.3 %terms.3 = bf16[2048,128]{1,0:T(8,128)(2,1)} custom-call(s32[3]{0:T(128)} %pad_add_fusion.refs_0_, bf16[512,512]{1,0:T(8,128)(2,1)} %copy-done.5, bf16[512,512]{1,0:T(8,128)(2,1)} %copy-done.5, bf16[1024,512]{1,0:T(8,128)(2,1)} %get-tuple-element.55.refs_15_.refs_3_.refs_17_), custom_call_target="tpu_custom_call" | custom-call | flops 1400000000 | bytes 2000000 | tf_op jit(solution)/shard_map/terms/pallas_call | solution.py:480
  60.8 0.6 collective-permute-start.10
  61.5 0.6 stack.89.refs_0_
  62.1 2.2 %collective-permute-done.10.refs_19_ = bf16[2048,128]{1,0:T(8,128)(2,1)S(1)} collective-permute-done((bf16[2048,128]{1,0:T(8,128)(2,1)}, bf16[2048,128]{1,0:T(8,128)(2,1)S(1)}, u32[]{:S(2)}, u32[]{:S(2)}) %collective-permute-start.10) | collective-permute-done | bytes 524320 | tf_op jit(solution)/shard_map/ppermute | solution.py:668
  64.3 0.8 copy-done.8
  65.0 7.7 %terms_added.1 = bf16[16384,128]{1,0:T(8,128)(2,1)} custom-call(s32[10]{0:T(128)} %stack.89.refs_0_, bf16[512,512]{1,0:T(8,128)(2,1)} %refs_0_.1, bf16[512,512]{1,0:T(8,128)(2,1)} %refs_0_.1, bf16[512,512]{1,0:T(8,128)(2,1)} %copy-done, bf16[512,512]{1,0:T(8,128)(2,1)} %copy-done, bf16[512,512]{1,0:T(8,128)(2,1)} %copy-done.1, bf16[512,512]{1,0:T(8,128)(2,1)} %copy-done.1, ...), custom_call_target="tpu_custom_call" | custom-call | flops 6300000256 | bytes 2000000 | tf_op jit(solution)/shard_map/terms_added/pallas_call | solution.py:480
  72.8 0.6 stack.83.places
  73.4 12.8 %all-gather.2.cloned.1.call-done.refs_8_ = bf16[4096,1024]{1,0:T(8,128)(2,1)} async-done(((bf16[128,1024]{1,0:T(8,128)(2,1)}), bf16[4096,1024]{1,0:T(8,128)(2,1)}) %all-gather.2.cloned.1.call-update) | async-done | bytes 8388624 | tf_op jit(solution)/shard_map/all_gather | solution.py:637
  86.1 11.5 %products.1 = (f32[512,1024]{1,0:T(8,128)}, f32[1,1024]{1,0:T(1,128)}, f32[512,128]{1,0:T(8,128)}) custom-call(s32[8]{0:T(128)} %stack.83.places, bf16[512,512]{1,0:T(8,128)(2,1)} %refs_0_.1, bf16[512,512]{1,0:T(8,128)(2,1)} %copy-done, bf16[512,512]{1,0:T(8,128)(2,1)} %copy-done.1, bf16[512,512]{1,0:T(8,128)(2,1)} %copy-done.4, bf16[512,512]{1,0:T(8,128)(2,1)} %copy-done.7, ...), custom_call_target="tpu_custom_call" | custom-call | flops 12000000000 | bytes 16000000 | tf_op jit(solution)/shard_map/products/pallas_call | solution.py:556
  97.6 17.0 %scan_backward.1 = (bf16[512,1024]{1,0:T(8,128)(2,1)}, bf16[512,1024]{1,0:T(8,128)(2,1)}, bf16[512,256]{1,0:T(8,128)(2,1)}, bf16[512,256]{1,0:T(8,128)(2,1)}, f32[16,512]{1,0:T(8,128)}, /*index=5*/f32[8,128]{1,0:T(8,128)}) custom-call(bf16[512,1024]{1,0:T(8,128)(2,1)} %x_ref.1, bf16[512,1024]{1,0:T(8,128)(2,1)} %g_ref.3, ...), custom_call_target="tpu_custom_call" | custom-call | flops 20000000000 | bytes 10000000 | tf_op jit(solution)/shard_map/scan_backward/pallas_call | solution.py:386
  114.7 0.7 pad_maximum_fusion.1
  115.6 0.9 collective-permute-done.11
  116.5 0.7 fusion
  117.2 0.7 collective-permute-start.12
  117.9 3.3 %collective-permute-done.12 = f32[16,128]{1,0:T(8,128)S(1)} collective-permute-done((f32[16,128]{1,0:T(8,128)S(1)}, f32[16,128]{1,0:T(8,128)S(1)}, u32[]{:S(2)}, u32[]{:S(2)}) %collective-permute-start.12) | collective-permute-done | bytes 8224 | tf_op jit(solution)/shard_map/ppermute | solution.py:687
  121.2 1.7 %collective-permute-start.13 = (f32[16,128]{1,0:T(8,128)S(1)}, f32[16,128]{1,0:T(8,128)S(1)}, u32[]{:S(2)}, u32[]{:S(2)}) collective-permute-start(f32[16,128]{1,0:T(8,128)S(1)} %add.120), channel_id=1, source_target_pairs={{0,64},{8,72},{16,80},{24,88},{32,96},{40,104},{48,112},{56,120},{... | collective-permute-start | bytes 24584 | tf_op jit(solution)/shard_map/ppermute | solution.py:687
  122.9 3.3 %collective-permute-done.13 = f32[16,128]{1,0:T(8,128)S(1)} collective-permute-done((f32[16,128]{1,0:T(8,128)S(1)}, f32[16,128]{1,0:T(8,128)S(1)}, u32[]{:S(2)}, u32[]{:S(2)}) %collective-permute-start.13) | collective-permute-done | bytes 8224 | tf_op jit(solution)/shard_map/ppermute | solution.py:687
  126.2 4.1 %collective-permute-start.14 = (f32[16,128]{1,0:T(8,128)S(1)}, f32[16,128]{1,0:T(8,128)S(1)}, u32[]{:S(2)}, u32[]{:S(2)}) collective-permute-start(f32[16,128]{1,0:T(8,128)S(1)} %add.121), channel_id=1, source_target_pairs={{0,128},{8,136},{16,144},{24,152},{32,160},{40,168},{48,176},{56,1... | collective-permute-start | bytes 24584 | tf_op jit(solution)/shard_map/ppermute | solution.py:687
  130.2 1.1 pad_maximum_fusion
  131.3 2.4 %collective-permute-done.14 = f32[16,128]{1,0:T(8,128)S(1)} collective-permute-done((f32[16,128]{1,0:T(8,128)S(1)}, f32[16,128]{1,0:T(8,128)S(1)}, u32[]{:S(2)}, u32[]{:S(2)}) %collective-permute-start.14) | collective-permute-done | bytes 8224 | tf_op jit(solution)/shard_map/ppermute | solution.py:687
  133.8 1.0 slice.31
  134.7 1.4 collective-permute-start.15
  136.2 0.7 collective-permute-start.16
  136.8 1.3 copy.19
  138.2 3.1 %collective-permute-done.16 = f32[16,128]{1,0:T(8,128)S(1)} collective-permute-done((f32[16,128]{1,0:T(8,128)S(1)}, f32[16,128]{1,0:T(8,128)S(1)}, u32[]{:S(2)}, u32[]{:S(2)}) %collective-permute-start.16) | collective-permute-done | bytes 8224 | tf_op jit(solution)/shard_map/ppermute | solution.py:691
  141.3 0.6 slice_bitcast_fusion
  142.5 2.0 %finish.1 = f32[128,1024]{1,0:T(8,128)} custom-call(bf16[2048,128]{1,0:T(8,128)(2,1)} %reduce-scatter.2.cloned.1.call-done.refs_0_, bf16[1024,128]{1,0:T(8,128)(2,1)} %copy-done.9), custom_call_target="tpu_custom_call" | custom-call | flops 4000000000 | bytes 1000000 | tf_op jit(solution)/shard_map/finish/pallas_call | solution.py:512
  (47 shorter events, 2.6 us)
Async XLA Ops:
  8.0 78.1 %all-gather.2.cloned.1.call-start = ((), (), s32[]{:S(2)}) async-start(), calls=%async_computation.1 | async-start | bytes 8650752 | tf_op jit(solution)/shard_map/all_gather | solution.py:637
  8.7 125.0 %reduce-scatter.2.cloned.1.call-start = ((), (), s32[]{:S(2)}) async-start(), calls=%async_computation.2 | async-start | bytes 4718592 | tf_op jit(solution)/shard_map/reduce_scatter | solution.py:670
  8.8 15.5 %collective-permute-start = (bf16[512,512]{1,0:T(8,128)(2,1)}, bf16[512,512]{1,0:T(8,128)(2,1)S(1)}, u32[]{:S(2)}, u32[]{:S(2)}) collective-permute-start(bf16[512,512]{1,0:T(8,128)(2,1)} %refs_0_.1), channel_id=1, source_target_pairs={{0,1},{1,0},{2,3},{3,2},{4,5},{5,4},{6,7},{7,6},{8,9},{9,8},{10,11... | collective-permute-start | bytes 1572872 | tf_op jit(solution)/shard_map/ppermute | solution.py:639
  12.1 13.6 %collective-permute-start.1 = (bf16[512,512]{1,0:T(8,128)(2,1)}, bf16[512,512]{1,0:T(8,128)(2,1)S(1)}, u32[]{:S(2)}, u32[]{:S(2)}) collective-permute-start(bf16[512,512]{1,0:T(8,128)(2,1)} %refs_0_.1), channel_id=1, source_target_pairs={{0,2},{1,3},{2,4},{3,5},{4,6},{5,7},{6,0},{7,1},{8,10},{9,11},{10,... | collective-permute-start | bytes 1572872 | tf_op jit(solution)/shard_map/ppermute | solution.py:593
  12.6 14.5 %collective-permute-start.2 = (bf16[512,512]{1,0:T(8,128)(2,1)}, bf16[512,512]{1,0:T(8,128)(2,1)S(1)}, u32[]{:S(2)}, u32[]{:S(2)}) collective-permute-start(bf16[512,512]{1,0:T(8,128)(2,1)} %refs_0_.1), channel_id=1, source_target_pairs={{0,6},{1,7},{2,0},{3,1},{4,2},{5,3},{6,4},{7,5},{8,14},{9,15},{10,... | collective-permute-start | bytes 1572872 | tf_op jit(solution)/shard_map/ppermute | solution.py:593
  24.3 21.1 %copy-start.7 = (bf16[512,512]{1,0:T(8,128)(2,1)}, bf16[512,512]{1,0:T(8,128)(2,1)S(1)}, u32[]{:S(2)}) copy-start(bf16[512,512]{1,0:T(8,128)(2,1)S(1)} %collective-permute-done.refs_9_.refs_10_.refs_4_) | copy-start | bytes 1572868
  25.7 19.7 %copy-start = (bf16[512,512]{1,0:T(8,128)(2,1)}, bf16[512,512]{1,0:T(8,128)(2,1)S(1)}, u32[]{:S(2)}) copy-start(bf16[512,512]{1,0:T(8,128)(2,1)S(1)} %collective-permute-done.1.refs_3_.refs_4_.refs_1_) | copy-start | bytes 1572868
  27.1 18.3 %copy-start.1 = (bf16[512,512]{1,0:T(8,128)(2,1)}, bf16[512,512]{1,0:T(8,128)(2,1)S(1)}, u32[]{:S(2)}) copy-start(bf16[512,512]{1,0:T(8,128)(2,1)S(1)} %collective-permute-done.2.refs_5_.refs_6_.refs_2_) | copy-start | bytes 1572868
  27.1 19.4 %collective-permute-start.3 = (bf16[512,512]{1,0:T(8,128)(2,1)S(1)}, bf16[512,512]{1,0:T(8,128)(2,1)S(1)}, u32[]{:S(2)}, u32[]{:S(2)}) collective-permute-start(bf16[512,512]{1,0:T(8,128)(2,1)S(1)} %collective-permute-done.refs_9_.refs_10_.refs_4_), channel_id=1, source_target_pairs={{0,2},{1,3},{2,4},{3,5},{4,6},{5,7},{6,0},{7,1},{8,10},{9,11},{10,... | collective-permute-start | bytes 1572872 | tf_op jit(solution)/shard_map/ppermute | solution.py:593
  27.4 19.0 %collective-permute-start.4 = (bf16[512,512]{1,0:T(8,128)(2,1)S(1)}, bf16[512,512]{1,0:T(8,128)(2,1)S(1)}, u32[]{:S(2)}, u32[]{:S(2)}) collective-permute-start(bf16[512,512]{1,0:T(8,128)(2,1)S(1)} %collective-permute-done.refs_9_.refs_10_.refs_4_), channel_id=1, source_target_pairs={{0,6},{1,7},{2,0},{3,1},{4,2},{5,3},{6,4},{7,5},{8,14},{9,15},{10,... | collective-permute-start | bytes 1572872 | tf_op jit(solution)/shard_map/ppermute | solution.py:593
  29.1 16.3 %collective-permute-start.5 = (bf16[256,512]{1,0:T(8,128)(2,1)S(1)}, bf16[256,512]{1,0:T(8,128)(2,1)S(1)}, u32[]{:S(2)}, u32[]{:S(2)}) collective-permute-start(bf16[256,512]{1,0:T(8,128)(2,1)S(1)} %slice.27), channel_id=1, source_target_pairs={{0,2},{1,3},{2,4},{3,5},{4,6},{5,7},{6,0},{7,1},{8,10},{9,11},{10,... | collective-permute-start | bytes 786440 | tf_op jit(solution)/shard_map/ppermute | solution.py:598
  30.8 15.7 %collective-permute-start.6 = (bf16[256,512]{1,0:T(8,128)(2,1)S(1)}, bf16[256,512]{1,0:T(8,128)(2,1)S(1)}, u32[]{:S(2)}, u32[]{:S(2)}) collective-permute-start(bf16[256,512]{1,0:T(8,128)(2,1)S(1)} %slice.28), channel_id=1, source_target_pairs={{0,6},{1,7},{2,0},{3,1},{4,2},{5,3},{6,4},{7,5},{8,14},{9,15},{10,... | collective-permute-start | bytes 786440 | tf_op jit(solution)/shard_map/ppermute | solution.py:599
  46.5 2.3 %copy-start.2 = (bf16[512,512]{1,0:T(8,128)(2,1)}, bf16[512,512]{1,0:T(8,128)(2,1)S(1)}, u32[]{:S(2)}) copy-start(bf16[512,512]{1,0:T(8,128)(2,1)S(1)} %collective-permute-done.3.refs_11_.refs_12_.refs_5_) | copy-start | bytes 1572868
  46.5 2.3 %copy-start.3 = (bf16[512,512]{1,0:T(8,128)(2,1)}, bf16[512,512]{1,0:T(8,128)(2,1)S(1)}, u32[]{:S(2)}) copy-start(bf16[512,512]{1,0:T(8,128)(2,1)S(1)} %collective-permute-done.4.refs_13_.refs_14_.refs_6_) | copy-start | bytes 1572868
  46.5 9.1 %collective-permute-start.7 = (bf16[256,512]{1,0:T(8,128)(2,1)S(1)}, bf16[256,512]{1,0:T(8,128)(2,1)S(1)}, u32[]{:S(2)}, u32[]{:S(2)}) collective-permute-start(bf16[256,512]{1,0:T(8,128)(2,1)S(1)} %slice.29), channel_id=1, source_target_pairs={{0,2},{1,3},{2,4},{3,5},{4,6},{5,7},{6,0},{7,1},{8,10},{9,11},{10,... | collective-permute-start | bytes 786440 | tf_op jit(solution)/shard_map/ppermute | solution.py:598
  48.4 7.7 %collective-permute-start.8 = (bf16[256,512]{1,0:T(8,128)(2,1)S(1)}, bf16[256,512]{1,0:T(8,128)(2,1)S(1)}, u32[]{:S(2)}, u32[]{:S(2)}) collective-permute-start(bf16[256,512]{1,0:T(8,128)(2,1)S(1)} %slice.30), channel_id=1, source_target_pairs={{0,6},{1,7},{2,0},{3,1},{4,2},{5,3},{6,4},{7,5},{8,14},{9,15},{10,... | collective-permute-start | bytes 786440 | tf_op jit(solution)/shard_map/ppermute | solution.py:599
  48.8 0.8 copy-start.4
  56.0 8.2 %collective-permute-start.9 = (bf16[14336,128]{1,0:T(8,128)(2,1)}, bf16[14336,128]{1,0:T(8,128)(2,1)}, u32[]{:S(2)}, u32[]{:S(2)}) collective-permute-start(bf16[14336,128]{1,0:T(8,128)(2,1)} %terms.2), channel_id=1, source_target_pairs={{0,8},{8,0},{16,24},{24,16},{32,40},{40,32},{48,56},{56,48},{64,72... | collective-permute-start | bytes 11010056 | tf_op jit(solution)/shard_map/ppermute | solution.py:666
  56.7 0.8 copy-start.5
  60.8 3.4 %collective-permute-start.10 = (bf16[2048,128]{1,0:T(8,128)(2,1)}, bf16[2048,128]{1,0:T(8,128)(2,1)S(1)}, u32[]{:S(2)}, u32[]{:S(2)}) collective-permute-start(bf16[2048,128]{1,0:T(8,128)(2,1)} %terms.3), channel_id=1, source_target_pairs={{0,8},{8,0},{16,24},{24,16},{32,40},{40,32},{48,56},{56,48},{64,72... | collective-permute-start | bytes 1572872 | tf_op jit(solution)/shard_map/ppermute | solution.py:668
  64.3 0.8 copy-start.8
  97.6 17.0 %copy-start.6 = (f32[1,1024]{1,0:T(1,128)S(1)}, f32[1,1024]{1,0:T(1,128)}, u32[]{:S(2)}) copy-start(f32[1,1024]{1,0:T(1,128)} %get-tuple-element.74) | copy-start | bytes 12292
  115.4 1.2 collective-permute-start.11
  117.2 4.0 %collective-permute-start.12 = (f32[16,128]{1,0:T(8,128)S(1)}, f32[16,128]{1,0:T(8,128)S(1)}, u32[]{:S(2)}, u32[]{:S(2)}) collective-permute-start(f32[16,128]{1,0:T(8,128)S(1)} %fusion), channel_id=1, source_target_pairs={{0,32},{8,40},{16,48},{24,56},{32,0},{40,8},{48,16},{56,24},{64,96... | collective-permute-start | bytes 24584 | tf_op jit(solution)/shard_map/ppermute | solution.py:687
  121.2 5.0 %collective-permute-start.13 = (f32[16,128]{1,0:T(8,128)S(1)}, f32[16,128]{1,0:T(8,128)S(1)}, u32[]{:S(2)}, u32[]{:S(2)}) collective-permute-start(f32[16,128]{1,0:T(8,128)S(1)} %add.120), channel_id=1, source_target_pairs={{0,64},{8,72},{16,80},{24,88},{32,96},{40,104},{48,112},{56,120},{... | collective-permute-start | bytes 24584 | tf_op jit(solution)/shard_map/ppermute | solution.py:687
  126.2 7.6 %collective-permute-start.14 = (f32[16,128]{1,0:T(8,128)S(1)}, f32[16,128]{1,0:T(8,128)S(1)}, u32[]{:S(2)}, u32[]{:S(2)}) collective-permute-start(f32[16,128]{1,0:T(8,128)S(1)} %add.121), channel_id=1, source_target_pairs={{0,128},{8,136},{16,144},{24,152},{32,160},{40,168},{48,176},{56,1... | collective-permute-start | bytes 24584 | tf_op jit(solution)/shard_map/ppermute | solution.py:687
  134.7 6.6 %collective-permute-start.15 = (bf16[1024,128]{1,0:T(8,128)(2,1)S(1)}, bf16[1024,128]{1,0:T(8,128)(2,1)S(1)}, u32[]{:S(2)}, u32[]{:S(2)}) collective-permute-start(bf16[1024,128]{1,0:T(8,128)(2,1)S(1)} %slice.31), channel_id=1, source_target_pairs={{0,16},{8,24},{16,0},{24,8},{32,48},{40,56},{48,32},{56,40},{64,80... | collective-permute-start | bytes 786440 | tf_op jit(solution)/shard_map/ppermute | solution.py:690
  136.2 5.1 %collective-permute-start.16 = (f32[16,128]{1,0:T(8,128)S(1)}, f32[16,128]{1,0:T(8,128)S(1)}, u32[]{:S(2)}, u32[]{:S(2)}) collective-permute-start(f32[16,128]{1,0:T(8,128)S(1)} %add.122), channel_id=1, source_target_pairs={{0,16},{8,24},{16,0},{24,8},{32,48},{40,56},{48,32},{56,40},{64,80... | collective-permute-start | bytes 24584 | tf_op jit(solution)/shard_map/ppermute | solution.py:691
  141.3 1.2 copy-start.9
Sparse Core Ops, SparseCore 0:
  10.7 75.3 all-gather.1
Sparse Core Ops, SparseCore 1:
  72.8 55.9 reduce-scatter.1
